TPU v7x, 512 devices: a whole 4x4x16 slice. The times are simulated.
512 devices in a mesh: seq: 8 (over z_lo, core), row: 4 (over y), col: 16 (over z_hi, x).
Axes of the slice: x: 4, y: 4, z: 16 (z_hi: 4, z_lo: 4; z = z_hi * 4 + z_lo), core: 2. Of those that a mesh axis runs over, the one named last changes fastest.
Arguments:
- stream: bfloat16 [2048, 4096], P('seq', ('row', 'col')), may hold values from -6 to 6
- query_heads: bfloat16 [2048, 4096], P('seq', ('row', 'col')), may hold values from -24 to 24
- key_heads: bfloat16 [2048, 4096], P('seq', ('row', 'col')), may hold values from -24 to 24
- value_heads: bfloat16 [2048, 4096], P('seq', ('row', 'col')), may hold values from -6 to 6
- windows: int32 [64], replicated, may hold values from 32 to 256, as said below
- norm_gain: float32 [4096], P(('row', 'col')), may hold values from 0.4 to 1.6
- up_weight: bfloat16 [4096, 16384], P('row', ('seq', 'col')), may hold values from -0.125 to 0.125
- down_weight: bfloat16 [16384, 4096], P(('seq', 'col'), 'row'), may hold values from -0.0625 to 0.0625
- up_rows: int32 [2048], replicated, may hold values from 0 to 31, as said below
- up_cols: int32 [2048], replicated, may hold values from 0 to 127, as said below
- down_rows: int32 [2048], replicated, may hold values from 0 to 127, as said below
- down_cols: int32 [2048], replicated, may hold values from 0 to 31, as said below
- cotangent: bfloat16 [2048, 4096], P('seq', ('row', 'col')), may hold values from -6 to 6
Outputs:
- grad_stream: bfloat16 [2048, 4096], P('seq', ('row', 'col'))
- grad_query: bfloat16 [2048, 4096], P('seq', ('row', 'col'))
- grad_key: bfloat16 [2048, 4096], P('seq', ('row', 'col'))
- grad_value: bfloat16 [2048, 4096], P('seq', ('row', 'col'))
- grad_gain: float32 [4096], P(('row', 'col'))
- grad_up: bfloat16 [4096, 16384], P('row', ('seq', 'col'))
- grad_down: bfloat16 [16384, 4096], P(('seq', 'col'), 'row')
Inputs may be any that keep to these rules, and one draw needn't show every extreme that they name: Some head has windows[h] exactly 256. The pairs (up_rows[t], up_cols[t]) are distinct: half of all blocks. `up_cols`: see up_rows. The pairs (down_rows[t], down_cols[t]) are distinct: half of all blocks. `down_cols`: see down_rows.
All inputs are finite; a program needn't handle non-finite values.
Results may differ from a plain program's by a relative error of at most 0.034.
Values may be sent and summed in bfloat16 or wider, within the bound.
No kernel may reach another device: no remote copies, remote signals or barrier semaphores. Data moves between devices by JAX's collectives and lax.ppermute only.
A program may use at most 64 MiB of HBM per device.

v0:
```python
import jax
import jax.numpy as jnp
from jax import lax
from jax.sharding import PartitionSpec as P

BLK = 128


GELU_C = 0.7978845608028654
GELU_A = 0.044715
EPSILON = 1e-05


def padded(shard, sides, width):
    for axis, dim in sides:
        size, length = (lax.axis_size(axis), shard.shape[dim])
        up = [(i, (i + 1) % size) for i in range(size - 1)]
        down = [(j, i) for i, j in up]
        last = lax.slice_in_dim(shard, length - width, length, axis=dim)
        initial = lax.slice_in_dim(shard, 0, width, axis=dim)
        before = lax.ppermute(last, axis, up)
        after = lax.ppermute(initial, axis, down)
        shard = jnp.concatenate([before, shard, after], axis=dim)
    return shard


def from_behind(value, axis, steps):
    count = lax.axis_size(axis)
    initial, last = (max(0, -steps), min(count, count - steps))
    return lax.ppermute(value, axis, [(source, source + steps) for source in range(initial, last)])


def gelu_value(pre_act):
    tanh_arg = GELU_C * (pre_act + GELU_A * pre_act * pre_act * pre_act)
    return 0.5 * pre_act * (1.0 + jnp.tanh(tanh_arg))


def gelu_slope(pre_act):
    tanh_arg = GELU_C * (pre_act + GELU_A * pre_act * pre_act * pre_act)
    tanh_val = jnp.tanh(tanh_arg)
    return 0.5 * (1.0 + tanh_val) + 0.5 * pre_act * (1.0 - tanh_val * tanh_val) * GELU_C * (
        1.0 + 3.0 * GELU_A * pre_act * pre_act
    )


def block_mask(row_ids, col_ids, row_count, col_count):
    row_hot = (row_ids[:, None] == jnp.arange(row_count, dtype=jnp.int32)[None, :]).astype(
        jnp.float32
    )
    col_hot = (col_ids[:, None] == jnp.arange(col_count, dtype=jnp.int32)[None, :]).astype(
        jnp.float32
    )
    return jnp.dot(row_hot.T, col_hot, precision=lax.Precision.HIGHEST)


def apply_mask(weight, block_flags):
    row_len, col_len = weight.shape
    blocked = weight.reshape(row_len // BLK, BLK, col_len // BLK, BLK)
    return (blocked * block_flags.astype(weight.dtype)[:, None, :, None]).reshape(row_len, col_len)


def on_device(
    stream,
    query_heads,
    key_heads,
    value_heads,
    windows,
    norm_gain,
    up_weight,
    down_weight,
    up_rows,
    up_cols,
    down_rows,
    down_cols,
    cotangent,
):
    tok_count = stream.shape[0]
    head_size = stream.shape[1]
    seq_devs = lax.axis_size("seq")
    row_devs = lax.axis_size("row")
    col_devs = lax.axis_size("col")
    seq_index = lax.axis_index("seq")
    row_index = lax.axis_index("row")
    col_index = lax.axis_index("col")
    width_total = head_size * row_devs * col_devs
    seq_total = tok_count * seq_devs
    score_scale = float(head_size) ** (-0.5)
    head_index = row_index * col_devs + col_index
    reach_width = lax.dynamic_index_in_dim(windows, head_index, 0, keepdims=False)
    paired = jnp.concatenate([key_heads, value_heads], axis=1)
    widened = padded(paired, (("seq", 0),), tok_count)
    key_ext = widened[:, :head_size]
    value_ext = widened[:, head_size:]
    query_place = seq_index * tok_count + jnp.arange(tok_count, dtype=jnp.int32)
    key_place = (seq_index - 1) * tok_count + jnp.arange(3 * tok_count, dtype=jnp.int32)
    reached = (
        (jnp.abs(query_place[:, None] - key_place[None, :]) <= reach_width)
        & (key_place[None, :] >= 0)
        & (key_place[None, :] < seq_total)
    )
    scores = jnp.dot(query_heads, key_ext.T, preferred_element_type=jnp.float32) * score_scale
    scores = jnp.where(reached, scores, -1e30)
    row_peak = jnp.max(scores, axis=1, keepdims=True)
    weights = jnp.where(reached, jnp.exp(scores - row_peak), 0.0)
    attn_probs = weights / jnp.sum(weights, axis=1, keepdims=True)
    probs_low = attn_probs.astype(jnp.bfloat16)
    attended = jnp.dot(probs_low, value_ext, preferred_element_type=jnp.float32)
    hidden = (stream.astype(jnp.float32) + attended).astype(jnp.bfloat16)
    hidden_f = hidden.astype(jnp.float32)
    square_total = lax.psum(jnp.sum(hidden_f * hidden_f, axis=1), ("row", "col"))
    inv_rms = lax.rsqrt(square_total / width_total + EPSILON)[:, None]
    normed = (hidden_f * inv_rms * norm_gain).astype(jnp.bfloat16)
    norm_panel = lax.all_gather(normed, "col", axis=1, tiled=True)
    shard_cols = up_weight.shape[1]
    shard_blocks = shard_cols // BLK
    row_blocks = up_weight.shape[0] // BLK
    total_fblocks = shard_blocks * seq_devs * col_devs
    total_dblocks = width_total // BLK
    up_flags = block_mask(up_rows, up_cols, total_dblocks, total_fblocks)
    up_row_flags = lax.dynamic_slice_in_dim(up_flags, row_index * row_blocks, row_blocks, 0)
    up_grid = up_row_flags.reshape(row_blocks, seq_devs, col_devs, shard_blocks)
    up_panel_flags = lax.dynamic_index_in_dim(up_grid, col_index, 2, keepdims=False)
    up_own_flags = lax.dynamic_index_in_dim(up_panel_flags, seq_index, 1, keepdims=False)
    up_panel_flags = up_panel_flags.reshape(row_blocks, seq_devs * shard_blocks)
    down_flags = block_mask(down_rows, down_cols, total_fblocks, total_dblocks)
    down_col_flags = lax.dynamic_slice_in_dim(down_flags, row_index * row_blocks, row_blocks, 1)
    down_grid = down_col_flags.reshape(seq_devs, col_devs, shard_blocks, row_blocks)
    down_panel_flags = lax.dynamic_index_in_dim(down_grid, col_index, 1, keepdims=False)
    down_own_flags = lax.dynamic_index_in_dim(down_panel_flags, seq_index, 0, keepdims=False)
    down_panel_flags = down_panel_flags.reshape(seq_devs * shard_blocks, row_blocks)
    up_panel = lax.all_gather(up_weight, "seq", axis=1, tiled=True)
    up_masked = apply_mask(up_panel, up_panel_flags)
    pre_act = lax.psum(
        jnp.dot(norm_panel, up_masked, preferred_element_type=jnp.float32).astype(jnp.bfloat16),
        "row",
    ).astype(jnp.float32)
    activation = gelu_value(pre_act).astype(jnp.bfloat16)
    grad_panel = lax.all_gather(cotangent, "col", axis=1, tiled=True)
    down_panel = lax.all_gather(down_weight, "seq", axis=0, tiled=True)
    down_masked = apply_mask(down_panel, down_panel_flags)
    grad_pre = lax.psum(
        jnp.dot(grad_panel, down_masked.T, preferred_element_type=jnp.float32).astype(jnp.bfloat16),
        "row",
    ).astype(jnp.float32)
    grad_down_sum = lax.psum_scatter(
        jnp.dot(activation.T, grad_panel, preferred_element_type=jnp.float32).astype(jnp.bfloat16),
        "seq",
        scatter_dimension=0,
        tiled=True,
    ).astype(jnp.float32)
    grad_down = apply_mask(grad_down_sum, down_own_flags).astype(jnp.bfloat16)
    grad_act = (grad_pre * gelu_slope(pre_act)).astype(jnp.bfloat16)
    grad_up_sum = lax.psum_scatter(
        jnp.dot(norm_panel.T, grad_act, preferred_element_type=jnp.float32).astype(jnp.bfloat16),
        "seq",
        scatter_dimension=1,
        tiled=True,
    ).astype(jnp.float32)
    grad_up = apply_mask(grad_up_sum, up_own_flags).astype(jnp.bfloat16)
    norm_part = jnp.dot(grad_act, up_masked.T, preferred_element_type=jnp.float32)
    full_sum = lax.psum(norm_part.astype(jnp.bfloat16), "col").astype(jnp.float32)
    grad_norm = lax.dynamic_slice_in_dim(full_sum, col_index * head_size, head_size, 1)
    grad_gain = lax.psum(jnp.sum(grad_norm * hidden_f * inv_rms, axis=0), "seq")
    gained = grad_norm * norm_gain
    token_total = lax.psum(jnp.sum(gained * hidden_f, axis=1), ("row", "col"))[:, None]
    grad_hidden = (
        inv_rms * gained
        - hidden_f * inv_rms * inv_rms * inv_rms * token_total / width_total
        + cotangent.astype(jnp.float32)
    )
    grad_stream = grad_hidden.astype(jnp.bfloat16)
    grad_probs = jnp.dot(grad_stream, value_ext.T, preferred_element_type=jnp.float32)
    center = jnp.sum(attn_probs * grad_probs, axis=1, keepdims=True)
    grad_scores = (attn_probs * (grad_probs - center)).astype(jnp.bfloat16)
    grad_query = (
        jnp.dot(grad_scores, key_ext, preferred_element_type=jnp.float32) * score_scale
    ).astype(jnp.bfloat16)
    key_grad_ext = (
        jnp.dot(grad_scores.T, query_heads, preferred_element_type=jnp.float32) * score_scale
    )
    value_grad_ext = jnp.dot(probs_low.T, grad_stream, preferred_element_type=jnp.float32)
    pair_grads = jnp.concatenate([key_grad_ext, value_grad_ext], axis=1)
    from_upper = from_behind(pair_grads[:tok_count].astype(jnp.bfloat16), "seq", -1).astype(
        jnp.float32
    )
    from_lower = from_behind(pair_grads[2 * tok_count :].astype(jnp.bfloat16), "seq", 1).astype(
        jnp.float32
    )
    pair_total = pair_grads[tok_count : 2 * tok_count] + from_upper + from_lower
    grad_key = pair_total[:, :head_size].astype(jnp.bfloat16)
    grad_value = pair_total[:, head_size:].astype(jnp.bfloat16)
    return (grad_stream, grad_query, grad_key, grad_value, grad_gain, grad_up, grad_down)


def solution(mesh):
    in_specs = (
        P("seq", ("row", "col")),
        P("seq", ("row", "col")),
        P("seq", ("row", "col")),
        P("seq", ("row", "col")),
        P(),
        P(("row", "col")),
        P("row", ("seq", "col")),
        P(("seq", "col"), "row"),
        P(),
        P(),
        P(),
        P(),
        P("seq", ("row", "col")),
    )
    out_specs = (
        P("seq", ("row", "col")),
        P("seq", ("row", "col")),
        P("seq", ("row", "col")),
        P("seq", ("row", "col")),
        P(("row", "col")),
        P("row", ("seq", "col")),
        P(("seq", "col"), "row"),
    )
    return jax.shard_map(
        on_device, mesh=mesh, in_specs=in_specs, out_specs=out_specs, check_vma=False
    )
```

profile of v0, /device:TPU:1, one launch (start us, length us, event | category | flops | bytes accessed | tf_op | source)
XLA Modules:
  0.0 896.5 jit_solution(16263997181730136396)
XLA Ops:
  7.2 0.0 copy-start
  7.2 0.0 all-gather.5.cloned.1.call-start
  7.2 0.7 all-gather.5.cloned.1.call-update
  7.9 0.0 all-gather.3.cloned.1.call-start
  8.0 0.7 all-gather.3.cloned.1.call-update
  8.7 0.0 all-reduce.6.cloned.1.call-start
  8.7 0.8 constant_dynamic-update-slice_fusion.1
  9.5 0.8 constant_dynamic-update-slice_fusion
  10.3 8.8 collective-permute-start.1
  19.0 1.9 collective-permute-start
  21.0 1.7 fusion.20
  22.7 0.1 reshape.91
  22.8 0.1 constant_dynamic-slice_fusion.1
  22.8 0.7 copy.43
  23.6 1.7 fusion.21
  25.3 0.1 reshape.92
  25.4 0.6 dynamic_slice.29
  25.9 0.7 fusion.56
  26.7 54.4 %all_gather.13 = bf16[256,1024]{0,1:T(8,128)(2,1)S(1)} all-gather(bf16[256,64]{0,1:T(8,128)(2,1)S(1)} %copy-done.4), channel_id=1, replica_groups=mesh['seq'=8,'row'=4,'col'=16] {'col'}, dimensions={1}, use_global_device_ids=true | all-gather | bytes 557056 | tf_op jit(solution)/shard_map/all_gather | solution.py:138
  81.2 0.0 copy-start.2
  81.2 1.1 fusion.69
  82.4 1.4 fusion.25
  83.8 1.2 multiply_reduce_fusion.1
  85.1 190.1 %psum.42 = f32[256]{0:T(256)S(1)} all-reduce(f32[256]{0:T(256)S(1)} %get-tuple-element.17), channel_id=1, replica_groups=mesh['seq'=8,'row'=4,'col'=16] {'row','col'}, use_global_device_ids=true, to_apply=%region_3.4 | all-reduce | flops 256 | bytes 2048 | tf_op jit(solution)/shard_map/psum | solution.py:110
  275.2 0.1 multiply_convert_fusion.3
  275.3 46.1 %all_gather.14 = bf16[256,1024]{0,1:T(8,128)(2,1)} all-gather(bf16[256,64]{0,1:T(8,128)(2,1)S(1)} %multiply_convert_fusion.3), channel_id=1, replica_groups=mesh['seq'=8,'row'=4,'col'=16] {'col'}, dimensions={1}, use_global_device_ids=true | all-gather | bytes 557056 | tf_op jit(solution)/shard_map/all_gather | solution.py:113
  321.3 1.1 mul.231
  322.4 3.4 convolution_convert_fusion.3
  325.8 1.2 mul.225
  327.0 0.4 copy-done.16
  327.4 1.5 fusion.7
  328.9 0.0 all-reduce.6.cloned.1.call-update
  329.0 0.0 all-reduce.4.cloned.1.call-start
  329.0 95.0 %all-reduce.6.cloned.1.call-done = (bf16[256,1024]{0,1:T(8,128)(2,1)}, bf16[256,1024]{0,1:T(8,128)(2,1)}) async-done(((bf16[256,1024]{0,1:T(8,128)(2,1)}, bf16[256,1024]{0,1:T(8,128)(2,1)}), (bf16[256,1024]{0,1:T(8,128)(2,1)}, bf16[256,1024]{0,1:T(8,128)(2,1)})) %all-reduce.6.cloned.1.call-update) | async-done | bytes 1048592 | tf_op jit(solution)/shard_map/psum | solution.py:133
  424.0 4.1 convolution_convert_fusion.2
  428.1 0.0 all-reduce.4.cloned.1.call-update
  428.2 0.0 reduce-scatter.7.cloned.1.call-start
  428.2 2.6 convolution_convert_fusion.1
  430.8 2.6 copy.41
  433.4 0.0 reduce-scatter.7.cloned.1.call-update
  433.4 0.0 reduce-scatter.5.cloned.1.call-start
  433.5 1.0 copy-done.17
  434.5 2.2 convolution_convert_fusion
  436.6 0.0 reduce-scatter.5.cloned.1.call-update
  436.7 1.0 dynamic-slice_reduce_fusion
  437.7 1.0 dynamic-slice_reduce_fusion.1
  438.7 0.1 broadcast_bitcast_fusion
  438.7 0.1 broadcast_bitcast_fusion.1
  438.8 185.4 %all-reduce.4.cloned.1.call-done = bf16[256,1024]{0,1:T(8,128)(2,1)} async-done(((bf16[256,1024]{0,1:T(8,128)(2,1)}), bf16[256,1024]{0,1:T(8,128)(2,1)}) %all-reduce.4.cloned.1.call-update) | async-done | bytes 524304 | tf_op jit(solution)/shard_map/psum | solution.py:161
  624.2 1.0 fusion.55
  625.2 197.1 %psum.46 = f32[256]{0:T(256)S(1)} all-reduce(f32[256]{0:T(256)S(1)} %get-tuple-element.8), channel_id=1, replica_groups=mesh['seq'=8,'row'=4,'col'=16] {'row','col'}, use_global_device_ids=true, to_apply=%region_8.9 | all-reduce | flops 256 | bytes 2048 | tf_op jit(solution)/shard_map/psum | solution.py:165
  822.3 0.8 fusion.52
  823.2 1.3 multiply_reduce_fusion
  824.4 1.4 multiply_convert_fusion
  825.9 0.3 convolution_multiply_fusion.1
  826.2 1.2 fusion.36
  827.4 41.2 %collective-permute-start.2 = (bf16[256,128]{0,1:T(8,128)(2,1)S(1)}, bf16[256,128]{0,1:T(8,128)(2,1)S(1)}, u32[]{:S(2)}, u32[]{:S(2)}) collective-permute-start(bf16[256,128]{0,1:T(8,128)(2,1)S(1)} %get-tuple-element.11), channel_id=1, source_target_pairs={{64,0},{128,64},{192,128},{256,192},{320,256},{384,320},{448,384},... | collective-permute-start | bytes 196616 | tf_op jit(solution)/shard_map/ppermute | solution.py:30
  868.6 2.8 collective-permute-start.3
  871.4 0.8 fusion.10
  872.2 13.1 %psum.47 = f32[64]{0:T(128)} all-reduce(f32[64]{0:T(128)S(1)} %get-tuple-element.7), channel_id=1, replica_groups=mesh['seq'=8,'row'=4,'col'=16] {'seq'}, use_global_device_ids=true, to_apply=%region_11.12 | all-reduce | flops 64 | bytes 512 | tf_op jit(solution)/shard_map/psum | solution.py:163
  885.3 0.6 fusion.68
  885.9 1.1 copy.42
  887.1 0.9 multiply_convert_fusion.2
  888.0 1.7 multiply_convert_fusion.1
  (54 shorter events, 0.2 us)
Async XLA Ops:
  7.2 74.1 %copy-start = (bf16[256,64]{0,1:T(8,128)(2,1)S(1)}, bf16[256,64]{0,1:T(8,128)(2,1)}, u32[]{:S(2)}) copy-start(bf16[256,64]{0,1:T(8,128)(2,1)} %param.14) | copy-start | bytes 98308
  7.2 18.2 %copy-start.19 = (s32[64]{0:T(128)S(1)}, s32[64]{0:T(128)}, u32[]{:S(2)}) copy-start(s32[64]{0:T(128)} %param.17) | copy-start | bytes 772
  7.2 19.5 %copy-start.4 = (bf16[256,64]{0,1:T(8,128)(2,1)S(1)}, bf16[256,64]{0,1:T(8,128)(2,1)}, u32[]{:S(2)}) copy-start(bf16[256,64]{0,1:T(8,128)(2,1)} %param.25) | copy-start | bytes 98308
  7.2 314.1 %all-gather.5.cloned.1.call-start = ((), (), s32[]{:S(2)}) async-start(), calls=%async_computation.3 | async-start | bytes 2359296 | tf_op jit(solution)/shard_map/all_gather | solution.py:131
  7.9 317.9 %all-gather.3.cloned.1.call-start = ((), (), s32[]{:S(2)}) async-start(), calls=%async_computation.2 | async-start | bytes 2359296 | tf_op jit(solution)/shard_map/all_gather | solution.py:139
  8.7 415.3 %all-reduce.6.cloned.1.call-start = ((), (), s32[]{:S(2)}) async-start(), calls=%async_computation.7 | async-start | bytes 2097152 | tf_op jit(solution)/shard_map/psum | solution.py:133
  10.3 70.9 %collective-permute-start.1 = (bf16[256,128]{0,1:T(8,128)(2,1)S(1)}, bf16[256,128]{0,1:T(8,128)(2,1)S(1)}, u32[]{:S(2)}, u32[]{:S(2)}) collective-permute-start(bf16[256,128]{0,1:T(8,128)(2,1)S(1)} %constant_dynamic-update-slice_fusion), channel_id=1, source_target_pairs={{64,0},{128,64},{192,128},{256,192},{320,256},{384,320},{448,384},... | collective-permute-start | bytes 196616 | tf_op jit(solution)/shard_map/ppermute | solution.py:22
  19.0 62.1 %collective-permute-start = (bf16[256,128]{0,1:T(8,128)(2,1)S(1)}, bf16[256,128]{0,1:T(8,128)(2,1)S(1)}, u32[]{:S(2)}, u32[]{:S(2)}) collective-permute-start(bf16[256,128]{0,1:T(8,128)(2,1)S(1)} %constant_dynamic-update-slice_fusion), channel_id=1, source_target_pairs={{0,64},{64,128},{128,192},{192,256},{256,320},{320,384},{384,448},... | collective-permute-start | bytes 196616 | tf_op jit(solution)/shard_map/ppermute | solution.py:21
  22.8 58.5 %copy-start.5 = (f32[8,16,1,8]{1,0,3,2:T(8,128)}, f32[8,16,1,8]{1,0,3,2:T(8,128)S(1)}, u32[]{:S(2)}) copy-start(f32[8,16,1,8]{1,0,3,2:T(8,128)S(1)} %reshape.91) | copy-start | bytes 12292
  23.6 60.2 %copy-start.18 = (bf16[256,64]{0,1:T(8,128)(2,1)S(1)}, bf16[256,64]{0,1:T(8,128)(2,1)}, u32[]{:S(2)}) copy-start(bf16[256,64]{0,1:T(8,128)(2,1)} %param.13) | copy-start | bytes 98308
  25.3 55.9 %copy-start.6 = (f32[8,8,16,1]{2,1,0,3:T(8,128)}, f32[8,8,16,1]{2,1,0,3:T(8,128)S(1)}, u32[]{:S(2)}) copy-start(f32[8,8,16,1]{2,1,0,3:T(8,128)S(1)} %reshape.92) | copy-start | bytes 12292
  81.2 3.9 copy-start.10
  81.2 3.8 copy-start.2
  82.4 2.7 copy-start.12
  83.8 1.3 copy-start.14
  83.8 191.4 %copy-start.8 = (f32[64]{0:T(128)S(1)}, f32[64]{0:T(128)}, u32[]{:S(2)}) copy-start(f32[64]{0:T(128)} %param.18) | copy-start | bytes 772
  321.3 1.1 copy-start.1
  325.8 1.6 copy-start.16
  329.0 295.3 %all-reduce.4.cloned.1.call-start = ((), (), s32[]{:S(2)}) async-start(), calls=%async_computation.4 | async-start | bytes 1048576 | tf_op jit(solution)/shard_map/psum | solution.py:161
  428.2 457.8 %reduce-scatter.7.cloned.1.call-start = ((), (), s32[]{:S(2)}) async-start(), calls=%async_computation.6 | async-start | bytes 2359296
  433.4 1.0 copy-start.17
  433.4 454.5 %reduce-scatter.5.cloned.1.call-start = ((), (), s32[]{:S(2)}) async-start(), calls=%async_computation.5 | async-start | bytes 2359296 | tf_op jit(solution)/shard_map/reduce_scatter | solution.py:145
  436.6 187.6 %copy-start.9 = (f32[64]{0:T(128)S(1)}, f32[64]{0:T(128)}, u32[]{:S(2)}) copy-start(f32[64]{0:T(128)} %param.18) | copy-start | bytes 772
  436.6 386.5 %copy-start.3 = (bf16[768,128]{0,1:T(8,128)(2,1)S(1)}, bf16[768,128]{0,1:T(8,128)(2,1)}, u32[]{:S(2)}) copy-start(bf16[768,128]{0,1:T(8,128)(2,1)} %copy-done.2) | copy-start | bytes 589828
  436.6 386.5 %copy-start.11 = (s32[256]{0:T(256)S(1)}, s32[256]{0:T(256)}, u32[]{:S(2)}) copy-start(s32[256]{0:T(256)} %copy-done.10) | copy-start | bytes 3076
  436.6 386.6 %copy-start.13 = (f32[256]{0:T(256)S(1)}, f32[256]{0:T(256)}, u32[]{:S(2)}) copy-start(f32[256]{0:T(256)} %copy-done.12) | copy-start | bytes 3076
  436.6 386.6 %copy-start.15 = (f32[256]{0:T(256)S(1)}, f32[256]{0:T(256)}, u32[]{:S(2)}) copy-start(f32[256]{0:T(256)} %copy-done.14) | copy-start | bytes 3076
  823.2 3.0 copy-start.7
  827.4 57.9 %collective-permute-start.2 = (bf16[256,128]{0,1:T(8,128)(2,1)S(1)}, bf16[256,128]{0,1:T(8,128)(2,1)S(1)}, u32[]{:S(2)}, u32[]{:S(2)}) collective-permute-start(bf16[256,128]{0,1:T(8,128)(2,1)S(1)} %get-tuple-element.11), channel_id=1, source_target_pairs={{64,0},{128,64},{192,128},{256,192},{320,256},{384,320},{448,384},... | collective-permute-start | bytes 196616 | tf_op jit(solution)/shard_map/ppermute | solution.py:30
  868.6 16.7 %collective-permute-start.3 = (bf16[256,128]{0,1:T(8,128)(2,1)S(1)}, bf16[256,128]{0,1:T(8,128)(2,1)S(1)}, u32[]{:S(2)}, u32[]{:S(2)}) collective-permute-start(bf16[256,128]{0,1:T(8,128)(2,1)S(1)} %get-tuple-element.12), channel_id=1, source_target_pairs={{0,64},{64,128},{128,192},{192,256},{256,320},{320,384},{384,448},... | collective-permute-start | bytes 196616 | tf_op jit(solution)/shard_map/ppermute | solution.py:30
Sparse Core Ops, SparseCore 0:
  10.0 58.6 all-gather.4
  70.8 42.7 all-gather.2
  329.1 94.8 all-reduce.5
  428.3 195.8 all-reduce.3
  626.9 54.2 reduce-scatter.6
  683.9 46.0 reduce-scatter.4
where the time goes:
time: 898 us; the launch traced here: 897 us
  blocking collectives  501 us (56%)
  waiting for transfers between devices  282 us (31%)
  starting transfers between devices  54.9 us (6%)
  matrix products  23.1 us (3%)
  between operations  14.5 us (2%)
  local copies, waits for them, and re-layouts  14 us (2%)
    psum x1, blocking collectives, on_device(): lax.psum(jnp.sum(gained * hidden_f, axis=1), ('row', 'col'))[:, None]  197 us
    psum x1, blocking collectives, on_device(): lax.psum(jnp.sum(hidden_f * hidden_f, axis=1), ('row', 'col'))  190 us
    psum x1, waiting for transfers between devices, on_device(): lax.psum(norm_part.astype(jnp.bfloat16), 'col').astype(jnp.float32)  185 us
    psum x1, waiting for transfers between devices, on_device(): lax.psum(jnp.dot(norm_panel, up_masked, preferred_element_type=jnp.float3...  95 us
    all_gather x1, blocking collectives, on_device(): grad_panel = lax.all_gather(cotangent, 'col', axis=1, tiled=True)  54.4 us
    all_gather x1, blocking collectives, on_device(): norm_panel = lax.all_gather(normed, 'col', axis=1, tiled=True)  46.1 us
    ppermute x2, starting transfers between devices, from_behind(): lax.ppermute(value, axis, [(source, source + steps) for source in range(i...  44 us
  transfers between devices with their start and end apart: 10, of which 2 were waited for; matrix products, arithmetic and copies ran while one was open for 4% of the time, Pallas kernels for 0%

commit v1 on v0

v1 whole, which is shorter than its diff:
```python
import jax
import jax.numpy as jnp
from jax import lax
from jax.sharding import Mesh
from jax.sharding import PartitionSpec as P

BLK = 128
GELU_C = 0.7978845608028654
GELU_A = 0.044715
EPSILON = 1e-05
TAIL = 16
BF = jnp.bfloat16
F32 = jnp.float32


def gelu_value(pre_act):
    tanh_arg = GELU_C * (pre_act + GELU_A * pre_act * pre_act * pre_act)
    return 0.5 * pre_act * (1.0 + jnp.tanh(tanh_arg))


def gelu_slope(pre_act):
    tanh_arg = GELU_C * (pre_act + GELU_A * pre_act * pre_act * pre_act)
    tanh_val = jnp.tanh(tanh_arg)
    return 0.5 * (1.0 + tanh_val) + 0.5 * pre_act * (1.0 - tanh_val * tanh_val) * GELU_C * (
        1.0 + 3.0 * GELU_A * pre_act * pre_act
    )


def tail_rows(vector):
    high = lax.reduce_precision(vector, 8, 7)
    low = vector - high
    pair = jnp.stack([high, low]).astype(BF)
    return jnp.pad(pair, ((0, TAIL - 2), (0, 0)))


def tail_value(rows):
    return rows[..., 0, :].astype(F32) + rows[..., 1, :].astype(F32)


def spread(array, axis):
    count = lax.axis_size(axis)
    copies = jnp.broadcast_to(array[None], (count,) + array.shape)
    return lax.all_to_all(copies, axis, 0, 0, tiled=True)


def exchange(pieces, axis):
    return lax.all_to_all(pieces, axis, 0, 0, tiled=True)


def own_flags(inner_ids, outer_ids, own_outer, first_inner, inner_count):
    wanted = first_inner + jnp.arange(inner_count, dtype=jnp.int32)
    hit = (inner_ids[None, :] == wanted[:, None]) & (outer_ids == own_outer)[None, :]
    return jnp.any(hit, axis=1)


def on_device(
    stream,
    query_heads,
    key_heads,
    value_heads,
    windows,
    norm_gain,
    up_weight,
    down_weight,
    up_rows,
    up_cols,
    down_rows,
    down_cols,
    cotangent,
):
    tok, head = stream.shape
    n_zl, n_core, n_row, n_zh, n_x = (lax.axis_size(a) for a in ("zl", "core", "row", "zh", "x"))
    seq_devs = n_zl * n_core
    col_devs = n_zh * n_x
    seq_index = lax.axis_index(("zl", "core"))
    row_index = lax.axis_index("row")
    col_index = lax.axis_index(("zh", "x"))
    width_total = head * n_row * col_devs
    depth, units = up_weight.shape
    blocks = depth // BLK
    score_scale = float(head) ** (-0.5)
    swap = [(i, n_core - 1 - i) for i in range(n_core)]

    own_block = seq_index * col_devs + col_index
    up_flags = own_flags(up_rows, up_cols, own_block, row_index * blocks, blocks)
    down_flags = own_flags(down_cols, down_rows, own_block, row_index * blocks, blocks)
    up_own = up_weight.reshape(blocks, BLK, units) * up_flags.astype(BF)[:, None, None]
    down_own = down_weight.reshape(units, blocks, BLK).transpose(1, 0, 2)
    down_own = down_own * down_flags.astype(BF)[:, None, None]
    both = jnp.concatenate([up_own, down_own], axis=0)
    both = lax.all_gather(both, "zl", axis=0, tiled=False)
    up_all = both[:, :blocks].reshape(n_zl, depth, units)
    down_all = both[:, blocks:]

    query_t, stream_t, cot_t = query_heads.T, stream.T, cotangent.T
    paired = jnp.concatenate([key_heads.T, value_heads.T], axis=0)
    up_pairs = [(i, i + 1) for i in range(seq_devs - 1)]
    before = lax.ppermute(paired, ("zl", "core"), up_pairs)
    after = lax.ppermute(paired, ("zl", "core"), [(j, i) for i, j in up_pairs])
    widened = jnp.concatenate([before, paired, after], axis=1)
    key_ext, value_ext = widened[:head], widened[head:]
    reach_width = lax.dynamic_index_in_dim(
        windows, row_index * col_devs + col_index, 0, keepdims=False
    )
    query_place = seq_index * tok + jnp.arange(tok, dtype=jnp.int32)
    key_place = (seq_index - 1) * tok + jnp.arange(3 * tok, dtype=jnp.int32)
    reached = (
        (jnp.abs(query_place[None, :] - key_place[:, None]) <= reach_width)
        & (key_place[:, None] >= 0)
        & (key_place[:, None] < tok * seq_devs)
    )
    scores = jnp.dot(key_ext.T, query_t, preferred_element_type=F32) * score_scale
    scores = jnp.where(reached, scores, -1e30)
    peak = jnp.max(scores, axis=0, keepdims=True)
    weights = jnp.where(reached, jnp.exp(scores - peak), 0.0)
    probs = weights / jnp.sum(weights, axis=0, keepdims=True)
    probs_low = probs.astype(BF)
    attended = jnp.dot(value_ext, probs_low, preferred_element_type=F32)
    hidden = (stream_t.astype(F32) + attended).astype(BF)
    hidden_f = hidden.astype(F32)
    gain = norm_gain[:, None]
    gained = (hidden_f * gain).astype(BF)
    squares = jnp.sum(hidden_f * hidden_f, axis=0)

    send = jnp.concatenate([gained, cot_t, tail_rows(squares)], axis=0)
    panel = lax.all_gather(send, "zh", axis=0, tiled=False)
    panel = spread(panel, "x")
    other = lax.ppermute(panel, "core", swap)
    panel = jnp.concatenate([panel, other], axis=3).transpose(1, 0, 2, 3)
    feats = panel[:, :, :head].reshape(depth, n_core * tok)
    cots = panel[:, :, head : 2 * head].reshape(depth, n_core * tok)
    square_part = jnp.sum(tail_value(panel[:, :, 2 * head :]), axis=(0, 1))

    pre_part = jnp.einsum("zdf,dt->zft", up_all, feats, preferred_element_type=F32)
    cot_blocks = cots.reshape(blocks, BLK, n_core * tok)
    grad_part = jnp.einsum("zbfd,bdt->zft", down_all, cot_blocks, preferred_element_type=F32)
    square_tail = jnp.broadcast_to(tail_rows(square_part)[None], (n_zl, TAIL, n_core * tok))
    parts = jnp.concatenate([pre_part.astype(BF), grad_part.astype(BF), square_tail], axis=1)
    parts = exchange(parts, "row")
    summed = jnp.sum(parts[:, : 2 * units].astype(F32), axis=0)
    square_total = jnp.sum(tail_value(parts[:, 2 * units :]), axis=0)
    inv_rms = lax.rsqrt(square_total / width_total + EPSILON)
    pre_act = summed[:units] * inv_rms
    activation = gelu_value(pre_act).astype(BF)
    grad_act = (summed[units:] * gelu_slope(pre_act) * inv_rms).astype(BF)
    inner_part = jnp.sum(grad_act.astype(F32) * pre_act, axis=0)
    acts = spread(jnp.concatenate([activation, grad_act, tail_rows(inner_part)], axis=0), "row")
    act_all, grad_all = acts[:, :units], acts[:, units : 2 * units]
    inner_part = jnp.sum(tail_value(acts[:, 2 * units :]), axis=0)

    norm_part = jnp.einsum("zdf,zft->dt", up_all, grad_all, preferred_element_type=F32).astype(BF)
    norm_part = jnp.concatenate([norm_part, tail_rows(inner_part)], axis=0)
    theirs = lax.ppermute(norm_part[:, tok:], "core", swap)
    norm_sum = (norm_part[:depth, :tok].astype(F32) + theirs[:depth].astype(F32)).astype(BF)
    inner_part = tail_value(norm_part[depth:, :tok]) + tail_value(theirs[depth:])
    pieces = norm_sum.reshape(n_zh, n_x, head, tok).transpose(1, 0, 2, 3)
    pieces = pieces.reshape(n_x, n_zh * head, tok)
    inner_tail = jnp.broadcast_to(tail_rows(inner_part)[None], (n_x, TAIL, tok))
    pieces = exchange(jnp.concatenate([pieces, inner_tail], axis=1), "x")
    norm_sum = jnp.sum(pieces[:, : n_zh * head].astype(F32), axis=0).astype(BF)
    inner_part = jnp.sum(tail_value(pieces[:, n_zh * head :]), axis=0)
    inner_tail = jnp.broadcast_to(tail_rows(inner_part)[None], (n_zh, TAIL, tok))
    pieces = jnp.concatenate([norm_sum.reshape(n_zh, head, tok), inner_tail], axis=1)
    pieces = exchange(pieces, "zh")
    grad_norm = jnp.sum(pieces[:, :head].astype(F32), axis=0)
    inner = jnp.sum(tail_value(pieces[:, head:]), axis=0)

    grad_up_part = jnp.einsum("dt,zft->zdf", feats, grad_all, preferred_element_type=F32)
    grad_up_part = grad_up_part.astype(BF).reshape(n_zl, blocks, BLK, units)
    grad_down_part = jnp.einsum("zft,bdt->zbfd", act_all, cot_blocks, preferred_element_type=F32)
    grad_parts = jnp.concatenate([grad_up_part, grad_down_part.astype(BF)], axis=1)
    grad_parts = grad_parts.reshape(n_zl * 2 * depth, units)
    grads = lax.psum_scatter(grad_parts, "zl", scatter_dimension=0, tiled=True)
    grads = grads.reshape(2 * blocks, BLK, units)
    grad_up = grads[:blocks] * up_flags.astype(BF)[:, None, None]
    grad_up = grad_up.reshape(depth, units)
    grad_down = grads[blocks:] * down_flags.astype(BF)[:, None, None]
    grad_down = grad_down.transpose(1, 0, 2).reshape(units, depth)

    grad_gain = lax.psum(jnp.sum(grad_norm * hidden_f, axis=1), ("zl", "core"))
    scale = inv_rms[:tok] * inner / width_total
    grad_hidden = gain * grad_norm - hidden_f * scale + cot_t.astype(F32)
    grad_stream = grad_hidden.astype(BF)
    grad_probs = jnp.dot(value_ext.T, grad_stream, preferred_element_type=F32)
    center = jnp.sum(probs * grad_probs, axis=0, keepdims=True)
    grad_scores = (probs * (grad_probs - center)).astype(BF)
    grad_query = (jnp.dot(key_ext, grad_scores, preferred_element_type=F32) * score_scale).astype(BF)
    key_grad = jnp.dot(query_t, grad_scores.T, preferred_element_type=F32) * score_scale
    value_grad = jnp.dot(grad_stream, probs_low.T, preferred_element_type=F32)
    pair_grads = jnp.concatenate([key_grad, value_grad], axis=0)
    from_upper = lax.ppermute(
        pair_grads[:, :tok].astype(BF), ("zl", "core"), [(j, i) for i, j in up_pairs]
    )
    from_lower = lax.ppermute(pair_grads[:, 2 * tok :].astype(BF), ("zl", "core"), up_pairs)
    pair_total = pair_grads[:, tok : 2 * tok] + from_upper.astype(F32) + from_lower.astype(F32)
    pair_total = pair_total.astype(BF)
    return (
        grad_stream.T,
        grad_query.T,
        pair_total[:head].T,
        pair_total[head:].T,
        grad_gain,
        grad_up,
        grad_down,
    )


def solution(mesh):
    seq, row, col = (mesh.shape[a] for a in ("seq", "row", "col"))
    fine = Mesh(
        mesh.devices.reshape(seq // 2, 2, row, 4, col // 4), ("zl", "core", "row", "zh", "x")
    )
    features = P(("zl", "core"), ("row", "zh", "x"))
    gain_spec = P(("row", "zh", "x"))
    up_spec = P("row", ("zl", "core", "zh", "x"))
    down_spec = P(("zl", "core", "zh", "x"), "row")
    in_specs = (
        (features,) * 4 + (P(), gain_spec, up_spec, down_spec) + (P(),) * 4 + (features,)
    )
    out_specs = (features,) * 4 + (gain_spec, up_spec, down_spec)
    return jax.shard_map(
        on_device, mesh=fine, in_specs=in_specs, out_specs=out_specs, check_vma=False
    )
```

time: 898 us -> 211 us (0.23)
  blocking collectives: 501 us -> 90.7 us
  waiting for transfers between devices: 282 us -> 27.9 us
  starting transfers between devices: 54.9 us -> 42.8 us
  matrix products: 23.1 us -> 11.2 us
    psum x3 -> x1, blocking collectives: 400 us -> 12.7 us  [on_device(): grad_gain = lax.psum(jnp.sum(grad_norm * hidden_f, axis=1), ('zl', 'core'))]
    psum x2 -> x0, waiting for transfers between devices: 280 us -> none  [the longest x1 185 us: on_device(): lax.psum(norm_part.astype(jnp.bfloat16), 'col').astype(jnp.float32)]
    all_gather x2 -> x1, blocking collectives: 101 us -> 23.9 us  [on_device(): panel = lax.all_gather(send, 'zh', axis=0, tiled=False)]
    all_to_all x0 -> x3, blocking collectives: none -> 54.1 us  [the longest x2 35 us: spread(): return lax.all_to_all(copies, axis, 0, 0, tiled=True)]
    ppermute x4 -> x6, starting transfers between devices: 54.7 us -> 31.5 us  [the longest x1 9.73 us: on_device(): lax.ppermute(pair_grads[:, 2 * tok:].astype(BF), ('zl', 'core'), up_pairs)]
    all_to_all x0 -> x2, waiting for transfers between devices: none -> 21.4 us  [exchange(): return lax.all_to_all(pieces, axis, 0, 0, tiled=True)]
    dot_general x13 -> x11, matrix products: 23.1 us -> 11.2 us  [the longest x1 1.84 us: on_device(): attended = jnp.dot(value_ext, probs_low, preferred_element_type=F32)]
    all_to_all x0 -> x2, starting transfers between devices: none -> 11.3 us  [exchange(): return lax.all_to_all(pieces, axis, 0, 0, tiled=True)]
  transfers between devices with their start and end apart: 10 -> 10, of which waited for: 2 -> 4; matrix products, arithmetic and copies ran while one was open for 4% -> 10% of each run, Pallas kernels for 0% -> 0%
where the time goes in v1:
time: 211 us; the launch traced here: 210 us
  blocking collectives  90.7 us (43%)
  starting transfers between devices  42.8 us (20%)
  waiting for transfers between devices  27.9 us (13%)
  between operations  14.9 us (7%)
  other arithmetic  13.5 us (6%)
  matrix products  11.2 us (5%)
  local copies, waits for them, and re-layouts  9.28 us (4%)
    all_to_all x2, blocking collectives, spread(): return lax.all_to_all(copies, axis, 0, 0, tiled=True)  35 us
    all_gather x1, blocking collectives, on_device(): panel = lax.all_gather(send, 'zh', axis=0, tiled=False)  23.9 us
    all_to_all x2, waiting for transfers between devices, exchange(): return lax.all_to_all(pieces, axis, 0, 0, tiled=True)  21.4 us
    all_to_all x1, blocking collectives, exchange(): return lax.all_to_all(pieces, axis, 0, 0, tiled=True)  19 us
    psum x1, blocking collectives, on_device(): grad_gain = lax.psum(jnp.sum(grad_norm * hidden_f, axis=1), ('zl', 'core'))  12.7 us
    all_to_all x2, starting transfers between devices, exchange(): return lax.all_to_all(pieces, axis, 0, 0, tiled=True)  11.3 us
    ppermute x1, starting transfers between devices, on_device(): lax.ppermute(pair_grads[:, 2 * tok:].astype(BF), ('zl', 'core'), up_pairs)  9.73 us
    ppermute x1, starting transfers between devices, on_device(): after = lax.ppermute(paired, ('zl', 'core'), [(j, i) for i, j in up_pairs])  8.77 us
  transfers between devices with their start and end apart: 10, of which 4 were waited for; matrix products, arithmetic and copies ran while one was open for 10% of the time, Pallas kernels for 0%

profile of v1, /device:TPU:1, one launch (start us, length us, event | category | flops | bytes accessed | tf_op | source)
XLA Modules:
  0.0 210.3 jit_solution(17579807227411409077)
XLA Ops:
  7.3 0.8 pad_maximum_fusion.10
  8.1 8.8 %collective-permute-start.1 = (bf16[128,256]{1,0:T(8,128)(2,1)S(1)}, bf16[128,256]{1,0:T(8,128)(2,1)S(1)}, u32[]{:S(2)}, u32[]{:S(2)}) collective-permute-start(bf16[128,256]{1,0:T(8,128)(2,1)S(1)} %pad_maximum_fusion.10), channel_id=1, source_target_pairs={{64,0},{128,64},{192,128},{256,192},{320,256},{384,320},{448,384},... | collective-permute-start | bytes 196616 | tf_op jit(solution)/shard_map/ppermute | solution.py:99
  16.9 1.9 collective-permute-start
  18.8 1.1 copy.94
  20.0 0.2 copy.95
  20.2 0.2 and_reduce_fusion.1
  20.5 0.1 multiply_bitcast_fusion.1
  20.6 0.4 copy-done.25
  21.0 0.1 broadcast_multiply_fusion
  21.1 0.8 pad_maximum_fusion.4
  22.0 0.6 dynamic_slice.4
  22.7 1.2 fusion.90
  23.9 1.4 fusion.8
  25.3 1.8 fusion.36
  27.3 23.9 %all-gather.1 = bf16[576,256]{1,0:T(8,128)(2,1)S(1)} all-gather(bf16[144,256]{1,0:T(8,128)(2,1)S(1)} %pad_maximum_fusion.9), channel_id=3, replica_groups=mesh['zl'=4,'core'=2,'row'=4,'zh'=4,'x'=4] {'zh'}, dimensions={0}, use_global_device_ids=true | all-gather | bytes 368640 | tf_op jit(solution)/shard_map/all_gather | solution.py:126
  51.1 0.1 broadcast_in_dim.19
  51.2 18.8 %all_to_all.25 = bf16[4,4,144,256]{3,2,1,0:T(8,128)(2,1)S(1)} all-to-all(bf16[4,4,144,256]{3,2,1,0:T(8,128)(2,1)S(1)} %broadcast_in_dim.19), channel_id=1, replica_groups=mesh['zl'=4,'core'=2,'row'=4,'zh'=4,'x'=4] {'x'}, dimensions={0} | all-to-all | bytes 2359296 | tf_op jit(solution)/shard_map/all_to_all | solution.py:43
  70.0 4.4 %collective-permute-start.2 = (bf16[4,4,144,256]{3,2,1,0:T(8,128)(2,1)S(1)}, bf16[4,4,144,256]{3,2,1,0:T(8,128)(2,1)S(1)}, u32[]{:S(2)}, u32[]{:S(2)}) collective-permute-start(bf16[4,4,144,256]{3,2,1,0:T(8,128)(2,1)S(1)} %all_to_all.25), channel_id=1, source_target_pairs={{0,64},{64,0},{1,65},{65,1},{2,66},{66,2},{3,67},{67,3},{4,68},{68... | collective-permute-start | bytes 3538952 | tf_op jit(solution)/shard_map/ppermute | solution.py:128
  74.4 2.5 %collective-permute-done.2 = bf16[4,4,144,256]{3,2,1,0:T(8,128)(2,1)S(1)} collective-permute-done((bf16[4,4,144,256]{3,2,1,0:T(8,128)(2,1)S(1)}, bf16[4,4,144,256]{3,2,1,0:T(8,128)(2,1)S(1)}, u32[]{:S(2)}, u32[]{:S(2)}) %collective-permute-start.2) | collective-permute-done | bytes 1179680 | tf_op jit(solution)/shard_map/ppermute | solution.py:128
  76.8 0.2 maximum_bitcast_fusion
  77.1 0.2 fusion.86
  77.3 0.1 copy.98
  77.4 0.1 copy.97
  77.6 3.9 %all-gather.4.cloned.1.call-done = bf16[64,128,128]{2,1,0:T(8,128)(2,1)} async-done(((bf16[16,128,128]{2,1,0:T(8,128)(2,1)}), bf16[64,128,128]{2,1,0:T(8,128)(2,1)}) %all-gather.4.cloned.1.call-update) | async-done | bytes 2097168 | tf_op jit(solution)/shard_map/all_gather | solution.py:91
  81.5 1.4 slice.184
  83.0 0.4 copy-done.5
  83.4 0.7 fusion.1
  84.2 0.7 convolution_convert_fusion.2
  84.9 0.1 pad_maximum_fusion.1
  85.0 19.0 %all_to_all.26 = bf16[4,272,512]{2,1,0:T(8,128)(2,1)S(1)} all-to-all(bf16[4,272,512]{2,1,0:T(8,128)(2,1)S(1)} %pad_maximum_fusion.1), channel_id=1, replica_groups=mesh['zl'=4,'core'=2,'row'=4,'zh'=4,'x'=4] {'row'}, dimensions={0} | all-to-all | bytes 2228224 | tf_op jit(solution)/shard_map/all_to_all | solution.py:47
  104.1 0.1 convert_reduce_fusion
  104.3 0.2 multiply_reduce_fusion.1
  104.5 0.1 broadcast_in_dim.21
  104.6 16.3 %all_to_all.27 = bf16[4,272,512]{2,1,0:T(8,128)(2,1)S(1)} all-to-all(bf16[4,272,512]{2,1,0:T(8,128)(2,1)S(1)} %broadcast_in_dim.21), channel_id=1, replica_groups=mesh['zl'=4,'core'=2,'row'=4,'zh'=4,'x'=4] {'row'}, dimensions={0} | all-to-all | bytes 2228224 | tf_op jit(solution)/shard_map/all_to_all | solution.py:43
  121.0 0.7 bitcast_convert_fusion
  121.7 1.0 copy-done.1
  122.7 4.8 %collective-permute-start.3 = (bf16[1040,256]{1,0:T(8,128)(2,1)S(1)}, bf16[1040,256]{1,0:T(8,128)(2,1)}, u32[]{:S(2)}, u32[]{:S(2)}) collective-permute-start(bf16[1040,256]{1,0:T(8,128)(2,1)S(1)} %pad_maximum_fusion.3), channel_id=1, source_target_pairs={{0,64},{64,0},{1,65},{65,1},{2,66},{66,2},{3,67},{67,3},{4,68},{68... | collective-permute-start | bytes 1597448 | tf_op jit(solution)/shard_map/ppermute | solution.py:153
  127.5 0.7 convolution_convert_fusion.1
  128.3 0.3 copy.113
  128.6 0.8 copy.103
  129.4 0.8 reduce-precision_convert_fusion.4
  130.1 1.3 add_convert_fusion
  131.6 0.8 pad_maximum_fusion.2
  132.4 4.0 %all-to-all-start.3 = ((bf16[4,272,256]{2,1,0:T(8,128)(2,1)}), bf16[4,272,256]{2,1,0:T(8,128)(2,1)S(1)}, u32[]{:S(2)}, u32[]{:S(2)}) async-start(bf16[4,272,256]{2,1,0:T(8,128)(2,1)} %pad_maximum_fusion.2), calls=%async_computation.3 | async-start | bytes 1114112 | tf_op jit(solution)/shard_map/all_to_all | solution.py:47
  136.4 1.8 fusion
  138.2 0.2 pad_maximum_fusion
  138.4 1.6 copy.104
  140.1 5.8 %all-to-all-done.3 = bf16[4,272,256]{2,1,0:T(8,128)(2,1)S(1)} async-done(((bf16[4,272,256]{2,1,0:T(8,128)(2,1)}), bf16[4,272,256]{2,1,0:T(8,128)(2,1)S(1)}, u32[]{:S(2)}, u32[]{:S(2)}) %all-to-all-start.3) | async-done | bytes 557088 | tf_op jit(solution)/shard_map/all_to_all | solution.py:47
  146.1 0.7 pad_maximum_fusion.8
  146.7 7.2 %all-to-all-start.4 = ((bf16[4,80,256]{2,1,0:T(8,128)(2,1)}), bf16[4,80,256]{2,1,0:T(8,128)(2,1)S(1)}, u32[]{:S(2)}, u32[]{:S(2)}) async-start(bf16[4,80,256]{2,1,0:T(8,128)(2,1)} %pad_maximum_fusion.8), calls=%async_computation.4 | async-start | bytes 327680 | tf_op jit(solution)/shard_map/all_to_all | solution.py:47
  154.0 15.6 %all-to-all-done.4 = bf16[4,80,256]{2,1,0:T(8,128)(2,1)S(1)} async-done(((bf16[4,80,256]{2,1,0:T(8,128)(2,1)}), bf16[4,80,256]{2,1,0:T(8,128)(2,1)S(1)}, u32[]{:S(2)}, u32[]{:S(2)}) %all-to-all-start.4) | async-done | bytes 163872 | tf_op jit(solution)/shard_map/all_to_all | solution.py:47
  169.7 0.1 fusion.41
  169.9 1.2 multiply_reduce_fusion
  171.1 1.4 multiply_convert_fusion
  172.5 0.3 fusion.3
  172.8 1.2 fusion.20
  174.1 9.7 %collective-permute-start.5 = (bf16[128,256]{1,0:T(8,128)(2,1)S(1)}, bf16[128,256]{1,0:T(8,128)(2,1)S(1)}, u32[]{:S(2)}, u32[]{:S(2)}) collective-permute-start(bf16[128,256]{1,0:T(8,128)(2,1)S(1)} %get-tuple-element.21), channel_id=1, source_target_pairs={{0,64},{64,128},{128,192},{192,256},{256,320},{320,384},{384,448},... | collective-permute-start | bytes 196616 | tf_op jit(solution)/shard_map/ppermute | solution.py:194
  183.8 1.9 collective-permute-start.4
  185.7 0.8 fusion.4
  186.6 0.7 fusion.43
  187.3 12.7 %psum.7 = f32[64]{0:T(128)} all-reduce(f32[64]{0:T(128)S(1)} %get-tuple-element.24), channel_id=1, replica_groups=mesh['zl'=4,'core'=2,'row'=4,'zh'=4,'x'=4] {'zl','core'}, use_global_device_ids=true, to_apply=%region_16.17 | all-reduce | flops 64 | bytes 512 | tf_op jit(solution)/shard_map/psum | solution.py:180
  200.0 0.6 slice_bitcast_fusion.2
  200.7 1.9 fusion.87
  202.6 0.8 copy_bitcast_fusion
  (113 shorter events, 1.0 us)
Async XLA Ops:
  7.2 15.5 %copy-start = (bf16[256,64]{0,1:T(8,128)(2,1)S(1)}, bf16[256,64]{0,1:T(8,128)(2,1)}, u32[]{:S(2)}) copy-start(bf16[256,64]{0,1:T(8,128)(2,1)} %param.14) | copy-start | bytes 98308
  7.2 13.0 %copy-start.15 = (s32[2048]{0:T(1024)S(1)}, s32[2048]{0:T(1024)}, u32[]{:S(2)}) copy-start(s32[2048]{0:T(1024)} %param.23) | copy-start | bytes 24580
  7.2 13.0 %copy-start.16 = (s32[2048]{0:T(1024)S(1)}, s32[2048]{0:T(1024)}, u32[]{:S(2)}) copy-start(s32[2048]{0:T(1024)} %param.22) | copy-start | bytes 24580
  7.2 13.0 %copy-start.17 = (s32[2048]{0:T(1024)S(1)}, s32[2048]{0:T(1024)}, u32[]{:S(2)}) copy-start(s32[2048]{0:T(1024)} %param.21) | copy-start | bytes 24580
  7.2 13.0 %copy-start.18 = (s32[2048]{0:T(1024)S(1)}, s32[2048]{0:T(1024)}, u32[]{:S(2)}) copy-start(s32[2048]{0:T(1024)} %param.24) | copy-start | bytes 24580
  7.2 13.8 %copy-start.9 = (bf16[1024,128]{1,0:T(8,128)(2,1)S(1)}, bf16[1024,128]{1,0:T(8,128)(2,1)}, u32[]{:S(2)}) copy-start(bf16[1024,128]{1,0:T(8,128)(2,1)} %param.19) | copy-start | bytes 786436
  7.2 74.3 %all-gather.4.cloned.1.call-start = ((), (), s32[]{:S(2)}) async-start(), calls=%async_computation.7 | async-start | bytes 2621440 | tf_op jit(solution)/shard_map/all_gather | solution.py:91
  8.1 14.5 %collective-permute-start.1 = (bf16[128,256]{1,0:T(8,128)(2,1)S(1)}, bf16[128,256]{1,0:T(8,128)(2,1)S(1)}, u32[]{:S(2)}, u32[]{:S(2)}) collective-permute-start(bf16[128,256]{1,0:T(8,128)(2,1)S(1)} %pad_maximum_fusion.10), channel_id=1, source_target_pairs={{64,0},{128,64},{192,128},{256,192},{320,256},{384,320},{448,384},... | collective-permute-start | bytes 196616 | tf_op jit(solution)/shard_map/ppermute | solution.py:99
  16.9 5.7 %collective-permute-start = (bf16[128,256]{1,0:T(8,128)(2,1)S(1)}, bf16[128,256]{1,0:T(8,128)(2,1)S(1)}, u32[]{:S(2)}, u32[]{:S(2)}) collective-permute-start(bf16[128,256]{1,0:T(8,128)(2,1)S(1)} %pad_maximum_fusion.10), channel_id=1, source_target_pairs={{0,64},{64,128},{128,192},{192,256},{256,320},{320,384},{384,448},... | collective-permute-start | bytes 196616 | tf_op jit(solution)/shard_map/ppermute | solution.py:98
  20.5 0.5 copy-start.25
  20.5 0.5 copy-start.27
  21.0 1.0 copy-start.31
  21.0 1.6 copy-start.10
  21.0 1.6 copy-start.11
  22.6 2.7 %copy-start.19 = (s32[256]{0:T(256)}, s32[256]{0:T(256)S(1)}, u32[]{:S(2)}) copy-start(s32[256]{0:T(256)S(1)} %iota_add_fusion.1) | copy-start | bytes 3076
  22.6 2.6 %copy-start.6 = (bf16[128,768]{1,0:T(8,128)(2,1)}, bf16[128,768]{1,0:T(8,128)(2,1)S(1)}, u32[]{:S(2)}) copy-start(bf16[128,768]{1,0:T(8,128)(2,1)S(1)} %pad_maximum_fusion.7) | copy-start | bytes 589828
  22.7 2.6 %copy-start.13 = (bf16[256,64]{0,1:T(8,128)(2,1)S(1)}, bf16[256,64]{0,1:T(8,128)(2,1)}, u32[]{:S(2)}) copy-start(bf16[256,64]{0,1:T(8,128)(2,1)} %param.13) | copy-start | bytes 98308
  22.7 2.6 %copy-start.29 = (f32[64]{0:T(128)S(1)}, f32[64]{0:T(128)}, u32[]{:S(2)}) copy-start(f32[64]{0:T(128)} %param.18) | copy-start | bytes 772
  23.9 3.3 %copy-start.21 = (f32[256]{0:T(256)}, f32[256]{0:T(256)S(1)}, u32[]{:S(2)}) copy-start(f32[256]{0:T(256)S(1)} %get-tuple-element.38) | copy-start | bytes 3076
  25.3 1.9 copy-start.23
  25.3 1.9 copy-start.8
  70.0 6.8 %collective-permute-start.2 = (bf16[4,4,144,256]{3,2,1,0:T(8,128)(2,1)S(1)}, bf16[4,4,144,256]{3,2,1,0:T(8,128)(2,1)S(1)}, u32[]{:S(2)}, u32[]{:S(2)}) collective-permute-start(bf16[4,4,144,256]{3,2,1,0:T(8,128)(2,1)S(1)} %all_to_all.25), channel_id=1, source_target_pairs={{0,64},{64,0},{1,65},{65,1},{2,66},{66,2},{3,67},{67,3},{4,68},{68... | collective-permute-start | bytes 3538952 | tf_op jit(solution)/shard_map/ppermute | solution.py:128
  77.4 5.6 %copy-start.3 = (bf16[4,4,64,512]{3,2,1,0:T(8,128)(2,1)}, bf16[4,4,64,512]{3,2,1,0:T(8,128)(2,1)S(1)}, u32[]{:S(2)}) copy-start(bf16[4,4,64,512]{3,2,1,0:T(8,128)(2,1)S(1)} %copy.98) | copy-start | bytes 3145732
  81.5 1.9 copy-start.5
  120.9 6.6 %copy-start.2 = (bf16[4,272,512]{2,1,0:T(8,128)(2,1)}, bf16[4,272,512]{2,1,0:T(8,128)(2,1)S(1)}, u32[]{:S(2)}) copy-start(bf16[4,272,512]{2,1,0:T(8,128)(2,1)S(1)} %all_to_all.27) | copy-start | bytes 3342340
  121.7 1.0 copy-start.1
  122.7 6.7 %collective-permute-start.3 = (bf16[1040,256]{1,0:T(8,128)(2,1)S(1)}, bf16[1040,256]{1,0:T(8,128)(2,1)}, u32[]{:S(2)}, u32[]{:S(2)}) collective-permute-start(bf16[1040,256]{1,0:T(8,128)(2,1)S(1)} %pad_maximum_fusion.3), channel_id=1, source_target_pairs={{0,64},{64,0},{1,65},{65,1},{2,66},{66,2},{3,67},{67,3},{4,68},{68... | collective-permute-start | bytes 1597448 | tf_op jit(solution)/shard_map/ppermute | solution.py:153
  131.5 4.9 %copy-start.4 = (bf16[4,4,64,512]{3,2,1,0:T(8,128)(2,1)S(1)}, bf16[4,4,64,512]{3,2,1,0:T(8,128)(2,1)}, u32[]{:S(2)}) copy-start(bf16[4,4,64,512]{3,2,1,0:T(8,128)(2,1)} %copy-done.3) | copy-start | bytes 3145732
  132.4 13.5 %all-to-all-start.3 = ((bf16[4,272,256]{2,1,0:T(8,128)(2,1)}), bf16[4,272,256]{2,1,0:T(8,128)(2,1)S(1)}, u32[]{:S(2)}, u32[]{:S(2)}) async-start(bf16[4,272,256]{2,1,0:T(8,128)(2,1)} %pad_maximum_fusion.2), calls=%async_computation.3 | async-start | bytes 1114112 | tf_op jit(solution)/shard_map/all_to_all | solution.py:47
  136.4 64.2 %reduce-scatter.2.cloned.1.call-start = ((), (), s32[]{:S(2)}) async-start(), calls=%async_computation.6 | async-start | bytes 2621440 | tf_op jit(solution)/shard_map/reduce_scatter | solution.py:173
  140.0 13.9 %copy-start.28 = (bf16[8]{0:T(256)(128)(2,1)S(1)}, bf16[8]{0:T(256)(128)(2,1)}, u32[]{:S(2)}) copy-start(bf16[8]{0:T(256)(128)(2,1)} %copy-done.27) | copy-start | bytes 52
  140.0 29.7 %copy-start.30 = (f32[64]{0:T(128)S(1)}, f32[64]{0:T(128)}, u32[]{:S(2)}) copy-start(f32[64]{0:T(128)} %param.18) | copy-start | bytes 772
  140.0 29.8 %copy-start.7 = (bf16[128,768]{1,0:T(8,128)(2,1)S(1)}, bf16[128,768]{1,0:T(8,128)(2,1)}, u32[]{:S(2)}) copy-start(bf16[128,768]{1,0:T(8,128)(2,1)} %copy-done.6) | copy-start | bytes 589828
  140.1 29.8 %copy-start.20 = (s32[256]{0:T(256)S(1)}, s32[256]{0:T(256)}, u32[]{:S(2)}) copy-start(s32[256]{0:T(256)} %copy-done.19) | copy-start | bytes 3076
  140.1 29.8 %copy-start.22 = (f32[256]{0:T(256)S(1)}, f32[256]{0:T(256)}, u32[]{:S(2)}) copy-start(f32[256]{0:T(256)} %copy-done.21) | copy-start | bytes 3076
  140.1 29.8 %copy-start.24 = (f32[256]{0:T(256)S(1)}, f32[256]{0:T(256)}, u32[]{:S(2)}) copy-start(f32[256]{0:T(256)} %copy-done.23) | copy-start | bytes 3076
  146.7 22.9 %all-to-all-start.4 = ((bf16[4,80,256]{2,1,0:T(8,128)(2,1)}), bf16[4,80,256]{2,1,0:T(8,128)(2,1)S(1)}, u32[]{:S(2)}, u32[]{:S(2)}) async-start(bf16[4,80,256]{2,1,0:T(8,128)(2,1)} %pad_maximum_fusion.8), calls=%async_computation.4 | async-start | bytes 327680 | tf_op jit(solution)/shard_map/all_to_all | solution.py:47
  174.0 12.6 %copy-start.12 = (f32[64,256]{1,0:T(8,128)S(1)}, f32[64,256]{1,0:T(8,128)}, u32[]{:S(2)}) copy-start(f32[64,256]{1,0:T(8,128)} %get-tuple-element.40) | copy-start | bytes 196612
  174.0 12.6 %copy-start.14 = (bf16[256,64]{0,1:T(8,128)(2,1)S(1)}, bf16[256,64]{0,1:T(8,128)(2,1)}, u32[]{:S(2)}) copy-start(bf16[256,64]{0,1:T(8,128)(2,1)} %param.13) | copy-start | bytes 98308
  174.1 25.9 %collective-permute-start.5 = (bf16[128,256]{1,0:T(8,128)(2,1)S(1)}, bf16[128,256]{1,0:T(8,128)(2,1)S(1)}, u32[]{:S(2)}, u32[]{:S(2)}) collective-permute-start(bf16[128,256]{1,0:T(8,128)(2,1)S(1)} %get-tuple-element.21), channel_id=1, source_target_pairs={{0,64},{64,128},{128,192},{192,256},{256,320},{320,384},{384,448},... | collective-permute-start | bytes 196616 | tf_op jit(solution)/shard_map/ppermute | solution.py:194
  183.8 18.8 %copy-start.26 = (bf16[8]{0:T(256)(128)(2,1)S(1)}, bf16[8]{0:T(256)(128)(2,1)}, u32[]{:S(2)}) copy-start(bf16[8]{0:T(256)(128)(2,1)} %copy-done.25) | copy-start | bytes 52
  183.8 16.2 %collective-permute-start.4 = (bf16[128,256]{1,0:T(8,128)(2,1)S(1)}, bf16[128,256]{1,0:T(8,128)(2,1)S(1)}, u32[]{:S(2)}, u32[]{:S(2)}) collective-permute-start(bf16[128,256]{1,0:T(8,128)(2,1)S(1)} %get-tuple-element.20), channel_id=1, source_target_pairs={{64,0},{128,64},{192,128},{256,192},{320,256},{384,320},{448,384},... | collective-permute-start | bytes 196616 | tf_op jit(solution)/shard_map/ppermute | solution.py:191
Sparse Core Ops, SparseCore 0:
  22.1 59.4 all-gather.3
  140.1 57.7 reduce-scatter.1

commit v2 on v1

--- a/solution.py
+++ b/solution.py
@@ -51,6 +51,21 @@
     wanted = first_inner + jnp.arange(inner_count, dtype=jnp.int32)
     hit = (inner_ids[None, :] == wanted[:, None]) & (outer_ids == own_outer)[None, :]
     return jnp.any(hit, axis=1)
+
+
+def window_send(array, slot, n_zh, n_zl, n_core, home):
+    ring = n_zh * n_zl
+    pairs = []
+    for place in range(ring):
+        for core in range(n_core):
+            step = (slot - n_zl // 2) * (1 if core == 0 else -1)
+            owner, worker = (
+                ((z % n_zl) * n_core + core) * n_zh + z // n_zl for z in ((place + step) % ring, place)
+            )
+            pairs.append((worker, owner) if home else (owner, worker))
+    if all(source == target for source, target in pairs):
+        return array
+    return lax.ppermute(array, ("zl", "core", "zh"), pairs)
 
 
 def on_device(
@@ -88,9 +103,9 @@
     down_own = down_weight.reshape(units, blocks, BLK).transpose(1, 0, 2)
     down_own = down_own * down_flags.astype(BF)[:, None, None]
     both = jnp.concatenate([up_own, down_own], axis=0)
-    both = lax.all_gather(both, "zl", axis=0, tiled=False)
-    up_all = both[:, :blocks].reshape(n_zl, depth, units)
-    down_all = both[:, blocks:]
+    slots = [window_send(both, w, n_zh, n_zl, n_core, False) for w in range(n_zl)]
+    up_all = jnp.stack([slot[:blocks] for slot in slots]).reshape(n_zl, depth, units)
+    down_all = jnp.stack([slot[blocks:] for slot in slots])
 
     query_t, stream_t, cot_t = query_heads.T, stream.T, cotangent.T
     paired = jnp.concatenate([key_heads.T, value_heads.T], axis=0)
@@ -169,12 +184,12 @@
     grad_up_part = grad_up_part.astype(BF).reshape(n_zl, blocks, BLK, units)
     grad_down_part = jnp.einsum("zft,bdt->zbfd", act_all, cot_blocks, preferred_element_type=F32)
     grad_parts = jnp.concatenate([grad_up_part, grad_down_part.astype(BF)], axis=1)
-    grad_parts = grad_parts.reshape(n_zl * 2 * depth, units)
-    grads = lax.psum_scatter(grad_parts, "zl", scatter_dimension=0, tiled=True)
-    grads = grads.reshape(2 * blocks, BLK, units)
-    grad_up = grads[:blocks] * up_flags.astype(BF)[:, None, None]
+    grads = sum(
+        window_send(grad_parts[w], w, n_zh, n_zl, n_core, True).astype(F32) for w in range(n_zl)
+    )
+    grad_up = (grads[:blocks] * up_flags.astype(F32)[:, None, None]).astype(BF)
     grad_up = grad_up.reshape(depth, units)
-    grad_down = grads[blocks:] * down_flags.astype(BF)[:, None, None]
+    grad_down = (grads[blocks:] * down_flags.astype(F32)[:, None, None]).astype(BF)
     grad_down = grad_down.transpose(1, 0, 2).reshape(units, depth)
 
     grad_gain = lax.psum(jnp.sum(grad_norm * hidden_f, axis=1), ("zl", "core"))

time: 211 us -> 215 us (1.019)
  blocking collectives: 90.7 us -> 72.2 us
  between operations: 14.9 us -> 1.47 us
  starting transfers between devices: 42.8 us -> 55.5 us
  waiting for transfers between devices: 27.9 us -> 39.9 us
  local copies, waits for them, and re-layouts: 9.28 us -> 15.9 us
  other arithmetic: 13.5 us -> 16.2 us
    ppermute x0 -> x6, waiting for transfers between devices: none -> 28 us  [window_send(): return lax.ppermute(array, ('zl', 'core', 'zh'), pairs)]
    all_to_all x2, waiting for transfers between devices: 21.4 us -> 0.01 us  [exchange(): return lax.all_to_all(pieces, axis, 0, 0, tiled=True)]
    all_to_all x2 -> x1, blocking collectives: 35 us -> 16 us  [spread(): return lax.all_to_all(copies, axis, 0, 0, tiled=True)]
    ppermute x0 -> x6, starting transfers between devices: none -> 17.2 us  [window_send(): return lax.ppermute(array, ('zl', 'core', 'zh'), pairs)]
    all_to_all x0 -> x1, waiting for transfers between devices: none -> 11.4 us  [spread(): return lax.all_to_all(copies, axis, 0, 0, tiled=True)]
    ppermute x1, starting transfers between devices: 9.73 us -> 1.92 us  [on_device(): lax.ppermute(pair_grads[:, 2 * tok:].astype(BF), ('zl', 'core'), up_pairs)]
    all_to_all x0 -> x1, starting transfers between devices: none -> 4.51 us  [spread(): return lax.all_to_all(copies, axis, 0, 0, tiled=True)]
    all_gather x1 -> x0, waiting for transfers between devices: 3.94 us -> none  [on_device(): both = lax.all_gather(both, 'zl', axis=0, tiled=False)]
  transfers between devices with their start and end apart: 10 -> 15, of which waited for: 4 -> 6; matrix products, arithmetic and copies ran while one was open for 10% -> 11% of each run, Pallas kernels for 0% -> 0%
where the time goes in v2:
time: 215 us; the launch traced here: 213 us
  blocking collectives  72.2 us (34%)
  starting transfers between devices  55.5 us (26%)
  waiting for transfers between devices  39.9 us (19%)
  other arithmetic  16.2 us (8%)
  local copies, waits for them, and re-layouts  15.9 us (7%)
  matrix products  11.6 us (5%)
    ppermute x6, waiting for transfers between devices, window_send(): return lax.ppermute(array, ('zl', 'core', 'zh'), pairs)  28 us
    all_gather x1, blocking collectives, on_device(): panel = lax.all_gather(send, 'zh', axis=0, tiled=False)  23 us
    all_to_all x1, blocking collectives, exchange(): return lax.all_to_all(pieces, axis, 0, 0, tiled=True)  20.4 us
    ppermute x6, starting transfers between devices, window_send(): return lax.ppermute(array, ('zl', 'core', 'zh'), pairs)  17.2 us
    all_to_all x1, blocking collectives, spread(): return lax.all_to_all(copies, axis, 0, 0, tiled=True)  16 us
    psum x1, blocking collectives, on_device(): grad_gain = lax.psum(jnp.sum(grad_norm * hidden_f, axis=1), ('zl', 'core'))  12.8 us
    all_to_all x1, waiting for transfers between devices, spread(): return lax.all_to_all(copies, axis, 0, 0, tiled=True)  11.4 us
    all_to_all x2, starting transfers between devices, exchange(): return lax.all_to_all(pieces, axis, 0, 0, tiled=True)  10.1 us
  transfers between devices with their start and end apart: 15, of which 6 were waited for; matrix products, arithmetic and copies ran while one was open for 11% of the time, Pallas kernels for 0%

profile of v2, /device:TPU:1, one launch (start us, length us, event | category | flops | bytes accessed | tf_op | source)
XLA Modules:
  0.0 212.7 jit_solution(9326198176971341230)
XLA Ops:
  0.6 0.8 pad_maximum_fusion.13
  1.4 8.8 %collective-permute-start.4 = (bf16[128,256]{1,0:T(8,128)(2,1)S(1)}, bf16[128,256]{1,0:T(8,128)(2,1)S(1)}, u32[]{:S(2)}, u32[]{:S(2)}) collective-permute-start(bf16[128,256]{1,0:T(8,128)(2,1)S(1)} %pad_maximum_fusion.13), channel_id=1, source_target_pairs={{64,0},{128,64},{192,128},{256,192},{320,256},{384,320},{448,384},... | collective-permute-start | bytes 196616 | tf_op jit(solution)/shard_map/ppermute | solution.py:114
  10.2 1.9 collective-permute-start.3
  12.2 1.2 dynamic_slice.4
  13.4 0.7 broadcast_compare_fusion
  14.2 0.9 and_reduce_fusion.1
  15.2 0.8 pad_maximum_fusion.8
  16.0 1.2 fusion.115
  17.2 1.4 fusion.17
  18.6 1.8 fusion.54
  20.6 23.0 %all-gather = bf16[576,256]{1,0:T(8,128)(2,1)S(1)} all-gather(bf16[144,256]{1,0:T(8,128)(2,1)S(1)} %pad_maximum_fusion.12), channel_id=2, replica_groups=mesh['zl'=4,'core'=2,'row'=4,'zh'=4,'x'=4] {'zh'}, dimensions={0}, use_global_device_ids=true | all-gather | bytes 368640 | tf_op jit(solution)/shard_map/all_gather | solution.py:141
  43.6 1.1 broadcast_in_dim.19
  44.7 4.5 %all-to-all-start = ((bf16[4,4,144,256]{3,2,1,0:T(8,128)(2,1)}), bf16[4,4,144,256]{3,2,1,0:T(8,128)(2,1)S(1)}, u32[]{:S(2)}, u32[]{:S(2)}) async-start(bf16[4,4,144,256]{3,2,1,0:T(8,128)(2,1)} %broadcast_in_dim.19), calls=%async_computation | async-start | bytes 2359296 | tf_op jit(solution)/shard_map/all_to_all | solution.py:43
  49.2 0.5 fusion.113
  50.1 0.6 fusion.114
  50.7 0.8 multiply_bitcast_fusion.1
  51.6 1.9 collective-permute-start.2
  53.6 11.4 %all-to-all-done = bf16[4,4,144,256]{3,2,1,0:T(8,128)(2,1)S(1)} async-done(((bf16[4,4,144,256]{3,2,1,0:T(8,128)(2,1)}), bf16[4,4,144,256]{3,2,1,0:T(8,128)(2,1)S(1)}, u32[]{:S(2)}, u32[]{:S(2)}) %all-to-all-start) | async-done | bytes 1179680 | tf_op jit(solution)/shard_map/all_to_all | solution.py:43
  65.0 3.6 %collective-permute-start.5 = (bf16[4,4,144,256]{3,2,1,0:T(8,128)(2,1)S(1)}, bf16[4,4,144,256]{3,2,1,0:T(8,128)(2,1)}, u32[]{:S(2)}, u32[]{:S(2)}) collective-permute-start(bf16[4,4,144,256]{3,2,1,0:T(8,128)(2,1)S(1)} %all-to-all-done), channel_id=1, source_target_pairs={{0,64},{64,0},{1,65},{65,1},{2,66},{66,2},{3,67},{67,3},{4,68},{68... | collective-permute-start | bytes 3538952 | tf_op jit(solution)/shard_map/ppermute | solution.py:143
  68.6 1.9 collective-permute-start.1
  70.5 2.0 collective-permute-start
  72.8 1.8 fusion.110
  74.6 0.9 copy.135
  75.4 5.7 %collective-permute-done.1 = bf16[16,128,128]{2,1,0:T(8,128)(2,1)} collective-permute-done((bf16[16,128,128]{2,1,0:T(8,128)(2,1)S(1)}, bf16[16,128,128]{2,1,0:T(8,128)(2,1)}, u32[]{:S(2)}, u32[]{:S(2)}) %collective-permute-start.1) | collective-permute-done | bytes 524320 | tf_op jit(solution)/shard_map/ppermute | solution.py:68
  81.1 1.8 fusion.109
  82.9 0.9 copy.134
  83.8 2.3 %collective-permute-done = bf16[16,128,128]{2,1,0:T(8,128)(2,1)} collective-permute-done((bf16[16,128,128]{2,1,0:T(8,128)(2,1)S(1)}, bf16[16,128,128]{2,1,0:T(8,128)(2,1)}, u32[]{:S(2)}, u32[]{:S(2)}) %collective-permute-start) | collective-permute-done | bytes 524320 | tf_op jit(solution)/shard_map/ppermute | solution.py:68
  86.0 1.8 fusion.108
  87.8 0.8 copy.133
  88.7 1.5 maximum_bitcast_fusion
  90.8 1.0 copy-done.11
  91.7 0.3 copy-done.12
  92.2 0.7 fusion.2
  93.3 0.7 convolution_convert_fusion.2
  94.1 20.4 %all_to_all.25 = bf16[4,272,512]{2,1,0:T(8,128)(2,1)S(1)} all-to-all(bf16[4,272,512]{2,1,0:T(8,128)(2,1)S(1)} %pad_maximum_fusion), channel_id=1, replica_groups=mesh['zl'=4,'core'=2,'row'=4,'zh'=4,'x'=4] {'row'}, dimensions={0} | all-to-all | bytes 2228224 | tf_op jit(solution)/shard_map/all_to_all | solution.py:47
  115.0 16.0 %all_to_all.26 = bf16[4,272,512]{2,1,0:T(8,128)(2,1)S(1)} all-to-all(bf16[4,272,512]{2,1,0:T(8,128)(2,1)S(1)} %broadcast_in_dim.21), channel_id=1, replica_groups=mesh['zl'=4,'core'=2,'row'=4,'zh'=4,'x'=4] {'row'}, dimensions={0} | all-to-all | bytes 2228224 | tf_op jit(solution)/shard_map/all_to_all | solution.py:43
  131.1 0.8 bitcast_convert_fusion
  132.0 5.0 %collective-permute-start.6 = (bf16[1040,256]{1,0:T(8,128)(2,1)S(1)}, bf16[1040,256]{1,0:T(8,128)(2,1)S(1)}, u32[]{:S(2)}, u32[]{:S(2)}) collective-permute-start(bf16[1040,256]{1,0:T(8,128)(2,1)S(1)} %pad_maximum_fusion.3), channel_id=1, source_target_pairs={{0,64},{64,0},{1,65},{65,1},{2,66},{66,2},{3,67},{67,3},{4,68},{68... | collective-permute-start | bytes 1597448 | tf_op jit(solution)/shard_map/ppermute | solution.py:168
  137.0 0.7 fusion
  137.8 0.3 copy.145
  138.0 0.5 collective-permute-done.6
  138.8 0.8 pad_maximum_fusion.2
  139.6 3.5 %all-to-all-start.3 = ((bf16[4,272,256]{2,1,0:T(8,128)(2,1)}), bf16[4,272,256]{2,1,0:T(8,128)(2,1)S(1)}, u32[]{:S(2)}, u32[]{:S(2)}) async-start(bf16[4,272,256]{2,1,0:T(8,128)(2,1)} %pad_maximum_fusion.2), calls=%async_computation.3 | async-start | bytes 1114112 | tf_op jit(solution)/shard_map/all_to_all | solution.py:47
  143.1 2.1 fusion.1
  145.2 1.2 fusion.21
  146.4 7.4 %collective-permute-start.11 = (bf16[16,128,128]{1,2,0:T(8,128)(2,1)}, bf16[16,128,128]{1,2,0:T(8,128)(2,1)}, u32[]{:S(2)}, u32[]{:S(2)}) collective-permute-start(bf16[16,128,128]{1,2,0:T(8,128)(2,1)} %get-tuple-element.68), channel_id=1, source_target_pairs={{0,128},{64,460},{128,256},{192,64},{256,384},{320,192},{384,4},{4... | collective-permute-start | bytes 1572872 | tf_op jit(solution)/shard_map/ppermute | solution.py:68
  153.9 1.9 collective-permute-start.10
  155.8 2.0 collective-permute-start.9
  158.0 0.7 pad_maximum_fusion.11
  158.6 6.6 %all-to-all-start.4 = ((bf16[4,80,256]{2,1,0:T(8,128)(2,1)}), bf16[4,80,256]{2,1,0:T(8,128)(2,1)S(1)}, u32[]{:S(2)}, u32[]{:S(2)}) async-start(bf16[4,80,256]{2,1,0:T(8,128)(2,1)} %pad_maximum_fusion.11), calls=%async_computation.4 | async-start | bytes 327680 | tf_op jit(solution)/shard_map/all_to_all | solution.py:47
  165.3 1.8 collective-permute-done.10
  167.0 18.3 %collective-permute-done.9 = bf16[16,128,128]{1,2,0:T(8,128)(2,1)} collective-permute-done((bf16[16,128,128]{1,2,0:T(8,128)(2,1)}, bf16[16,128,128]{1,2,0:T(8,128)(2,1)}, u32[]{:S(2)}, u32[]{:S(2)}) %collective-permute-start.9) | collective-permute-done | bytes 524320 | tf_op jit(solution)/shard_map/ppermute | solution.py:68
  185.3 1.7 fusion.13
  187.2 0.9 copy.128
  188.1 0.8 copy.129
  189.1 1.2 multiply_reduce_fusion
  190.4 1.4 multiply_convert_fusion
  191.8 0.8 fusion.5
  192.9 1.2 fusion.38
  194.2 1.9 collective-permute-start.8
  196.1 2.4 %collective-permute-start.7 = (bf16[128,256]{1,0:T(8,128)(2,1)S(1)}, bf16[128,256]{1,0:T(8,128)(2,1)S(1)}, u32[]{:S(2)}, u32[]{:S(2)}) collective-permute-start(bf16[128,256]{1,0:T(8,128)(2,1)S(1)} %get-tuple-element.80), channel_id=1, source_target_pairs={{64,0},{128,64},{192,128},{256,192},{320,256},{384,320},{448,384},... | collective-permute-start | bytes 196616 | tf_op jit(solution)/shard_map/ppermute | solution.py:206
  198.6 0.7 fusion.61
  199.3 12.8 %psum.7 = f32[64]{0:T(128)} all-reduce(f32[64]{0:T(128)S(1)} %get-tuple-element.84), channel_id=1, replica_groups=mesh['zl'=4,'core'=2,'row'=4,'zh'=4,'x'=4] {'zl','core'}, use_global_device_ids=true, to_apply=%region_16.17 | all-reduce | flops 64 | bytes 512 | tf_op jit(solution)/shard_map/psum | solution.py:195
  212.1 0.6 slice_bitcast_fusion.5
  (119 shorter events, 3.7 us)
Async XLA Ops:
  0.6 15.3 %copy-start = (bf16[256,64]{0,1:T(8,128)(2,1)S(1)}, bf16[256,64]{0,1:T(8,128)(2,1)}, u32[]{:S(2)}) copy-start(bf16[256,64]{0,1:T(8,128)(2,1)} %param.14) | copy-start | bytes 98308
  1.4 13.7 %collective-permute-start.4 = (bf16[128,256]{1,0:T(8,128)(2,1)S(1)}, bf16[128,256]{1,0:T(8,128)(2,1)S(1)}, u32[]{:S(2)}, u32[]{:S(2)}) collective-permute-start(bf16[128,256]{1,0:T(8,128)(2,1)S(1)} %pad_maximum_fusion.13), channel_id=1, source_target_pairs={{64,0},{128,64},{192,128},{256,192},{320,256},{384,320},{448,384},... | collective-permute-start | bytes 196616 | tf_op jit(solution)/shard_map/ppermute | solution.py:114
  10.2 4.9 %collective-permute-start.3 = (bf16[128,256]{1,0:T(8,128)(2,1)S(1)}, bf16[128,256]{1,0:T(8,128)(2,1)S(1)}, u32[]{:S(2)}, u32[]{:S(2)}) collective-permute-start(bf16[128,256]{1,0:T(8,128)(2,1)S(1)} %pad_maximum_fusion.13), channel_id=1, source_target_pairs={{0,64},{64,128},{128,192},{192,256},{256,320},{320,384},{384,448},... | collective-permute-start | bytes 196616 | tf_op jit(solution)/shard_map/ppermute | solution.py:113
  15.1 3.4 %copy-start.18 = (s32[256]{0:T(256)}, s32[256]{0:T(256)S(1)}, u32[]{:S(2)}) copy-start(s32[256]{0:T(256)S(1)} %iota_add_fusion.1) | copy-start | bytes 3076
  16.0 2.6 %copy-start.4 = (bf16[128,768]{1,0:T(8,128)(2,1)}, bf16[128,768]{1,0:T(8,128)(2,1)S(1)}, u32[]{:S(2)}) copy-start(bf16[128,768]{1,0:T(8,128)(2,1)S(1)} %pad_maximum_fusion.8) | copy-start | bytes 589828
  16.0 2.6 %copy-start.16 = (bf16[256,64]{0,1:T(8,128)(2,1)S(1)}, bf16[256,64]{0,1:T(8,128)(2,1)}, u32[]{:S(2)}) copy-start(bf16[256,64]{0,1:T(8,128)(2,1)} %param.13) | copy-start | bytes 98308
  16.0 2.6 %copy-start.24 = (f32[64]{0:T(128)S(1)}, f32[64]{0:T(128)}, u32[]{:S(2)}) copy-start(f32[64]{0:T(128)} %param.18) | copy-start | bytes 772
  17.2 3.3 %copy-start.20 = (f32[256]{0:T(256)}, f32[256]{0:T(256)S(1)}, u32[]{:S(2)}) copy-start(f32[256]{0:T(256)S(1)} %get-tuple-element.102) | copy-start | bytes 3076
  18.6 1.9 copy-start.22
  18.6 1.9 copy-start.6
  44.7 5.0 %copy-start.7 = (bf16[128,1024]{1,0:T(8,128)(2,1)S(1)}, bf16[128,1024]{1,0:T(8,128)(2,1)}, u32[]{:S(2)}) copy-start(bf16[128,1024]{1,0:T(8,128)(2,1)} %param.20) | copy-start | bytes 786436
  44.7 20.3 %all-to-all-start = ((bf16[4,4,144,256]{3,2,1,0:T(8,128)(2,1)}), bf16[4,4,144,256]{3,2,1,0:T(8,128)(2,1)S(1)}, u32[]{:S(2)}, u32[]{:S(2)}) async-start(bf16[4,4,144,256]{3,2,1,0:T(8,128)(2,1)} %broadcast_in_dim.19), calls=%async_computation | async-start | bytes 2359296 | tf_op jit(solution)/shard_map/all_to_all | solution.py:43
  49.2 2.3 %copy-start.2 = (bf16[1024,128]{1,0:T(8,128)(2,1)S(1)}, bf16[1024,128]{1,0:T(8,128)(2,1)}, u32[]{:S(2)}) copy-start(bf16[1024,128]{1,0:T(8,128)(2,1)} %param.19) | copy-start | bytes 786436
  51.6 21.1 %collective-permute-start.2 = (bf16[16,128,128]{2,1,0:T(8,128)(2,1)S(1)}, bf16[16,128,128]{2,1,0:T(8,128)(2,1)}, u32[]{:S(2)}, u32[]{:S(2)}) collective-permute-start(bf16[16,128,128]{2,1,0:T(8,128)(2,1)S(1)} %pad_maximum_fusion.5), channel_id=1, source_target_pairs={{128,0},{460,64},{256,128},{64,192},{384,256},{192,320},{4,384},{3... | collective-permute-start | bytes 1572872 | tf_op jit(solution)/shard_map/ppermute | solution.py:68
  65.0 23.7 %collective-permute-start.5 = (bf16[4,4,144,256]{3,2,1,0:T(8,128)(2,1)S(1)}, bf16[4,4,144,256]{3,2,1,0:T(8,128)(2,1)}, u32[]{:S(2)}, u32[]{:S(2)}) collective-permute-start(bf16[4,4,144,256]{3,2,1,0:T(8,128)(2,1)S(1)} %all-to-all-done), channel_id=1, source_target_pairs={{0,64},{64,0},{1,65},{65,1},{2,66},{66,2},{3,67},{67,3},{4,68},{68... | collective-permute-start | bytes 3538952 | tf_op jit(solution)/shard_map/ppermute | solution.py:143
  68.6 12.5 %collective-permute-start.1 = (bf16[16,128,128]{2,1,0:T(8,128)(2,1)S(1)}, bf16[16,128,128]{2,1,0:T(8,128)(2,1)}, u32[]{:S(2)}, u32[]{:S(2)}) collective-permute-start(bf16[16,128,128]{2,1,0:T(8,128)(2,1)S(1)} %pad_maximum_fusion.5), channel_id=1, source_target_pairs={{396,0},{192,64},{0,128},{320,192},{128,256},{448,320},{256,384},{... | collective-permute-start | bytes 1572872 | tf_op jit(solution)/shard_map/ppermute | solution.py:68
  70.5 15.5 %collective-permute-start = (bf16[16,128,128]{2,1,0:T(8,128)(2,1)S(1)}, bf16[16,128,128]{2,1,0:T(8,128)(2,1)}, u32[]{:S(2)}, u32[]{:S(2)}) collective-permute-start(bf16[16,128,128]{2,1,0:T(8,128)(2,1)S(1)} %pad_maximum_fusion.5), channel_id=1, source_target_pairs={{268,0},{320,64},{396,128},{448,192},{0,256},{68,320},{128,384},{1... | collective-permute-start | bytes 1572872 | tf_op jit(solution)/shard_map/ppermute | solution.py:68
  90.6 2.3 %copy-start.3 = (bf16[4,4,64,512]{3,2,1,0:T(8,128)(2,1)}, bf16[4,4,64,512]{3,2,1,0:T(8,128)(2,1)S(1)}, u32[]{:S(2)}) copy-start(bf16[4,4,64,512]{3,2,1,0:T(8,128)(2,1)S(1)} %copy.119) | copy-start | bytes 3145732
  90.6 1.1 copy-start.11
  90.6 1.4 copy-start.12
  90.6 1.5 copy-start.13
  90.6 1.5 copy-start.14
  92.2 0.9 copy-start.8
  92.2 1.0 copy-start.9
  92.2 1.1 copy-start.10
  131.1 5.9 %copy-start.1 = (bf16[4,272,512]{2,1,0:T(8,128)(2,1)}, bf16[4,272,512]{2,1,0:T(8,128)(2,1)S(1)}, u32[]{:S(2)}) copy-start(bf16[4,272,512]{2,1,0:T(8,128)(2,1)S(1)} %all_to_all.26) | copy-start | bytes 3342340
  132.0 6.6 %collective-permute-start.6 = (bf16[1040,256]{1,0:T(8,128)(2,1)S(1)}, bf16[1040,256]{1,0:T(8,128)(2,1)S(1)}, u32[]{:S(2)}, u32[]{:S(2)}) collective-permute-start(bf16[1040,256]{1,0:T(8,128)(2,1)S(1)} %pad_maximum_fusion.3), channel_id=1, source_target_pairs={{0,64},{64,0},{1,65},{65,1},{2,66},{66,2},{3,67},{67,3},{4,68},{68... | collective-permute-start | bytes 1597448 | tf_op jit(solution)/shard_map/ppermute | solution.py:168
  139.6 18.2 %all-to-all-start.3 = ((bf16[4,272,256]{2,1,0:T(8,128)(2,1)}), bf16[4,272,256]{2,1,0:T(8,128)(2,1)S(1)}, u32[]{:S(2)}, u32[]{:S(2)}) async-start(bf16[4,272,256]{2,1,0:T(8,128)(2,1)} %pad_maximum_fusion.2), calls=%async_computation.3 | async-start | bytes 1114112 | tf_op jit(solution)/shard_map/all_to_all | solution.py:47
  146.4 18.8 %collective-permute-start.11 = (bf16[16,128,128]{1,2,0:T(8,128)(2,1)}, bf16[16,128,128]{1,2,0:T(8,128)(2,1)}, u32[]{:S(2)}, u32[]{:S(2)}) collective-permute-start(bf16[16,128,128]{1,2,0:T(8,128)(2,1)} %get-tuple-element.68), channel_id=1, source_target_pairs={{0,128},{64,460},{128,256},{192,64},{256,384},{320,192},{384,4},{4... | collective-permute-start | bytes 1572872 | tf_op jit(solution)/shard_map/ppermute | solution.py:68
  153.9 13.2 %collective-permute-start.10 = (bf16[16,128,128]{1,2,0:T(8,128)(2,1)}, bf16[16,128,128]{1,2,0:T(8,128)(2,1)}, u32[]{:S(2)}, u32[]{:S(2)}) collective-permute-start(bf16[16,128,128]{1,2,0:T(8,128)(2,1)} %get-tuple-element.67), channel_id=1, source_target_pairs={{0,396},{64,192},{128,0},{192,320},{256,128},{320,448},{384,256},{... | collective-permute-start | bytes 1572872 | tf_op jit(solution)/shard_map/ppermute | solution.py:68
  155.8 29.5 %collective-permute-start.9 = (bf16[16,128,128]{1,2,0:T(8,128)(2,1)}, bf16[16,128,128]{1,2,0:T(8,128)(2,1)}, u32[]{:S(2)}, u32[]{:S(2)}) collective-permute-start(bf16[16,128,128]{1,2,0:T(8,128)(2,1)} %get-tuple-element.66), channel_id=1, source_target_pairs={{0,268},{64,320},{128,396},{192,448},{256,0},{320,68},{384,128},{4... | collective-permute-start | bytes 1572872 | tf_op jit(solution)/shard_map/ppermute | solution.py:68
  158.6 30.3 %all-to-all-start.4 = ((bf16[4,80,256]{2,1,0:T(8,128)(2,1)}), bf16[4,80,256]{2,1,0:T(8,128)(2,1)S(1)}, u32[]{:S(2)}, u32[]{:S(2)}) async-start(bf16[4,80,256]{2,1,0:T(8,128)(2,1)} %pad_maximum_fusion.11), calls=%async_computation.4 | async-start | bytes 327680 | tf_op jit(solution)/shard_map/all_to_all | solution.py:47
  165.3 21.7 %copy-start.26 = (f32[8]{0:T(128)S(1)}, f32[8]{0:T(128)}, u32[]{:S(2)}) copy-start(f32[8]{0:T(128)} %get-tuple-element.98) | copy-start | bytes 100
  165.3 21.7 %copy-start.27 = (f32[8]{0:T(128)S(1)}, f32[8]{0:T(128)}, u32[]{:S(2)}) copy-start(f32[8]{0:T(128)} %get-tuple-element.100) | copy-start | bytes 100
  187.0 2.0 copy-start.25
  187.0 2.1 copy-start.5
  187.0 2.1 copy-start.19
  187.0 2.1 copy-start.21
  187.0 2.1 copy-start.23
  192.9 5.7 %copy-start.15 = (f32[64,256]{1,0:T(8,128)S(1)}, f32[64,256]{1,0:T(8,128)}, u32[]{:S(2)}) copy-start(f32[64,256]{1,0:T(8,128)} %get-tuple-element.104) | copy-start | bytes 196612
  192.9 5.7 %copy-start.17 = (bf16[256,64]{0,1:T(8,128)(2,1)S(1)}, bf16[256,64]{0,1:T(8,128)(2,1)}, u32[]{:S(2)}) copy-start(bf16[256,64]{0,1:T(8,128)(2,1)} %param.13) | copy-start | bytes 98308
  194.2 17.9 %collective-permute-start.8 = (bf16[128,256]{1,0:T(8,128)(2,1)S(1)}, bf16[128,256]{1,0:T(8,128)(2,1)S(1)}, u32[]{:S(2)}, u32[]{:S(2)}) collective-permute-start(bf16[128,256]{1,0:T(8,128)(2,1)S(1)} %get-tuple-element.81), channel_id=1, source_target_pairs={{0,64},{64,128},{128,192},{192,256},{256,320},{320,384},{384,448},... | collective-permute-start | bytes 196616 | tf_op jit(solution)/shard_map/ppermute | solution.py:209
  196.1 15.9 %collective-permute-start.7 = (bf16[128,256]{1,0:T(8,128)(2,1)S(1)}, bf16[128,256]{1,0:T(8,128)(2,1)S(1)}, u32[]{:S(2)}, u32[]{:S(2)}) collective-permute-start(bf16[128,256]{1,0:T(8,128)(2,1)S(1)} %get-tuple-element.80), channel_id=1, source_target_pairs={{64,0},{128,64},{192,128},{256,192},{320,256},{384,320},{448,384},... | collective-permute-start | bytes 196616 | tf_op jit(solution)/shard_map/ppermute | solution.py:206

commit v3 on v2

v3 whole, which is shorter than its diff:
```python
import functools

import jax
import jax.numpy as jnp
from jax import lax
from jax.experimental import pallas as pl
from jax.experimental.pallas import tpu as pltpu
from jax.sharding import Mesh
from jax.sharding import PartitionSpec as P

BLK = 128
GELU_C = 0.7978845608028654
GELU_A = 0.044715
EPSILON = 1e-05
TAIL = 16
BF = jnp.bfloat16
F32 = jnp.float32


def gelu_value(pre_act):
    tanh_arg = GELU_C * (pre_act + GELU_A * pre_act * pre_act * pre_act)
    return 0.5 * pre_act * (1.0 + jnp.tanh(tanh_arg))


def gelu_slope(pre_act):
    tanh_arg = GELU_C * (pre_act + GELU_A * pre_act * pre_act * pre_act)
    tanh_val = jnp.tanh(tanh_arg)
    return 0.5 * (1.0 + tanh_val) + 0.5 * pre_act * (1.0 - tanh_val * tanh_val) * GELU_C * (
        1.0 + 3.0 * GELU_A * pre_act * pre_act
    )


def tail_rows(vector):
    high = lax.reduce_precision(vector, 8, 7)
    low = vector - high
    pair = jnp.stack([high, low]).astype(BF)
    return jnp.pad(pair, ((0, TAIL - 2), (0, 0)))


def tail_value(rows):
    return rows[..., 0, :].astype(F32) + rows[..., 1, :].astype(F32)


def spread(array, axis):
    count = lax.axis_size(axis)
    copies = jnp.broadcast_to(array[None], (count,) + array.shape)
    return lax.all_to_all(copies, axis, 0, 0, tiled=True)


def exchange(pieces, axis):
    return lax.all_to_all(pieces, axis, 0, 0, tiled=True)


def window_send(array, slot, n_zh, n_zl, n_core, home):
    ring = n_zh * n_zl
    pairs = []
    for place in range(ring):
        for core in range(n_core):
            step = (slot - n_zl // 2) * (1 if core == 0 else -1)
            owner, worker = (
                ((z % n_zl) * n_core + core) * n_zh + z // n_zl for z in ((place + step) % ring, place)
            )
            pairs.append((worker, owner) if home else (owner, worker))
    if all(source == target for source, target in pairs):
        return array
    return lax.ppermute(array, ("zl", "core", "zh"), pairs)


def call_kernel(body, out_shapes, flops, *operands, loads=0, scratch=()):
    moved = sum(a.size * a.dtype.itemsize for a in operands)
    moved += sum(a.size * a.dtype.itemsize for a in out_shapes)
    vmem = pl.BlockSpec(memory_space=pltpu.VMEM)
    smem = pl.BlockSpec(memory_space=pltpu.SMEM)
    return pl.pallas_call(
        body,
        out_shape=out_shapes,
        in_specs=[pl.BlockSpec(memory_space=pltpu.HBM)] * loads
        + [smem if a.ndim == 1 else vmem for a in operands[loads:]],
        out_specs=[vmem] * len(out_shapes),
        scratch_shapes=list(scratch) + ([pltpu.SemaphoreType.DMA((loads,))] if loads else []),
        compiler_params=pltpu.CompilerParams(vmem_limit_bytes=(60 if loads else 40) * 1024 * 1024),
        cost_estimate=pl.CostEstimate(flops=flops, bytes_accessed=moved, transcendentals=0),
    )(*operands)


def load_all(sources, targets, arrived):
    copies = [
        pltpu.make_async_copy(source, target, arrived.at[i])
        for i, (source, target) in enumerate(zip(sources, targets, strict=True))
    ]
    for copy in copies:
        copy.start()
    for copy in copies:
        copy.wait()


def held(array):
    return pltpu.VMEM(array.shape, array.dtype)


def shaped(shape, dtype):
    return jax.ShapeDtypeStruct(shape, dtype)


def dot_first(left, right):
    return lax.dot_general(left, right, (((0,), (0,)), ((), ())), preferred_element_type=F32)


def dot_last(left, right):
    return lax.dot_general(left, right, (((1,), (1,)), ((), ())), preferred_element_type=F32)


def dot_plain(left, right):
    return jnp.dot(left, right, preferred_element_type=F32)


def write_tail(ref, index, first, vector):
    high = vector.astype(BF)
    low = (vector - high.astype(F32)).astype(BF)
    place = lax.broadcasted_iota(jnp.int32, (TAIL, vector.shape[1]), 0)
    rows = jnp.where(place == 0, high.astype(F32), jnp.where(place == 1, low.astype(F32), 0.0))
    ref[index + (slice(first, first + TAIL), slice(None))] = rows.astype(BF)


def read_tail(rows):
    rows = rows.astype(F32)
    return rows[0:1] + rows[1:2]


def prepare_body(blocks, *refs):
    sources, (both_ref, flag_ref, pair_ref) = refs[:8], refs[8:11]
    up_ref, down_ref, up_in, up_out, down_in, down_out, arrived = refs[11:]
    head = sources[6].shape[0]
    pair_halves = (pair_ref.at[:head, :], pair_ref.at[head:, :])
    load_all(sources, (up_ref, down_ref, up_in, up_out, down_in, down_out) + pair_halves, arrived)
    col_devs = lax.axis_size("zh") * lax.axis_size("x")
    seq_index = lax.axis_index("zl") * lax.axis_size("core") + lax.axis_index("core")
    col_index = lax.axis_index("zh") * lax.axis_size("x") + lax.axis_index("x")
    own_block = seq_index * col_devs + col_index
    first = lax.axis_index("row") * blocks
    for kind, (inner, outer) in enumerate(((up_in, up_out), (down_in, down_out))):
        shifted = jnp.where(outer[...] == own_block, inner[...] - first, -1)
        for b in range(blocks):
            hit = jnp.where(shifted == b, 1.0, 0.0)
            flag = jnp.max(jnp.max(hit, axis=0, keepdims=True), axis=1, keepdims=True)
            flag_ref[kind * blocks + b : kind * blocks + b + 1, :] = jnp.broadcast_to(flag, (1, BLK))
            if kind == 0:
                block = up_ref[b * BLK : (b + 1) * BLK, :]
            else:
                block = down_ref[:, b * BLK : (b + 1) * BLK]
            both_ref[kind * blocks + b] = (block.astype(F32) * flag).astype(BF)


def column(row):
    count = row.shape[1]
    across = lax.broadcasted_iota(jnp.int32, (count, count), 1)
    down = lax.broadcasted_iota(jnp.int32, (count, count), 0)
    return jnp.sum(jnp.where(across == down, row, 0.0), axis=1, keepdims=True)


def reached_part(part, tok, seq_devs, reach):
    seq_index = lax.axis_index("zl") * lax.axis_size("core") + lax.axis_index("core")
    place = lax.broadcasted_iota(jnp.int32, (tok, tok), 0)
    query = lax.broadcasted_iota(jnp.int32, (tok, tok), 1)
    owner = seq_index + (part - 1)
    inside = jnp.logical_and(owner >= 0, owner < seq_devs)
    limit = jnp.where(inside, reach, -1)
    return jnp.abs(place - query + (part - 1) * tok) <= limit


def sort_halo(inside, outside, halo):
    core = lax.axis_index("core")

    @pl.when(core == 0)
    def _():
        halo[0] = outside[...]
        halo[1] = inside[...]

    @pl.when(core != 0)
    def _():
        halo[0] = inside[...]
        halo[1] = outside[...]


def head_probs(parts, query, reach, seq_devs):
    head, tok = query.shape
    scale = float(head) ** (-0.5)
    masks = [reached_part(p, tok, seq_devs, reach) for p in range(3)]
    scores = [
        jnp.where(masks[p], dot_first(parts[p][:head, :], query[...]) * scale, -1e30)
        for p in range(3)
    ]
    peak = functools.reduce(jnp.maximum, [jnp.max(s, axis=0, keepdims=True) for s in scores])
    weights = [jnp.where(masks[p], jnp.exp(scores[p] - peak), 0.0) for p in range(3)]
    total = sum(jnp.sum(w, axis=0, keepdims=True) for w in weights)
    inverse = 1.0 / total
    return [w * inverse for w in weights]


def own_reach(reaches):
    col_devs = lax.axis_size("zh") * lax.axis_size("x")
    col_index = lax.axis_index("zh") * lax.axis_size("x") + lax.axis_index("x")
    return reaches[lax.axis_index("row") * col_devs + col_index]


def attend_body(seq_devs, *refs):
    sources, (inside, outside, own), (send, hidden_ref) = refs[:5], refs[5:8], refs[8:10]
    query, stream, gain_row, reaches, halo, arrived = refs[10:]
    head, tok = query.shape
    cot_rows = send.at[head : 2 * head, :]
    load_all(sources, (query, stream, gain_row, reaches, cot_rows), arrived)
    sort_halo(inside, outside, halo)
    parts = (halo.at[0], own, halo.at[1])
    probs = head_probs(parts, query, own_reach(reaches), seq_devs)
    attended = sum(dot_plain(parts[p][head:, :], probs[p].astype(BF)) for p in range(3))
    hidden = (stream[...].astype(F32) + attended).astype(BF)
    hidden_ref[...] = hidden
    hidden_f = hidden.astype(F32)
    send[:head, :] = (hidden_f * column(gain_row[...])).astype(BF)
    write_tail(send, (), 2 * head, jnp.sum(hidden_f * hidden_f, axis=0, keepdims=True))


def project_body(head, slots, *refs):
    weights, (mine, theirs), (parts, feats, cots) = refs[:slots], refs[slots : slots + 2], refs[slots + 2 :]
    n_x, n_zh, _, tok = mine.shape
    units = weights[0].shape[2]
    blocks = weights[0].shape[0] // 2
    depth = n_x * n_zh * head
    squares = []
    for side, panel in enumerate((mine, theirs)):
        lanes = slice(side * tok, (side + 1) * tok)
        square = jnp.zeros((1, tok), F32)
        for zh in range(n_zh):
            for x in range(n_x):
                rows = slice((zh * n_x + x) * head, (zh * n_x + x + 1) * head)
                feats[rows, lanes] = panel[x, zh, :head, :]
                cots[rows, lanes] = panel[x, zh, head : 2 * head, :]
                square += read_tail(panel[x, zh, 2 * head :, :])
        squares.append(square)
    square = jnp.concatenate(squares, axis=1)
    for w in range(slots):
        up = weights[w][:blocks].reshape(depth, units)
        parts[w, :units, :] = dot_first(up, feats[...]).astype(BF)
        total = jnp.zeros((units, 2 * tok), F32)
        for b in range(blocks):
            total += dot_plain(weights[w][blocks + b], cots[b * BLK : (b + 1) * BLK, :])
        parts[w, units : 2 * units, :] = total.astype(BF)
        write_tail(parts, (w,), 2 * units, square)


def norm_grad_body(head, n_zh, n_x, slots, acts, *refs):
    weights, (own, send) = refs[:slots], refs[slots:]
    units = weights[0].shape[2]
    blocks = weights[0].shape[0] // 2
    tok = acts.shape[2] // 2
    per_block = BLK // head
    for b in range(blocks):
        total = jnp.zeros((BLK, 2 * tok), F32)
        for w in range(slots):
            total += dot_plain(weights[w][b], acts[w, units : 2 * units, :])
        total = total.astype(BF)
        for k in range(per_block):
            zh, x = divmod(b * per_block + k, n_x)
            rows = slice(zh * head, (zh + 1) * head)
            own[x, rows, :] = total[k * head : (k + 1) * head, :tok]
            send[x, rows, :] = total[k * head : (k + 1) * head, tok:]
    inner = sum(read_tail(acts[w, 2 * units :, :]) for w in range(slots))
    for x in range(n_x):
        write_tail(own, (x,), n_zh * head, inner[:, :tok])
        write_tail(send, (x,), n_zh * head, inner[:, tok:])


def weight_grad_body(slots, acts, feats, cots, *homes):
    units = homes[0].shape[2]
    blocks = homes[0].shape[0] // 2
    for w in range(slots):
        grad = acts[w, units : 2 * units, :]
        homes[w][:blocks] = dot_last(feats[...], grad).astype(BF).reshape(blocks, BLK, units)
        active = acts[w, :units, :]
        for b in range(blocks):
            block = dot_last(active, cots[b * BLK : (b + 1) * BLK, :])
            homes[w][blocks + b] = block.astype(BF)


def core_sum_body(rows, own, theirs, out):
    for x in range(own.shape[0]):
        total = own[x, :rows, :].astype(F32) + theirs[x, :rows, :].astype(F32)
        out[x, :rows, :] = total.astype(BF)
        write_tail(out, (x,), rows, read_tail(own[x, rows:, :]) + read_tail(theirs[x, rows:, :]))


def x_sum_body(head, pieces, out):
    n_zh = out.shape[0]
    rows = n_zh * head
    inner = sum(read_tail(pieces[x, rows:, :]) for x in range(pieces.shape[0]))
    for zh in range(n_zh):
        span = slice(zh * head, (zh + 1) * head)
        total = sum(pieces[x, span, :].astype(F32) for x in range(pieces.shape[0]))
        out[zh, :head, :] = total.astype(BF)
        write_tail(out, (zh,), head, inner)


def attend_grad_body(width_total, seq_devs, *refs):
    cot, gain_row, reaches, query, pieces, hidden, inv_rms, inside, outside, own = refs[:10]
    stream_out, query_out, inside_out, outside_out, own_out, gain_out, halo = refs[10:]
    head, tok = query.shape
    scale = float(head) ** (-0.5)
    grad_norm = sum(pieces[z, :head, :].astype(F32) for z in range(pieces.shape[0]))
    inner = sum(read_tail(pieces[z, head:, :]) for z in range(pieces.shape[0]))
    hidden_f = hidden[...].astype(F32)
    ones = jnp.ones((gain_out.shape[0], tok), F32)
    gain_out[...] = lax.dot_general(
        ones,
        grad_norm * hidden_f,
        (((1,), (1,)), ((), ())),
        precision=lax.Precision.HIGHEST,
        preferred_element_type=F32,
    )
    shrink = inv_rms[:, :tok] * inner / width_total
    grad_hidden = column(gain_row[...]) * grad_norm - hidden_f * shrink + cot[...].astype(F32)
    grad_stream = grad_hidden.astype(BF)
    stream_out[...] = grad_stream
    sort_halo(inside, outside, halo)
    parts = (halo.at[0], own, halo.at[1])
    probs = head_probs(parts, query, own_reach(reaches), seq_devs)
    grad_probs = [dot_first(parts[p][head:, :], grad_stream) for p in range(3)]
    center = sum(jnp.sum(probs[p] * grad_probs[p], axis=0, keepdims=True) for p in range(3))
    grad_query = jnp.zeros((head, tok), F32)
    for p in range(3):
        grad_scores = (probs[p] * (grad_probs[p] - center)).astype(BF)
        grad_query += dot_plain(parts[p][:head, :], grad_scores)
        key_grad = dot_last(query[...], grad_scores) * scale
        value_grad = dot_last(grad_stream, probs[p].astype(BF))
        if p == 1:
            own_out[:head, :] = key_grad
            own_out[head:, :] = value_grad
        else:
            halo[p // 2, :head, :] = key_grad.astype(BF)
            halo[p // 2, head:, :] = value_grad.astype(BF)
    query_out[...] = (grad_query * scale).astype(BF)
    core = lax.axis_index("core")

    @pl.when(core == 0)
    def _():
        outside_out[...] = halo[0]
        inside_out[...] = halo[1]

    @pl.when(core != 0)
    def _():
        inside_out[...] = halo[0]
        outside_out[...] = halo[1]


def home_sum_body(slots, *refs):
    homes, (flags, grad_up, grad_down) = refs[:slots], refs[slots:]
    blocks = homes[0].shape[0] // 2
    for b in range(2 * blocks):
        total = sum(homes[w][b].astype(F32) for w in range(slots)) * flags[b : b + 1, :]
        if b < blocks:
            grad_up[b * BLK : (b + 1) * BLK, :] = total.astype(BF)
        else:
            grad_down[:, (b - blocks) * BLK : (b - blocks + 1) * BLK] = total.astype(BF)


def pair_sum_body(own, inside, outside, gains, key_out, value_out, gain_out):
    head = key_out.shape[0]
    gain_out[...] = jnp.sum(gains[...], axis=0, keepdims=True)
    total = (own[...] + inside[...].astype(F32) + outside[...].astype(F32)).astype(BF)
    key_out[...] = total[:head, :]
    value_out[...] = total[head:, :]


def on_device(
    stream,
    query_heads,
    key_heads,
    value_heads,
    windows,
    norm_gain,
    up_weight,
    down_weight,
    up_rows,
    up_cols,
    down_rows,
    down_cols,
    cotangent,
):
    tok, head = stream.shape
    n_zl, n_core, n_row, n_zh, n_x = (lax.axis_size(a) for a in ("zl", "core", "row", "zh", "x"))
    seq_devs = n_zl * n_core
    col_devs = n_zh * n_x
    row_index = lax.axis_index("row")
    col_index = lax.axis_index(("zh", "x"))
    width_total = head * n_row * col_devs
    depth, units = up_weight.shape
    blocks = depth // BLK
    both_toks = n_core * tok
    swap = [(i, n_core - 1 - i) for i in range(n_core)]
    cross = [(i, i + 1) for i in range(1, seq_devs - 1, 2)]
    cross += [(j, i) for i, j in cross]
    query_t, stream_t, cot_t = query_heads.T, stream.T, cotangent.T
    gain = norm_gain[None, :]

    ids = [a.reshape(-1, BLK) for a in (up_rows, up_cols, down_cols, down_rows)]
    both, flags, paired = call_kernel(
        functools.partial(prepare_body, blocks),
        [
            shaped((2 * blocks, BLK, units), BF),
            shaped((2 * blocks, BLK), F32),
            shaped((2 * head, tok), BF),
        ],
        0,
        up_weight,
        down_weight,
        *ids,
        key_heads.T,
        value_heads.T,
        loads=8,
        scratch=[held(a) for a in (up_weight, down_weight, *ids)],
    )
    inside = lax.ppermute(paired, "core", swap)
    outside = lax.ppermute(paired, ("zl", "core"), cross)

    halo = pltpu.VMEM((2, 2 * head, tok), BF)
    reaches = pltpu.SMEM(windows.shape, windows.dtype)
    send, hidden = call_kernel(
        functools.partial(attend_body, seq_devs),
        [shaped((2 * head + TAIL, tok), BF), shaped((head, tok), BF)],
        12 * tok * tok * head,
        query_t,
        stream_t,
        gain,
        windows,
        cot_t,
        inside,
        outside,
        paired,
        loads=5,
        scratch=[held(query_t), held(stream_t), held(gain), reaches, halo],
    )
    near = [window_send(both, w, n_zh, n_zl, n_core, False) for w in (1, 3)]

    panel = lax.all_gather(send, "zh", axis=0, tiled=False)
    panel, near = lax.optimization_barrier((panel, near))
    far = window_send(near[0], 1, n_zh, n_zl, n_core, False)
    panel = spread(panel, "x")
    panel, far = lax.optimization_barrier((panel, far))
    other = lax.ppermute(panel, "core", swap)
    slots = [far, near[0], both, near[1]]

    parts, feats, cots = call_kernel(
        functools.partial(project_body, head, n_zl),
        [
            shaped((n_zl, 2 * units + TAIL, both_toks), BF),
            shaped((depth, both_toks), BF),
            shaped((depth, both_toks), BF),
        ],
        4 * n_zl * depth * units * both_toks,
        *slots,
        panel,
        other,
    )
    parts = exchange(parts, "row")
    summed = jnp.sum(parts[:, : 2 * units].astype(F32), axis=0)
    square_total = jnp.sum(tail_value(parts[:, 2 * units :]), axis=0)
    inv_rms = lax.rsqrt(square_total / width_total + EPSILON)
    pre_act = summed[:units] * inv_rms
    activation = gelu_value(pre_act).astype(BF)
    grad_act = (summed[units:] * gelu_slope(pre_act) * inv_rms).astype(BF)
    inner_part = jnp.sum(grad_act.astype(F32) * pre_act, axis=0)
    acts = spread(jnp.concatenate([activation, grad_act, tail_rows(inner_part)], axis=0), "row")

    mine, theirs = call_kernel(
        functools.partial(norm_grad_body, head, n_zh, n_x, n_zl),
        [shaped((n_x, n_zh * head + TAIL, tok), BF)] * 2,
        2 * n_zl * depth * units * both_toks,
        acts,
        *slots,
    )
    theirs = lax.ppermute(theirs, "core", swap)
    homes = call_kernel(
        functools.partial(weight_grad_body, n_zl),
        [shaped((2 * blocks, BLK, units), BF)] * n_zl,
        4 * n_zl * depth * units * both_toks,
        acts,
        feats,
        cots,
    )
    pieces = call_kernel(
        functools.partial(core_sum_body, n_zh * head),
        [shaped((n_x, n_zh * head + TAIL, tok), BF)],
        0,
        mine,
        theirs,
    )[0]
    pieces = exchange(pieces, "x")
    pieces = call_kernel(
        functools.partial(x_sum_body, head),
        [shaped((n_zh, head + TAIL, tok), BF)],
        0,
        pieces,
    )[0]
    far = window_send(homes[0], 1, n_zh, n_zl, n_core, True)
    near = window_send(homes[3], 3, n_zh, n_zl, n_core, True)
    pieces, far = lax.optimization_barrier((pieces, far))
    far = (homes[1].astype(F32) + far.astype(F32)).astype(BF)
    far = window_send(far, 1, n_zh, n_zl, n_core, True)
    pieces = exchange(pieces, "zh")
    grad_stream, grad_query, inside_grad, outside_grad, own, gain_parts = call_kernel(
        functools.partial(attend_grad_body, width_total, seq_devs),
        [
            shaped((head, tok), BF),
            shaped((head, tok), BF),
            shaped((2 * head, tok), BF),
            shaped((2 * head, tok), BF),
            shaped((2 * head, tok), F32),
            shaped((seq_devs, head), F32),
        ],
        30 * tok * tok * head,
        cot_t,
        gain,
        windows,
        query_t,
        pieces,
        hidden,
        inv_rms[None],
        inside,
        outside,
        paired,
        scratch=[halo],
    )
    gain_parts, far, near = lax.optimization_barrier((gain_parts, far, near))
    gain_parts = exchange(gain_parts, ("zl", "core"))
    inside_grad = lax.ppermute(inside_grad, "core", swap)
    outside_grad = lax.ppermute(outside_grad, ("zl", "core"), cross)
    grad_up, grad_down = call_kernel(
        functools.partial(home_sum_body, 3),
        [shaped((depth, units), BF), shaped((units, depth), BF)],
        0,
        far,
        near,
        homes[2],
        flags,
    )
    grad_key, grad_value, grad_gain = call_kernel(
        pair_sum_body,
        [shaped((head, tok), BF), shaped((head, tok), BF), shaped((1, head), F32)],
        0,
        own,
        inside_grad,
        outside_grad,
        gain_parts,
    )
    grad_gain = grad_gain.reshape(head)
    return (
        grad_stream.T,
        grad_query.T,
        grad_key.T,
        grad_value.T,
        grad_gain,
        grad_up,
        grad_down,
    )


def solution(mesh):
    seq, row, col = (mesh.shape[a] for a in ("seq", "row", "col"))
    fine = Mesh(
        mesh.devices.reshape(seq // 2, 2, row, 4, col // 4), ("zl", "core", "row", "zh", "x")
    )
    features = P(("zl", "core"), ("row", "zh", "x"))
    gain_spec = P(("row", "zh", "x"))
    up_spec = P("row", ("zl", "core", "zh", "x"))
    down_spec = P(("zl", "core", "zh", "x"), "row")
    in_specs = (
        (features,) * 4 + (P(), gain_spec, up_spec, down_spec) + (P(),) * 4 + (features,)
    )
    out_specs = (features,) * 4 + (gain_spec, up_spec, down_spec)
    return jax.shard_map(
        on_device, mesh=fine, in_specs=in_specs, out_specs=out_specs, check_vma=False
    )
```

time: 215 us -> 184 us (0.86)
  Pallas kernels: 0 us -> 16.7 us
  other arithmetic: 16.2 us -> 1.65 us
  local copies, waits for them, and re-layouts: 15.9 us -> 1.9 us
  matrix products: 11.6 us -> 0 us
  starting transfers between devices: 55.5 us -> 67.1 us
  blocking collectives: 72.2 us -> 61.2 us
  waiting for transfers between devices: 39.9 us -> 33.2 us
    ppermute x6, waiting for transfers between devices: 28 us -> 8.01 us  [window_send(): return lax.ppermute(array, ('zl', 'core', 'zh'), pairs)]
    pallas_call x0 -> x10, Pallas kernels: none -> 16.7 us  [call_kernel(): pl.pallas_call(body, out_shape=out_shapes, in_specs=[pl.BlockSpec(memory_...]
    all_to_all x2 -> x3, waiting for transfers between devices: 0.01 us -> 15.5 us  [exchange(): return lax.all_to_all(pieces, axis, 0, 0, tiled=True)]
    psum x1 -> x0, blocking collectives: 12.8 us -> none  [on_device(): grad_gain = lax.psum(jnp.sum(grad_norm * hidden_f, axis=1), ('zl', 'core'))]
    dot_general x11 -> x0, matrix products: 11.6 us -> none  [the longest x1 2.09 us: on_device(): jnp.einsum('zft,bdt->zbfd', act_all, cot_blocks, preferred_element_type=F32)]
    ppermute x6, starting transfers between devices: 17.2 us -> 28.5 us  [window_send(): return lax.ppermute(array, ('zl', 'core', 'zh'), pairs)]
    all_to_all x1, waiting for transfers between devices: 11.4 us -> 3.22 us  [spread(): return lax.all_to_all(copies, axis, 0, 0, tiled=True)]
    slice x8 -> x0, local copies, waits for them, and re-layouts: 5.76 us -> none  [the longest x3 5.35 us: on_device(): slot[:blocks]]
  transfers between devices with their start and end apart: 15 -> 16, of which waited for: 6 -> 7; matrix products, arithmetic and copies ran while one was open for 11% -> 1% of each run, Pallas kernels for 0% -> 6%
where the time goes in v3:
time: 184 us; the launch traced here: 183 us
  starting transfers between devices  67.1 us (36%)
  blocking collectives  61.2 us (33%)
  waiting for transfers between devices  33.2 us (18%)
  Pallas kernels  16.7 us (9%)
  local copies, waits for them, and re-layouts  1.9 us (1%)
    ppermute x6, starting transfers between devices, window_send(): return lax.ppermute(array, ('zl', 'core', 'zh'), pairs)  28.5 us
    all_gather x1, blocking collectives, on_device(): panel = lax.all_gather(send, 'zh', axis=0, tiled=False)  25.3 us
    all_to_all x1, blocking collectives, exchange(): return lax.all_to_all(pieces, axis, 0, 0, tiled=True)  19.2 us
    all_to_all x1, blocking collectives, spread(): return lax.all_to_all(copies, axis, 0, 0, tiled=True)  16.7 us
    pallas_call x10, Pallas kernels, call_kernel(): pl.pallas_call(body, out_shape=out_shapes, in_specs=[pl.BlockSpec(memory_...  16.7 us
    all_to_all x3, waiting for transfers between devices, exchange(): return lax.all_to_all(pieces, axis, 0, 0, tiled=True)  15.5 us
    all_to_all x3, starting transfers between devices, exchange(): return lax.all_to_all(pieces, axis, 0, 0, tiled=True)  14.8 us
    ppermute x6, waiting for transfers between devices, window_send(): return lax.ppermute(array, ('zl', 'core', 'zh'), pairs)  8.01 us
  transfers between devices with their start and end apart: 16, of which 7 were waited for; matrix products, arithmetic and copies ran while one was open for 1% of the time, Pallas kernels for 6%

profile of v3, /device:TPU:1, one launch (start us, length us, event | category | flops | bytes accessed | tf_op | source)
XLA Modules:
  0.0 182.5 jit_solution(13294203308361700820)
XLA Ops:
  0.6 2.0 %shard_map.180 = (bf16[16,128,128]{2,1,0:T(8,128)(2,1)}, f32[16,128]{1,0:T(8,128)}, bf16[128,256]{1,0:T(8,128)(2,1)}) custom-call(bf16[1024,128]{1,0:T(8,128)(2,1)} %refs_0_.1, bf16[128,1024]{1,0:T(8,128)(2,1)} %refs_1_.1, s32[16,128]{1,0:T(8,128)} %bitcast.34, s32[16,128]{1,0:T(8,128)} %bitcast.35, s32[16,128]{1,0:T(8,128)} %bitcast.36, ...), custom_call_target="tpu_custom_call" | custom-call | bytes 1220608 | tf_op jit(solution)/shard_map/pallas_call | solution.py:74
  2.7 4.4 %collective-permute-start.3 = (bf16[16,128,128]{2,1,0:T(8,128)(2,1)}, bf16[16,128,128]{2,1,0:T(8,128)(2,1)S(1)}, u32[]{:S(2)}, u32[]{:S(2)}) collective-permute-start(bf16[16,128,128]{2,1,0:T(8,128)(2,1)} %get-tuple-element.44.refs_2_), channel_id=1, source_target_pairs={{128,0},{460,64},{256,128},{64,192},{384,256},{192,320},{4,384},{3... | collective-permute-start | bytes 1572872 | tf_op jit(solution)/shard_map/ppermute | solution.py:66
  7.1 9.5 %collective-permute-start.2 = (bf16[16,128,128]{2,1,0:T(8,128)(2,1)}, bf16[16,128,128]{2,1,0:T(8,128)(2,1)S(1)}, u32[]{:S(2)}, u32[]{:S(2)}) collective-permute-start(bf16[16,128,128]{2,1,0:T(8,128)(2,1)} %get-tuple-element.44.refs_2_), channel_id=1, source_target_pairs={{396,0},{192,64},{0,128},{320,192},{128,256},{448,320},{256,384},{... | collective-permute-start | bytes 1572872 | tf_op jit(solution)/shard_map/ppermute | solution.py:66
  16.6 1.9 %collective-permute-start.1 = (bf16[128,256]{1,0:T(8,128)(2,1)}, bf16[128,256]{1,0:T(8,128)(2,1)S(1)}, u32[]{:S(2)}, u32[]{:S(2)}) collective-permute-start(bf16[128,256]{1,0:T(8,128)(2,1)} %get-tuple-element.42.refs_7_.refs_9_), channel_id=1, source_target_pairs={{64,128},{192,256},{320,384},{128,64},{256,192},{384,320},{65,129}... | collective-permute-start | bytes 196616 | tf_op jit(solution)/shard_map/ppermute | solution.py:422
  18.5 1.9 %collective-permute-start = (bf16[128,256]{1,0:T(8,128)(2,1)}, bf16[128,256]{1,0:T(8,128)(2,1)S(1)}, u32[]{:S(2)}, u32[]{:S(2)}) collective-permute-start(bf16[128,256]{1,0:T(8,128)(2,1)} %get-tuple-element.42.refs_7_.refs_9_), channel_id=1, source_target_pairs={{0,64},{64,0},{1,65},{65,1},{2,66},{66,2},{3,67},{67,3},{4,68},{68... | collective-permute-start | bytes 196616 | tf_op jit(solution)/shard_map/ppermute | solution.py:421
  20.4 3.6 %collective-permute-done.1.refs_6_.refs_8_ = bf16[128,256]{1,0:T(8,128)(2,1)S(1)} collective-permute-done((bf16[128,256]{1,0:T(8,128)(2,1)}, bf16[128,256]{1,0:T(8,128)(2,1)S(1)}, u32[]{:S(2)}, u32[]{:S(2)}) %collective-permute-start.1) | collective-permute-done | bytes 65568 | tf_op jit(solution)/shard_map/ppermute | solution.py:422
  24.0 0.0 collective-permute-done.refs_5_.refs_7_
  24.0 0.6 copy-done.2
  24.6 0.0 copy-done.4
  24.7 3.2 %shard_map.181 = (bf16[144,256]{1,0:T(8,128)(2,1)}, bf16[64,256]{1,0:T(8,128)(2,1)}) custom-call(bf16[64,256]{1,0:T(8,128)(2,1)} %bitcast.24, bf16[64,256]{1,0:T(8,128)(2,1)} %bitcast.33, f32[1,64]{1,0:T(1,128)} %bitcast.28, s32[64]{0:T(128)} %refs_2_.1, bf16[64,256]{1,0:T(8,128)(2,1)} %bitcast.22, bf16[128,256]{1,0:T(8,128)(2,1)} %copy-done.4, ...), custom_call_target="tpu_custom_call" | custom-call | flops 50331648 | bytes 401920 | tf_op jit(solution)/shard_map/pallas_call | solution.py:74
  27.9 25.3 %all-gather = bf16[576,256]{1,0:T(8,128)(2,1)S(1)} all-gather(bf16[144,256]{1,0:T(8,128)(2,1)} %get-tuple-element.43), channel_id=2, replica_groups=mesh['zl'=4,'core'=2,'row'=4,'zh'=4,'x'=4] {'zh'}, dimensions={0}, use_global_device_ids=true | all-gather | bytes 368640 | tf_op jit(solution)/shard_map/all_gather | solution.py:443
  53.2 0.0 collective-permute-done.3.refs_3_
  53.2 0.0 collective-permute-done.2.refs_1_
  53.2 1.1 broadcast_in_dim.7
  54.3 4.2 %all-to-all-start = ((bf16[4,4,144,256]{3,2,1,0:T(8,128)(2,1)}), bf16[4,4,144,256]{3,2,1,0:T(8,128)(2,1)S(1)}, u32[]{:S(2)}, u32[]{:S(2)}) async-start(bf16[4,4,144,256]{3,2,1,0:T(8,128)(2,1)} %broadcast_in_dim.7), calls=%async_computation | async-start | bytes 2359296 | tf_op jit(solution)/shard_map/all_to_all | solution.py:47
  58.5 1.9 %collective-permute-start.4 = (bf16[16,128,128]{2,1,0:T(8,128)(2,1)S(1)}, bf16[16,128,128]{2,1,0:T(8,128)(2,1)S(1)}, u32[]{:S(2)}, u32[]{:S(2)}) collective-permute-start(bf16[16,128,128]{2,1,0:T(8,128)(2,1)S(1)} %collective-permute-done.2.refs_1_), channel_id=1, source_target_pairs={{396,0},{192,64},{0,128},{320,192},{128,256},{448,320},{256,384},{... | collective-permute-start | bytes 1572872 | tf_op jit(solution)/shard_map/ppermute | solution.py:66
  60.4 8.0 %collective-permute-done.4.refs_0_ = bf16[16,128,128]{2,1,0:T(8,128)(2,1)S(1)} collective-permute-done((bf16[16,128,128]{2,1,0:T(8,128)(2,1)S(1)}, bf16[16,128,128]{2,1,0:T(8,128)(2,1)S(1)}, u32[]{:S(2)}, u32[]{:S(2)}) %collective-permute-start.4) | collective-permute-done | bytes 524320 | tf_op jit(solution)/shard_map/ppermute | solution.py:66
  68.4 3.2 %all-to-all-done.refs_4_ = bf16[4,4,144,256]{3,2,1,0:T(8,128)(2,1)S(1)} async-done(((bf16[4,4,144,256]{3,2,1,0:T(8,128)(2,1)}), bf16[4,4,144,256]{3,2,1,0:T(8,128)(2,1)S(1)}, u32[]{:S(2)}, u32[]{:S(2)}) %all-to-all-start) | async-done | bytes 1179680 | tf_op jit(solution)/shard_map/all_to_all | solution.py:47
  71.6 1.9 %collective-permute-start.5 = (bf16[4,4,144,256]{3,2,1,0:T(8,128)(2,1)S(1)}, bf16[4,4,144,256]{3,2,1,0:T(8,128)(2,1)S(1)}, u32[]{:S(2)}, u32[]{:S(2)}) collective-permute-start(bf16[4,4,144,256]{3,2,1,0:T(8,128)(2,1)S(1)} %all-to-all-done.refs_4_), channel_id=1, source_target_pairs={{0,64},{64,0},{1,65},{65,1},{2,66},{66,2},{3,67},{67,3},{4,68},{68... | collective-permute-start | bytes 3538952 | tf_op jit(solution)/shard_map/ppermute | solution.py:448
  73.5 2.8 %collective-permute-done.5.refs_5_ = bf16[4,4,144,256]{3,2,1,0:T(8,128)(2,1)S(1)} collective-permute-done((bf16[4,4,144,256]{3,2,1,0:T(8,128)(2,1)S(1)}, bf16[4,4,144,256]{3,2,1,0:T(8,128)(2,1)S(1)}, u32[]{:S(2)}, u32[]{:S(2)}) %collective-permute-start.5) | collective-permute-done | bytes 1179680 | tf_op jit(solution)/shard_map/ppermute | solution.py:448
  76.3 0.0 copy-done
  76.3 1.9 %shard_map.182 = (bf16[4,272,512]{2,1,0:T(8,128)(2,1)S(1)}, bf16[1024,512]{1,0:T(8,128)(2,1)S(1)}, bf16[1024,512]{1,0:T(8,128)(2,1)S(1)}) custom-call(bf16[16,128,128]{2,1,0:T(8,128)(2,1)S(1)} %collective-permute-done.4.refs_0_, bf16[16,128,128]{2,1,0:T(8,128)(2,1)S(1)} %collective-permute-done.2.refs_1_, bf16[16,128,128]{2,1,0:T(8,128)(2,1)S(1)} %copy-done, ...), custom_call_target="tpu_custom_call" | custom-call | flops 1073741824 | bytes 7667712 | tf_op jit(solution)/shard_map/pallas_call | solution.py:74
  78.2 19.2 %all_to_all.36 = bf16[4,272,512]{2,1,0:T(8,128)(2,1)S(1)} all-to-all(bf16[4,272,512]{2,1,0:T(8,128)(2,1)S(1)} %get-tuple-element.50), channel_id=1, replica_groups=mesh['zl'=4,'core'=2,'row'=4,'zh'=4,'x'=4] {'row'}, dimensions={0} | all-to-all | bytes 2228224 | tf_op jit(solution)/shard_map/all_to_all | solution.py:51
  97.4 0.1 convert_reduce_fusion
  97.6 0.2 multiply_reduce_fusion
  97.9 0.1 broadcast_in_dim.8
  98.0 16.7 %all_to_all.37.acts = bf16[4,272,512]{2,1,0:T(8,128)(2,1)S(1)} all-to-all(bf16[4,272,512]{2,1,0:T(8,128)(2,1)S(1)} %broadcast_in_dim.8), channel_id=1, replica_groups=mesh['zl'=4,'core'=2,'row'=4,'zh'=4,'x'=4] {'row'}, dimensions={0} | all-to-all | bytes 2228224 | tf_op jit(solution)/shard_map/all_to_all | solution.py:47
  114.6 1.2 shard_map.183
  115.9 4.4 %collective-permute-start.6 = (bf16[4,272,256]{2,1,0:T(8,128)(2,1)S(1)}, bf16[4,272,256]{2,1,0:T(8,128)(2,1)S(1)}, u32[]{:S(2)}, u32[]{:S(2)}) collective-permute-start(bf16[4,272,256]{2,1,0:T(8,128)(2,1)S(1)} %get-tuple-element.52), channel_id=1, source_target_pairs={{0,64},{64,0},{1,65},{65,1},{2,66},{66,2},{3,67},{67,3},{4,68},{68... | collective-permute-start | bytes 1671176 | tf_op jit(solution)/shard_map/ppermute | solution.py:480
  120.3 2.3 %shard_map.186 = (bf16[16,128,128]{2,1,0:T(8,128)(2,1)}, bf16[16,128,128]{2,1,0:T(8,128)(2,1)S(1)}, bf16[16,128,128]{2,1,0:T(8,128)(2,1)S(1)}, bf16[16,128,128]{2,1,0:T(8,128)(2,1)S(1)}) custom-call(bf16[4,272,512]{2,1,0:T(8,128)(2,1)S(1)} %all_to_all.37.acts, bf16[1024,512]{1,0:T(8,128)(2,1)S(1)} %get-tuple-element.53.feats, ...), custom_call_target="tpu_custom_call" | custom-call | flops 1073741824 | bytes 5308416 | tf_op jit(solution)/shard_map/pallas_call | solution.py:74
  122.6 6.0 %collective-permute-start.7 = (bf16[16,128,128]{2,1,0:T(8,128)(2,1)}, bf16[16,128,128]{2,1,0:T(8,128)(2,1)}, u32[]{:S(2)}, u32[]{:S(2)}) collective-permute-start(bf16[16,128,128]{2,1,0:T(8,128)(2,1)} %get-tuple-element.55), channel_id=1, source_target_pairs={{0,396},{64,192},{128,0},{192,320},{256,128},{320,448},{384,256},{... | collective-permute-start | bytes 1572872 | tf_op jit(solution)/shard_map/ppermute | solution.py:66
  128.7 0.0 collective-permute-done.6.theirs
  128.7 0.9 shard_map.184
  129.6 3.5 %all-to-all-start.3 = ((bf16[4,272,256]{2,1,0:T(8,128)(2,1)}), bf16[4,272,256]{2,1,0:T(8,128)(2,1)S(1)}, u32[]{:S(2)}, u32[]{:S(2)}) async-start(bf16[4,272,256]{2,1,0:T(8,128)(2,1)} %shard_map.184), calls=%async_computation.3 | async-start | bytes 1114112 | tf_op jit(solution)/shard_map/all_to_all | solution.py:51
  133.1 1.9 %collective-permute-start.11 = (bf16[16,128,128]{2,1,0:T(8,128)(2,1)S(1)}, bf16[16,128,128]{2,1,0:T(8,128)(2,1)S(1)}, u32[]{:S(2)}, u32[]{:S(2)}) collective-permute-start(bf16[16,128,128]{2,1,0:T(8,128)(2,1)S(1)} %get-tuple-element.66), channel_id=1, source_target_pairs={{0,128},{64,460},{128,256},{192,64},{256,384},{320,192},{384,4},{4... | collective-permute-start | bytes 1572872 | tf_op jit(solution)/shard_map/ppermute | solution.py:66
  135.0 5.1 %all-to-all-done.3.pieces = bf16[4,272,256]{2,1,0:T(8,128)(2,1)S(1)} async-done(((bf16[4,272,256]{2,1,0:T(8,128)(2,1)}), bf16[4,272,256]{2,1,0:T(8,128)(2,1)S(1)}, u32[]{:S(2)}, u32[]{:S(2)}) %all-to-all-start.3) | async-done | bytes 557088 | tf_op jit(solution)/shard_map/all_to_all | solution.py:51
  140.2 0.7 shard_map.185
  140.9 0.0 copy-start.7
  140.9 0.0 copy-start.9
  141.0 0.0 copy-start.10
  141.0 0.0 copy-start.11
  141.0 0.0 copy-start.8
  141.0 0.0 collective-permute-done.7
  141.0 6.5 %all-to-all-start.4 = ((bf16[4,80,256]{2,1,0:T(8,128)(2,1)}), bf16[4,80,256]{2,1,0:T(8,128)(2,1)S(1)}, u32[]{:S(2)}, u32[]{:S(2)}) async-start(bf16[4,80,256]{2,1,0:T(8,128)(2,1)} %shard_map.185), calls=%async_computation.4 | async-start | bytes 327680 | tf_op jit(solution)/shard_map/all_to_all | solution.py:51
  147.5 1.2 add_convert_fusion
  148.7 4.8 %collective-permute-start.10 = (bf16[16,128,128]{2,1,0:T(8,128)(2,1)S(1)}, bf16[16,128,128]{2,1,0:T(8,128)(2,1)S(1)}, u32[]{:S(2)}, u32[]{:S(2)}) collective-permute-start(bf16[16,128,128]{2,1,0:T(8,128)(2,1)S(1)} %add_convert_fusion), channel_id=1, source_target_pairs={{0,396},{64,192},{128,0},{192,320},{256,128},{320,448},{384,256},{... | collective-permute-start | bytes 1572872 | tf_op jit(solution)/shard_map/ppermute | solution.py:66
  153.5 6.5 %all-to-all-done.4.refs_4_ = bf16[4,80,256]{2,1,0:T(8,128)(2,1)S(1)} async-done(((bf16[4,80,256]{2,1,0:T(8,128)(2,1)}), bf16[4,80,256]{2,1,0:T(8,128)(2,1)S(1)}, u32[]{:S(2)}, u32[]{:S(2)}) %all-to-all-start.4) | async-done | bytes 163872 | tf_op jit(solution)/shard_map/all_to_all | solution.py:51
  160.0 0.0 copy-done.1
  160.1 0.0 copy-done.3
  160.1 0.0 copy-done.5
  160.1 0.0 copy-done.6
  160.1 0.0 copy-done.7
  160.1 0.0 copy-done.9
  160.1 2.7 %shard_map.187 = (bf16[64,256]{1,0:T(8,128)(2,1)}, bf16[64,256]{1,0:T(8,128)(2,1)}, bf16[128,256]{1,0:T(8,128)(2,1)S(1)}, bf16[128,256]{1,0:T(8,128)(2,1)S(1)}, f32[128,256]{1,0:T(8,128)S(1)}, /*index=5*/f32[8,64]{1,0:T(8,128)}) custom-call(bf16[64,256]{1,0:T(8,128)(2,1)S(1)} %bitcast.23, f32[1,64]{1,0:T(1,128)S(1)} %bitcast.29, s32[64]{0:T(128)S(1)} %copy-done.10, ...), custom_call_target="tpu_custom_call" | custom-call | flops 125829120 | bytes 791040 | tf_op jit(solution)/shard_map/pallas_call | solution.py:74
  162.8 1.9 %collective-permute-start.8 = (bf16[128,256]{1,0:T(8,128)(2,1)S(1)}, bf16[128,256]{1,0:T(8,128)(2,1)S(1)}, u32[]{:S(2)}, u32[]{:S(2)}) collective-permute-start(bf16[128,256]{1,0:T(8,128)(2,1)S(1)} %get-tuple-element.61), channel_id=1, source_target_pairs={{0,64},{64,0},{1,65},{65,1},{2,66},{66,2},{3,67},{67,3},{4,68},{68... | collective-permute-start | bytes 196616 | tf_op jit(solution)/shard_map/ppermute | solution.py:534
  164.7 7.5 %collective-permute-start.9 = (bf16[128,256]{1,0:T(8,128)(2,1)S(1)}, bf16[128,256]{1,0:T(8,128)(2,1)S(1)}, u32[]{:S(2)}, u32[]{:S(2)}) collective-permute-start(bf16[128,256]{1,0:T(8,128)(2,1)S(1)} %get-tuple-element.62), channel_id=1, source_target_pairs={{64,128},{192,256},{320,384},{128,64},{256,192},{384,320},{65,129}... | collective-permute-start | bytes 196616 | tf_op jit(solution)/shard_map/ppermute | solution.py:535
  172.3 0.0 collective-permute-done.11.refs_1_
  172.3 0.0 collective-permute-done.10.refs_0_
  172.3 4.8 %all-to-all-start.5 = ((f32[8,1,64]{2,1,0:T(1,128)}), f32[8,1,64]{2,1,0:T(1,128)S(1)}, u32[]{:S(2)}, u32[]{:S(2)}) async-start(f32[8,1,64]{2,1,0:T(1,128)} %bitcast.16), calls=%async_computation.5 | async-start | bytes 8192 | tf_op jit(solution)/shard_map/all_to_all | solution.py:51
  177.1 0.9 shard_map.189
  178.0 3.8 %all-to-all-done.5 = f32[8,1,64]{2,1,0:T(1,128)S(1)} async-done(((f32[8,1,64]{2,1,0:T(1,128)}), f32[8,1,64]{2,1,0:T(1,128)S(1)}, u32[]{:S(2)}, u32[]{:S(2)}) %all-to-all-start.5) | async-done | bytes 2080 | tf_op jit(solution)/shard_map/all_to_all | solution.py:51
  181.9 0.0 collective-permute-done.8.inside
  181.9 0.0 collective-permute-done.9.outside
  181.9 0.6 shard_map.188
  (15 shorter events, 0.1 us)
Async XLA Ops:
  2.7 50.5 %collective-permute-start.3 = (bf16[16,128,128]{2,1,0:T(8,128)(2,1)}, bf16[16,128,128]{2,1,0:T(8,128)(2,1)S(1)}, u32[]{:S(2)}, u32[]{:S(2)}) collective-permute-start(bf16[16,128,128]{2,1,0:T(8,128)(2,1)} %get-tuple-element.44.refs_2_), channel_id=1, source_target_pairs={{128,0},{460,64},{256,128},{64,192},{384,256},{192,320},{4,384},{3... | collective-permute-start | bytes 1572872 | tf_op jit(solution)/shard_map/ppermute | solution.py:66
  7.1 46.1 %collective-permute-start.2 = (bf16[16,128,128]{2,1,0:T(8,128)(2,1)}, bf16[16,128,128]{2,1,0:T(8,128)(2,1)S(1)}, u32[]{:S(2)}, u32[]{:S(2)}) collective-permute-start(bf16[16,128,128]{2,1,0:T(8,128)(2,1)} %get-tuple-element.44.refs_2_), channel_id=1, source_target_pairs={{396,0},{192,64},{0,128},{320,192},{128,256},{448,320},{256,384},{... | collective-permute-start | bytes 1572872 | tf_op jit(solution)/shard_map/ppermute | solution.py:66
  16.6 7.4 %collective-permute-start.1 = (bf16[128,256]{1,0:T(8,128)(2,1)}, bf16[128,256]{1,0:T(8,128)(2,1)S(1)}, u32[]{:S(2)}, u32[]{:S(2)}) collective-permute-start(bf16[128,256]{1,0:T(8,128)(2,1)} %get-tuple-element.42.refs_7_.refs_9_), channel_id=1, source_target_pairs={{64,128},{192,256},{320,384},{128,64},{256,192},{384,320},{65,129}... | collective-permute-start | bytes 196616 | tf_op jit(solution)/shard_map/ppermute | solution.py:422
  18.5 5.5 %collective-permute-start = (bf16[128,256]{1,0:T(8,128)(2,1)}, bf16[128,256]{1,0:T(8,128)(2,1)S(1)}, u32[]{:S(2)}, u32[]{:S(2)}) collective-permute-start(bf16[128,256]{1,0:T(8,128)(2,1)} %get-tuple-element.42.refs_7_.refs_9_), channel_id=1, source_target_pairs={{0,64},{64,0},{1,65},{65,1},{2,66},{66,2},{3,67},{67,3},{4,68},{68... | collective-permute-start | bytes 196616 | tf_op jit(solution)/shard_map/ppermute | solution.py:421
  24.0 0.6 copy-start.2
  24.0 0.7 copy-start.4
  54.3 22.0 %copy-start = (bf16[16,128,128]{2,1,0:T(8,128)(2,1)S(1)}, bf16[16,128,128]{2,1,0:T(8,128)(2,1)}, u32[]{:S(2)}) copy-start(bf16[16,128,128]{2,1,0:T(8,128)(2,1)} %get-tuple-element.44.refs_2_) | copy-start | bytes 1572868
  54.3 17.3 %all-to-all-start = ((bf16[4,4,144,256]{3,2,1,0:T(8,128)(2,1)}), bf16[4,4,144,256]{3,2,1,0:T(8,128)(2,1)S(1)}, u32[]{:S(2)}, u32[]{:S(2)}) async-start(bf16[4,4,144,256]{3,2,1,0:T(8,128)(2,1)} %broadcast_in_dim.7), calls=%async_computation | async-start | bytes 2359296 | tf_op jit(solution)/shard_map/all_to_all | solution.py:47
  58.5 9.9 %collective-permute-start.4 = (bf16[16,128,128]{2,1,0:T(8,128)(2,1)S(1)}, bf16[16,128,128]{2,1,0:T(8,128)(2,1)S(1)}, u32[]{:S(2)}, u32[]{:S(2)}) collective-permute-start(bf16[16,128,128]{2,1,0:T(8,128)(2,1)S(1)} %collective-permute-done.2.refs_1_), channel_id=1, source_target_pairs={{396,0},{192,64},{0,128},{320,192},{128,256},{448,320},{256,384},{... | collective-permute-start | bytes 1572872 | tf_op jit(solution)/shard_map/ppermute | solution.py:66
  71.6 4.7 %collective-permute-start.5 = (bf16[4,4,144,256]{3,2,1,0:T(8,128)(2,1)S(1)}, bf16[4,4,144,256]{3,2,1,0:T(8,128)(2,1)S(1)}, u32[]{:S(2)}, u32[]{:S(2)}) collective-permute-start(bf16[4,4,144,256]{3,2,1,0:T(8,128)(2,1)S(1)} %all-to-all-done.refs_4_), channel_id=1, source_target_pairs={{0,64},{64,0},{1,65},{65,1},{2,66},{66,2},{3,67},{67,3},{4,68},{68... | collective-permute-start | bytes 3538952 | tf_op jit(solution)/shard_map/ppermute | solution.py:448
  115.9 12.8 %collective-permute-start.6 = (bf16[4,272,256]{2,1,0:T(8,128)(2,1)S(1)}, bf16[4,272,256]{2,1,0:T(8,128)(2,1)S(1)}, u32[]{:S(2)}, u32[]{:S(2)}) collective-permute-start(bf16[4,272,256]{2,1,0:T(8,128)(2,1)S(1)} %get-tuple-element.52), channel_id=1, source_target_pairs={{0,64},{64,0},{1,65},{65,1},{2,66},{66,2},{3,67},{67,3},{4,68},{68... | collective-permute-start | bytes 1671176 | tf_op jit(solution)/shard_map/ppermute | solution.py:480
  122.6 18.4 %collective-permute-start.7 = (bf16[16,128,128]{2,1,0:T(8,128)(2,1)}, bf16[16,128,128]{2,1,0:T(8,128)(2,1)}, u32[]{:S(2)}, u32[]{:S(2)}) collective-permute-start(bf16[16,128,128]{2,1,0:T(8,128)(2,1)} %get-tuple-element.55), channel_id=1, source_target_pairs={{0,396},{64,192},{128,0},{192,320},{256,128},{320,448},{384,256},{... | collective-permute-start | bytes 1572872 | tf_op jit(solution)/shard_map/ppermute | solution.py:66
  129.6 10.6 %all-to-all-start.3 = ((bf16[4,272,256]{2,1,0:T(8,128)(2,1)}), bf16[4,272,256]{2,1,0:T(8,128)(2,1)S(1)}, u32[]{:S(2)}, u32[]{:S(2)}) async-start(bf16[4,272,256]{2,1,0:T(8,128)(2,1)} %shard_map.184), calls=%async_computation.3 | async-start | bytes 1114112 | tf_op jit(solution)/shard_map/all_to_all | solution.py:51
  133.1 39.2 %collective-permute-start.11 = (bf16[16,128,128]{2,1,0:T(8,128)(2,1)S(1)}, bf16[16,128,128]{2,1,0:T(8,128)(2,1)S(1)}, u32[]{:S(2)}, u32[]{:S(2)}) collective-permute-start(bf16[16,128,128]{2,1,0:T(8,128)(2,1)S(1)} %get-tuple-element.66), channel_id=1, source_target_pairs={{0,128},{64,460},{128,256},{192,64},{256,384},{320,192},{384,4},{4... | collective-permute-start | bytes 1572872 | tf_op jit(solution)/shard_map/ppermute | solution.py:66
  140.9 19.1 %copy-start.1 = (bf16[128,256]{1,0:T(8,128)(2,1)S(1)}, bf16[128,256]{1,0:T(8,128)(2,1)}, u32[]{:S(2)}) copy-start(bf16[128,256]{1,0:T(8,128)(2,1)} %get-tuple-element.42.refs_7_.refs_9_) | copy-start | bytes 196612
  140.9 19.1 %copy-start.3 = (bf16[128,256]{1,0:T(8,128)(2,1)S(1)}, bf16[128,256]{1,0:T(8,128)(2,1)}, u32[]{:S(2)}) copy-start(bf16[128,256]{1,0:T(8,128)(2,1)} %copy-done.2) | copy-start | bytes 196612
  140.9 19.1 %copy-start.5 = (bf16[128,256]{1,0:T(8,128)(2,1)S(1)}, bf16[128,256]{1,0:T(8,128)(2,1)}, u32[]{:S(2)}) copy-start(bf16[128,256]{1,0:T(8,128)(2,1)} %copy-done.4) | copy-start | bytes 196612
  140.9 19.1 %copy-start.6 = (bf16[256,64]{0,1:T(8,128)(2,1)S(1)}, bf16[256,64]{0,1:T(8,128)(2,1)}, u32[]{:S(2)}) copy-start(bf16[256,64]{0,1:T(8,128)(2,1)} %param.25) | copy-start | bytes 98308
  140.9 19.1 %copy-start.7 = (bf16[256,64]{0,1:T(8,128)(2,1)S(1)}, bf16[256,64]{0,1:T(8,128)(2,1)}, u32[]{:S(2)}) copy-start(bf16[256,64]{0,1:T(8,128)(2,1)} %param.14) | copy-start | bytes 98308
  140.9 19.1 %copy-start.9 = (f32[64]{0:T(128)S(1)}, f32[64]{0:T(128)}, u32[]{:S(2)}) copy-start(f32[64]{0:T(128)} %param.18) | copy-start | bytes 772
  141.0 19.1 %copy-start.10 = (s32[64]{0:T(128)S(1)}, s32[64]{0:T(128)}, u32[]{:S(2)}) copy-start(s32[64]{0:T(128)} %refs_2_.1) | copy-start | bytes 772
  141.0 19.1 %copy-start.11 = (bf16[64,256]{1,0:T(8,128)(2,1)S(1)}, bf16[64,256]{1,0:T(8,128)(2,1)}, u32[]{:S(2)}) copy-start(bf16[64,256]{1,0:T(8,128)(2,1)} %get-tuple-element.57.refs_5_) | copy-start | bytes 98308
  141.0 36.1 %copy-start.8 = (f32[16,128]{1,0:T(8,128)S(1)}, f32[16,128]{1,0:T(8,128)}, u32[]{:S(2)}) copy-start(f32[16,128]{1,0:T(8,128)} %get-tuple-element.74.refs_3_) | copy-start | bytes 24580
  141.0 19.0 %all-to-all-start.4 = ((bf16[4,80,256]{2,1,0:T(8,128)(2,1)}), bf16[4,80,256]{2,1,0:T(8,128)(2,1)S(1)}, u32[]{:S(2)}, u32[]{:S(2)}) async-start(bf16[4,80,256]{2,1,0:T(8,128)(2,1)} %shard_map.185), calls=%async_computation.4 | async-start | bytes 327680 | tf_op jit(solution)/shard_map/all_to_all | solution.py:51
  148.7 23.6 %collective-permute-start.10 = (bf16[16,128,128]{2,1,0:T(8,128)(2,1)S(1)}, bf16[16,128,128]{2,1,0:T(8,128)(2,1)S(1)}, u32[]{:S(2)}, u32[]{:S(2)}) collective-permute-start(bf16[16,128,128]{2,1,0:T(8,128)(2,1)S(1)} %add_convert_fusion), channel_id=1, source_target_pairs={{0,396},{64,192},{128,0},{192,320},{256,128},{320,448},{384,256},{... | collective-permute-start | bytes 1572872 | tf_op jit(solution)/shard_map/ppermute | solution.py:66
  162.8 19.1 %collective-permute-start.8 = (bf16[128,256]{1,0:T(8,128)(2,1)S(1)}, bf16[128,256]{1,0:T(8,128)(2,1)S(1)}, u32[]{:S(2)}, u32[]{:S(2)}) collective-permute-start(bf16[128,256]{1,0:T(8,128)(2,1)S(1)} %get-tuple-element.61), channel_id=1, source_target_pairs={{0,64},{64,0},{1,65},{65,1},{2,66},{66,2},{3,67},{67,3},{4,68},{68... | collective-permute-start | bytes 196616 | tf_op jit(solution)/shard_map/ppermute | solution.py:534
  164.7 17.2 %collective-permute-start.9 = (bf16[128,256]{1,0:T(8,128)(2,1)S(1)}, bf16[128,256]{1,0:T(8,128)(2,1)S(1)}, u32[]{:S(2)}, u32[]{:S(2)}) collective-permute-start(bf16[128,256]{1,0:T(8,128)(2,1)S(1)} %get-tuple-element.62), channel_id=1, source_target_pairs={{64,128},{192,256},{320,384},{128,64},{256,192},{384,320},{65,129}... | collective-permute-start | bytes 196616 | tf_op jit(solution)/shard_map/ppermute | solution.py:535
  172.3 9.6 %all-to-all-start.5 = ((f32[8,1,64]{2,1,0:T(1,128)}), f32[8,1,64]{2,1,0:T(1,128)S(1)}, u32[]{:S(2)}, u32[]{:S(2)}) async-start(f32[8,1,64]{2,1,0:T(1,128)} %bitcast.16), calls=%async_computation.5 | async-start | bytes 8192 | tf_op jit(solution)/shard_map/all_to_all | solution.py:51

commit v4 on v3

--- a/solution.py
+++ b/solution.py
@@ -78,7 +78,7 @@
         + [smem if a.ndim == 1 else vmem for a in operands[loads:]],
         out_specs=[vmem] * len(out_shapes),
         scratch_shapes=list(scratch) + ([pltpu.SemaphoreType.DMA((loads,))] if loads else []),
-        compiler_params=pltpu.CompilerParams(vmem_limit_bytes=(60 if loads else 40) * 1024 * 1024),
+        compiler_params=pltpu.CompilerParams(vmem_limit_bytes=(60 if loads else 24) * 1024 * 1024),
         cost_estimate=pl.CostEstimate(flops=flops, bytes_accessed=moved, transcendentals=0),
     )(*operands)
 
@@ -249,11 +249,13 @@
 
 
 def norm_grad_body(head, n_zh, n_x, slots, acts, *refs):
-    weights, (own, send) = refs[:slots], refs[slots:]
+    weights, out = refs[:slots], refs[slots]
     units = weights[0].shape[2]
     blocks = weights[0].shape[0] // 2
     tok = acts.shape[2] // 2
     per_block = BLK // head
+    own = lax.axis_index("core") * n_x
+    other = (1 - lax.axis_index("core")) * n_x
     for b in range(blocks):
         total = jnp.zeros((BLK, 2 * tok), F32)
         for w in range(slots):
@@ -262,12 +264,12 @@
         for k in range(per_block):
             zh, x = divmod(b * per_block + k, n_x)
             rows = slice(zh * head, (zh + 1) * head)
-            own[x, rows, :] = total[k * head : (k + 1) * head, :tok]
-            send[x, rows, :] = total[k * head : (k + 1) * head, tok:]
+            out[own + x, rows, :] = total[k * head : (k + 1) * head, :tok]
+            out[other + x, rows, :] = total[k * head : (k + 1) * head, tok:]
     inner = sum(read_tail(acts[w, 2 * units :, :]) for w in range(slots))
     for x in range(n_x):
-        write_tail(own, (x,), n_zh * head, inner[:, :tok])
-        write_tail(send, (x,), n_zh * head, inner[:, tok:])
+        write_tail(out, (own + x,), n_zh * head, inner[:, :tok])
+        write_tail(out, (other + x,), n_zh * head, inner[:, tok:])
 
 
 def weight_grad_body(slots, acts, feats, cots, *homes):
@@ -282,13 +284,6 @@
             homes[w][blocks + b] = block.astype(BF)
 
 
-def core_sum_body(rows, own, theirs, out):
-    for x in range(own.shape[0]):
-        total = own[x, :rows, :].astype(F32) + theirs[x, :rows, :].astype(F32)
-        out[x, :rows, :] = total.astype(BF)
-        write_tail(out, (x,), rows, read_tail(own[x, rows:, :]) + read_tail(theirs[x, rows:, :]))
-
-
 def x_sum_body(head, pieces, out):
     n_zh = out.shape[0]
     rows = n_zh * head
@@ -300,8 +295,15 @@
         write_tail(out, (zh,), head, inner)
 
 
-def attend_grad_body(width_total, seq_devs, *refs):
-    cot, gain_row, reaches, query, pieces, hidden, inv_rms, inside, outside, own = refs[:10]
+def probs_body(seq_devs, reaches, query, inside, outside, own, probs_ref, halo):
+    sort_halo(inside, outside, halo)
+    probs = head_probs((halo.at[0], own, halo.at[1]), query, own_reach(reaches), seq_devs)
+    for p in range(3):
+        probs_ref[p] = probs[p]
+
+
+def attend_grad_body(width_total, *refs):
+    cot, gain_row, probs, query, pieces, hidden, inv_rms, inside, outside, own = refs[:10]
     stream_out, query_out, inside_out, outside_out, own_out, gain_out, halo = refs[10:]
     head, tok = query.shape
     scale = float(head) ** (-0.5)
@@ -322,7 +324,6 @@
     stream_out[...] = grad_stream
     sort_halo(inside, outside, halo)
     parts = (halo.at[0], own, halo.at[1])
-    probs = head_probs(parts, query, own_reach(reaches), seq_devs)
     grad_probs = [dot_first(parts[p][head:, :], grad_stream) for p in range(3)]
     center = sum(jnp.sum(probs[p] * grad_probs[p], axis=0, keepdims=True) for p in range(3))
     grad_query = jnp.zeros((head, tok), F32)
@@ -438,13 +439,13 @@
         loads=5,
         scratch=[held(query_t), held(stream_t), held(gain), reaches, halo],
     )
+    far = window_send(both, 0, n_zh, n_zl, n_core, False)
+
+    panel = lax.all_gather(send, "zh", axis=0, tiled=False)
+    panel, far, both = lax.optimization_barrier((panel, far, both))
     near = [window_send(both, w, n_zh, n_zl, n_core, False) for w in (1, 3)]
-
-    panel = lax.all_gather(send, "zh", axis=0, tiled=False)
+    panel = spread(panel, "x")
     panel, near = lax.optimization_barrier((panel, near))
-    far = window_send(near[0], 1, n_zh, n_zl, n_core, False)
-    panel = spread(panel, "x")
-    panel, far = lax.optimization_barrier((panel, far))
     other = lax.ppermute(panel, "core", swap)
     slots = [far, near[0], both, near[1]]
 
@@ -470,14 +471,13 @@
     inner_part = jnp.sum(grad_act.astype(F32) * pre_act, axis=0)
     acts = spread(jnp.concatenate([activation, grad_act, tail_rows(inner_part)], axis=0), "row")
 
-    mine, theirs = call_kernel(
+    pieces = call_kernel(
         functools.partial(norm_grad_body, head, n_zh, n_x, n_zl),
-        [shaped((n_x, n_zh * head + TAIL, tok), BF)] * 2,
+        [shaped((n_core * n_x, n_zh * head + TAIL, tok), BF)],
         2 * n_zl * depth * units * both_toks,
         acts,
         *slots,
-    )
-    theirs = lax.ppermute(theirs, "core", swap)
+    )[0]
     homes = call_kernel(
         functools.partial(weight_grad_body, n_zl),
         [shaped((2 * blocks, BLK, units), BF)] * n_zl,
@@ -486,28 +486,32 @@
         feats,
         cots,
     )
-    pieces = call_kernel(
-        functools.partial(core_sum_body, n_zh * head),
-        [shaped((n_x, n_zh * head + TAIL, tok), BF)],
-        0,
-        mine,
-        theirs,
-    )[0]
-    pieces = exchange(pieces, "x")
+    pieces = exchange(pieces, ("core", "x"))
     pieces = call_kernel(
         functools.partial(x_sum_body, head),
         [shaped((n_zh, head + TAIL, tok), BF)],
         0,
         pieces,
     )[0]
-    far = window_send(homes[0], 1, n_zh, n_zl, n_core, True)
-    near = window_send(homes[3], 3, n_zh, n_zl, n_core, True)
-    pieces, far = lax.optimization_barrier((pieces, far))
-    far = (homes[1].astype(F32) + far.astype(F32)).astype(BF)
-    far = window_send(far, 1, n_zh, n_zl, n_core, True)
+    early = [window_send(homes[w], w, n_zh, n_zl, n_core, True) for w in (0, 1)]
+    late = window_send(homes[3], 3, n_zh, n_zl, n_core, True)
+    query_t, feats = lax.optimization_barrier((query_t, feats))
+    probs = call_kernel(
+        functools.partial(probs_body, seq_devs),
+        [shaped((3, tok, tok), F32)],
+        4 * 10**9,
+        windows,
+        query_t,
+        inside,
+        outside,
+        paired,
+        scratch=[halo],
+    )[0]
     pieces = exchange(pieces, "zh")
+    pieces, early = lax.optimization_barrier((pieces, early))
+
     grad_stream, grad_query, inside_grad, outside_grad, own, gain_parts = call_kernel(
-        functools.partial(attend_grad_body, width_total, seq_devs),
+        functools.partial(attend_grad_body, width_total),
         [
             shaped((head, tok), BF),
             shaped((head, tok), BF),
@@ -519,7 +523,7 @@
         30 * tok * tok * head,
         cot_t,
         gain,
-        windows,
+        probs,
         query_t,
         pieces,
         hidden,
@@ -529,16 +533,16 @@
         paired,
         scratch=[halo],
     )
-    gain_parts, far, near = lax.optimization_barrier((gain_parts, far, near))
+    own, late = lax.optimization_barrier((own, late))
     gain_parts = exchange(gain_parts, ("zl", "core"))
     inside_grad = lax.ppermute(inside_grad, "core", swap)
     outside_grad = lax.ppermute(outside_grad, ("zl", "core"), cross)
     grad_up, grad_down = call_kernel(
-        functools.partial(home_sum_body, 3),
+        functools.partial(home_sum_body, n_zl),
         [shaped((depth, units), BF), shaped((units, depth), BF)],
         0,
-        far,
-        near,
+        *early,
+        late,
         homes[2],
         flags,
     )

time: 184 us -> 181 us (0.984)
  blocking collectives: 61.2 us -> 54.6 us
  local copies, waits for them, and re-layouts: 1.9 us -> 4.35 us
    all_gather x1, blocking collectives: 25.3 us -> 18.6 us  [on_device(): panel = lax.all_gather(send, 'zh', axis=0, tiled=False)]
    ppermute x1 -> x0, starting transfers between devices: 4.39 us -> none  [on_device(): theirs = lax.ppermute(theirs, 'core', swap)]
    ppermute x6, waiting for transfers between devices: 8.01 us -> 11.5 us  [window_send(): return lax.ppermute(array, ('zl', 'core', 'zh'), pairs)]
    all_to_all x1, waiting for transfers between devices: 3.22 us -> 0.01 us  [spread(): return lax.all_to_all(copies, axis, 0, 0, tiled=True)]
    ppermute x1, starting transfers between devices: 7.54 us -> 5.04 us  [on_device(): outside_grad = lax.ppermute(outside_grad, ('zl', 'core'), cross)]
    unnamed x24 -> x42, local copies, waits for them, and re-layouts: 0.71 us -> 3.17 us
    all_to_all x3, starting transfers between devices: 14.8 us -> 17.2 us  [exchange(): return lax.all_to_all(pieces, axis, 0, 0, tiled=True)]
    ppermute x1, starting transfers between devices: 1.91 us -> 4.3 us  [on_device(): other = lax.ppermute(panel, 'core', swap)]
  transfers between devices with their start and end apart: 16 -> 15, of which waited for: 7 -> 7; matrix products, arithmetic and copies ran while one was open for 1% -> 0% of each run, Pallas kernels for 6% -> 6%
where the time goes in v4:
time: 181 us; the launch traced here: 180 us
  starting transfers between devices  67.6 us (37%)
  blocking collectives  54.6 us (30%)
  waiting for transfers between devices  34.5 us (19%)
  Pallas kernels  17 us (9%)
  local copies, waits for them, and re-layouts  4.35 us (2%)
    ppermute x6, starting transfers between devices, window_send(): return lax.ppermute(array, ('zl', 'core', 'zh'), pairs)  29 us
    all_to_all x1, blocking collectives, exchange(): return lax.all_to_all(pieces, axis, 0, 0, tiled=True)  19.2 us
    all_gather x1, blocking collectives, on_device(): panel = lax.all_gather(send, 'zh', axis=0, tiled=False)  18.6 us
    all_to_all x3, starting transfers between devices, exchange(): return lax.all_to_all(pieces, axis, 0, 0, tiled=True)  17.2 us
    pallas_call x10, Pallas kernels, call_kernel(): pl.pallas_call(body, out_shape=out_shapes, in_specs=[pl.BlockSpec(memory_...  17 us
    all_to_all x3, waiting for transfers between devices, exchange(): return lax.all_to_all(pieces, axis, 0, 0, tiled=True)  16.9 us
    all_to_all x1, blocking collectives, spread(): return lax.all_to_all(copies, axis, 0, 0, tiled=True)  16.8 us
    ppermute x6, waiting for transfers between devices, window_send(): return lax.ppermute(array, ('zl', 'core', 'zh'), pairs)  11.5 us
  transfers between devices with their start and end apart: 15, of which 7 were waited for; matrix products, arithmetic and copies ran while one was open for 0% of the time, Pallas kernels for 6%

profile of v4, /device:TPU:1, one launch (start us, length us, event | category | flops | bytes accessed | tf_op | source)
XLA Modules:
  0.0 179.6 jit_solution(11052212236759173096)
XLA Ops:
  0.6 2.1 %shard_map.180 = (bf16[16,128,128]{2,1,0:T(8,128)(2,1)}, f32[16,128]{1,0:T(8,128)}, bf16[128,256]{1,0:T(8,128)(2,1)}) custom-call(bf16[1024,128]{1,0:T(8,128)(2,1)} %refs_0_.1, bf16[128,1024]{1,0:T(8,128)(2,1)} %refs_1_.1, s32[16,128]{1,0:T(8,128)} %bitcast.35, s32[16,128]{1,0:T(8,128)} %bitcast.36, s32[16,128]{1,0:T(8,128)} %bitcast.37, ...), custom_call_target="tpu_custom_call" | custom-call | bytes 1220608 | tf_op jit(solution)/shard_map/pallas_call | solution.py:74
  2.7 12.4 %collective-permute-start.2 = (bf16[16,128,128]{2,1,0:T(8,128)(2,1)}, bf16[16,128,128]{2,1,0:T(8,128)(2,1)S(1)}, u32[]{:S(2)}, u32[]{:S(2)}) collective-permute-start(bf16[16,128,128]{2,1,0:T(8,128)(2,1)} %get-tuple-element.47.refs_2_), channel_id=1, source_target_pairs={{268,0},{320,64},{396,128},{448,192},{0,256},{68,320},{128,384},{1... | collective-permute-start | bytes 1572872 | tf_op jit(solution)/shard_map/ppermute | solution.py:66
  15.1 1.9 %collective-permute-start.1 = (bf16[128,256]{1,0:T(8,128)(2,1)}, bf16[128,256]{1,0:T(8,128)(2,1)S(1)}, u32[]{:S(2)}, u32[]{:S(2)}) collective-permute-start(bf16[128,256]{1,0:T(8,128)(2,1)} %get-tuple-element.42.refs_7_.own.refs_9_), channel_id=1, source_target_pairs={{64,128},{192,256},{320,384},{128,64},{256,192},{384,320},{65,129}... | collective-permute-start | bytes 196616 | tf_op jit(solution)/shard_map/ppermute | solution.py:423
  17.0 1.9 %collective-permute-start = (bf16[128,256]{1,0:T(8,128)(2,1)}, bf16[128,256]{1,0:T(8,128)(2,1)S(1)}, u32[]{:S(2)}, u32[]{:S(2)}) collective-permute-start(bf16[128,256]{1,0:T(8,128)(2,1)} %get-tuple-element.42.refs_7_.own.refs_9_), channel_id=1, source_target_pairs={{0,64},{64,0},{1,65},{65,1},{2,66},{66,2},{3,67},{67,3},{4,68},{68... | collective-permute-start | bytes 196616 | tf_op jit(solution)/shard_map/ppermute | solution.py:422
  19.0 3.6 %collective-permute-done.1.refs_6_.outside.refs_8_ = bf16[128,256]{1,0:T(8,128)(2,1)S(1)} collective-permute-done((bf16[128,256]{1,0:T(8,128)(2,1)}, bf16[128,256]{1,0:T(8,128)(2,1)S(1)}, u32[]{:S(2)}, u32[]{:S(2)}) %collective-permute-start.1) | collective-permute-done | bytes 65568 | tf_op jit(solution)/shard_map/ppermute | solution.py:423
  22.5 0.0 collective-permute-done.refs_5_.inside.refs_7_
  22.5 0.6 copy-done.6
  23.2 0.0 copy-done.8
  23.2 3.2 %shard_map.181 = (bf16[144,256]{1,0:T(8,128)(2,1)}, bf16[64,256]{1,0:T(8,128)(2,1)}) custom-call(bf16[64,256]{1,0:T(8,128)(2,1)} %bitcast.24, bf16[64,256]{1,0:T(8,128)(2,1)} %bitcast.34, f32[1,64]{1,0:T(1,128)} %bitcast.29, s32[64]{0:T(128)} %reaches.1, bf16[64,256]{1,0:T(8,128)(2,1)} %bitcast.22, bf16[128,256]{1,0:T(8,128)(2,1)} %copy-done.8, ...), custom_call_target="tpu_custom_call" | custom-call | flops 50331648 | bytes 401920 | tf_op jit(solution)/shard_map/pallas_call | solution.py:74
  26.4 18.6 %all-gather = bf16[576,256]{1,0:T(8,128)(2,1)S(1)} all-gather(bf16[144,256]{1,0:T(8,128)(2,1)} %get-tuple-element.43), channel_id=2, replica_groups=mesh['zl'=4,'core'=2,'row'=4,'zh'=4,'x'=4] {'zh'}, dimensions={0}, use_global_device_ids=true | all-gather | bytes 368640 | tf_op jit(solution)/shard_map/all_gather | solution.py:444
  45.0 0.0 collective-permute-done.2.refs_0_
  45.0 1.1 broadcast_in_dim.7
  46.1 5.1 %all-to-all-start = ((bf16[4,4,144,256]{3,2,1,0:T(8,128)(2,1)}), bf16[4,4,144,256]{3,2,1,0:T(8,128)(2,1)S(1)}, u32[]{:S(2)}, u32[]{:S(2)}) async-start(bf16[4,4,144,256]{3,2,1,0:T(8,128)(2,1)} %broadcast_in_dim.7), calls=%async_computation | async-start | bytes 2359296 | tf_op jit(solution)/shard_map/all_to_all | solution.py:47
  51.2 0.0 copy-done
  51.2 3.3 %collective-permute-start.4 = (bf16[16,128,128]{2,1,0:T(8,128)(2,1)S(1)}, bf16[16,128,128]{2,1,0:T(8,128)(2,1)S(1)}, u32[]{:S(2)}, u32[]{:S(2)}) collective-permute-start(bf16[16,128,128]{2,1,0:T(8,128)(2,1)S(1)} %copy-done), channel_id=1, source_target_pairs={{128,0},{460,64},{256,128},{64,192},{384,256},{192,320},{4,384},{3... | collective-permute-start | bytes 1572872 | tf_op jit(solution)/shard_map/ppermute | solution.py:66
  54.5 3.2 %collective-permute-start.3 = (bf16[16,128,128]{2,1,0:T(8,128)(2,1)S(1)}, bf16[16,128,128]{2,1,0:T(8,128)(2,1)S(1)}, u32[]{:S(2)}, u32[]{:S(2)}) collective-permute-start(bf16[16,128,128]{2,1,0:T(8,128)(2,1)S(1)} %copy-done), channel_id=1, source_target_pairs={{396,0},{192,64},{0,128},{320,192},{128,256},{448,320},{256,384},{... | collective-permute-start | bytes 1572872 | tf_op jit(solution)/shard_map/ppermute | solution.py:66
  57.7 4.9 %collective-permute-done.4.refs_3_ = bf16[16,128,128]{2,1,0:T(8,128)(2,1)S(1)} collective-permute-done((bf16[16,128,128]{2,1,0:T(8,128)(2,1)S(1)}, bf16[16,128,128]{2,1,0:T(8,128)(2,1)S(1)}, u32[]{:S(2)}, u32[]{:S(2)}) %collective-permute-start.4) | collective-permute-done | bytes 524320 | tf_op jit(solution)/shard_map/ppermute | solution.py:66
  62.6 6.6 %collective-permute-done.3.refs_1_ = bf16[16,128,128]{2,1,0:T(8,128)(2,1)S(1)} collective-permute-done((bf16[16,128,128]{2,1,0:T(8,128)(2,1)S(1)}, bf16[16,128,128]{2,1,0:T(8,128)(2,1)S(1)}, u32[]{:S(2)}, u32[]{:S(2)}) %collective-permute-start.3) | collective-permute-done | bytes 524320 | tf_op jit(solution)/shard_map/ppermute | solution.py:66
  69.2 0.0 all-to-all-done.refs_4_
  69.2 4.3 %collective-permute-start.5 = (bf16[4,4,144,256]{3,2,1,0:T(8,128)(2,1)S(1)}, bf16[4,4,144,256]{3,2,1,0:T(8,128)(2,1)S(1)}, u32[]{:S(2)}, u32[]{:S(2)}) collective-permute-start(bf16[4,4,144,256]{3,2,1,0:T(8,128)(2,1)S(1)} %all-to-all-done.refs_4_), channel_id=1, source_target_pairs={{0,64},{64,0},{1,65},{65,1},{2,66},{66,2},{3,67},{67,3},{4,68},{68... | collective-permute-start | bytes 3538952 | tf_op jit(solution)/shard_map/ppermute | solution.py:449
  73.5 2.5 %collective-permute-done.5.refs_5_ = bf16[4,4,144,256]{3,2,1,0:T(8,128)(2,1)S(1)} collective-permute-done((bf16[4,4,144,256]{3,2,1,0:T(8,128)(2,1)S(1)}, bf16[4,4,144,256]{3,2,1,0:T(8,128)(2,1)S(1)}, u32[]{:S(2)}, u32[]{:S(2)}) %collective-permute-start.5) | collective-permute-done | bytes 1179680 | tf_op jit(solution)/shard_map/ppermute | solution.py:449
  76.0 1.9 %shard_map.182 = (bf16[4,272,512]{2,1,0:T(8,128)(2,1)S(1)}, bf16[1024,512]{1,0:T(8,128)(2,1)S(1)}, bf16[1024,512]{1,0:T(8,128)(2,1)S(1)}) custom-call(bf16[16,128,128]{2,1,0:T(8,128)(2,1)S(1)} %collective-permute-done.2.refs_0_, bf16[16,128,128]{2,1,0:T(8,128)(2,1)S(1)} %collective-permute-done.3.refs_1_, bf16[16,128,128]{2,1,0:T(8,128)(2,1)S(1)} %copy-done, ...), custom_call_target="tpu_custom_call" | custom-call | flops 1073741824 | bytes 7667712 | tf_op jit(solution)/shard_map/pallas_call | solution.py:74
  77.8 0.0 copy-done.1
  77.9 0.0 copy-done.3
  77.9 0.0 copy-start.16
  77.9 19.2 %all_to_all.36 = bf16[4,272,512]{2,1,0:T(8,128)(2,1)S(1)} all-to-all(bf16[4,272,512]{2,1,0:T(8,128)(2,1)S(1)} %get-tuple-element.53), channel_id=1, replica_groups=mesh['zl'=4,'core'=2,'row'=4,'zh'=4,'x'=4] {'row'}, dimensions={0} | all-to-all | bytes 2228224 | tf_op jit(solution)/shard_map/all_to_all | solution.py:51
  97.1 0.0 copy-done.16
  97.1 0.1 convert_reduce_fusion
  97.3 0.2 multiply_reduce_fusion
  97.6 0.1 broadcast_in_dim.8
  97.7 16.8 %all_to_all.37.acts = bf16[4,272,512]{2,1,0:T(8,128)(2,1)S(1)} all-to-all(bf16[4,272,512]{2,1,0:T(8,128)(2,1)S(1)} %broadcast_in_dim.8), channel_id=1, replica_groups=mesh['zl'=4,'core'=2,'row'=4,'zh'=4,'x'=4] {'row'}, dimensions={0} | all-to-all | bytes 2228224 | tf_op jit(solution)/shard_map/all_to_all | solution.py:47
  114.5 0.0 copy-done.2
  114.5 2.3 %shard_map.184 = bf16[8,272,256]{2,1,0:T(8,128)(2,1)} custom-call(bf16[4,272,512]{2,1,0:T(8,128)(2,1)S(1)} %all_to_all.37.acts, bf16[16,128,128]{2,1,0:T(8,128)(2,1)S(1)} %collective-permute-done.2.refs_0_, bf16[16,128,128]{2,1,0:T(8,128)(2,1)S(1)} %copy-done.4, bf16[16,128,128]{2,1,0:T(8,128)(2,1)S(1)} %copy-done, bf16[16,128,128]{2,1,0:T(8,128)(2,1)S(1)} %copy-done.2), custom_call_target="tpu_custom_call" | custom-call | flops 536870912 | bytes 4325376 | tf_op jit(solution)/shard_map/pallas_call | solution.py:74
  116.8 7.2 %all-to-all-start.3 = ((bf16[8,272,256]{2,1,0:T(8,128)(2,1)}), bf16[8,272,256]{2,1,0:T(8,128)(2,1)S(1)}, u32[]{:S(2)}, u32[]{:S(2)}) async-start(bf16[8,272,256]{2,1,0:T(8,128)(2,1)} %shard_map.184), calls=%async_computation.3 | async-start | bytes 2228224 | tf_op jit(solution)/shard_map/all_to_all | solution.py:51
  124.0 1.2 copy-done.17
  125.3 1.2 copy-done.19
  126.5 2.3 %shard_map.186 = (bf16[16,128,128]{2,1,0:T(8,128)(2,1)}, bf16[16,128,128]{2,1,0:T(8,128)(2,1)}, bf16[16,128,128]{2,1,0:T(8,128)(2,1)S(1)}, bf16[16,128,128]{2,1,0:T(8,128)(2,1)S(1)}) custom-call(bf16[4,272,512]{2,1,0:T(8,128)(2,1)S(1)} %all_to_all.37.acts, bf16[1024,512]{1,0:T(8,128)(2,1)S(1)} %copy-done.17, bf16[1024,512]{1,0:T(8,128)(2,1)S(1)} %copy-done.19), custom_call_target="tpu_custom_call" | custom-call | flops 1073741824 | bytes 5308416 | tf_op jit(solution)/shard_map/pallas_call | solution.py:74
  128.9 0.0 copy-start.5
  128.9 0.0 copy-start.11
  128.9 0.0 copy-start.15
  128.9 2.1 %collective-permute-start.6 = (bf16[16,128,128]{2,1,0:T(8,128)(2,1)}, bf16[16,128,128]{2,1,0:T(8,128)(2,1)S(1)}, u32[]{:S(2)}, u32[]{:S(2)}) collective-permute-start(bf16[16,128,128]{2,1,0:T(8,128)(2,1)} %get-tuple-element.55), channel_id=1, source_target_pairs={{0,268},{64,320},{128,396},{192,448},{256,0},{320,68},{384,128},{4... | collective-permute-start | bytes 1572872 | tf_op jit(solution)/shard_map/ppermute | solution.py:66
  131.0 2.8 %collective-permute-start.7 = (bf16[16,128,128]{2,1,0:T(8,128)(2,1)}, bf16[16,128,128]{2,1,0:T(8,128)(2,1)S(1)}, u32[]{:S(2)}, u32[]{:S(2)}) collective-permute-start(bf16[16,128,128]{2,1,0:T(8,128)(2,1)} %get-tuple-element.56), channel_id=1, source_target_pairs={{0,396},{64,192},{128,0},{192,320},{256,128},{320,448},{384,256},{... | collective-permute-start | bytes 1572872 | tf_op jit(solution)/shard_map/ppermute | solution.py:66
  133.8 6.0 %all-to-all-done.3.pieces = bf16[8,272,256]{2,1,0:T(8,128)(2,1)S(1)} async-done(((bf16[8,272,256]{2,1,0:T(8,128)(2,1)}), bf16[8,272,256]{2,1,0:T(8,128)(2,1)S(1)}, u32[]{:S(2)}, u32[]{:S(2)}) %all-to-all-start.3) | async-done | bytes 1114144 | tf_op jit(solution)/shard_map/all_to_all | solution.py:51
  139.9 0.8 shard_map.185
  140.7 6.3 %all-to-all-start.4 = ((bf16[4,80,256]{2,1,0:T(8,128)(2,1)}), bf16[4,80,256]{2,1,0:T(8,128)(2,1)S(1)}, u32[]{:S(2)}, u32[]{:S(2)}) async-start(bf16[4,80,256]{2,1,0:T(8,128)(2,1)} %shard_map.185), calls=%async_computation.4 | async-start | bytes 327680 | tf_op jit(solution)/shard_map/all_to_all | solution.py:51
  147.0 0.0 copy-done.20
  147.0 0.0 copy-start.14
  147.0 5.2 %collective-permute-start.8 = (bf16[16,128,128]{2,1,0:T(8,128)(2,1)}, bf16[16,128,128]{2,1,0:T(8,128)(2,1)S(1)}, u32[]{:S(2)}, u32[]{:S(2)}) collective-permute-start(bf16[16,128,128]{2,1,0:T(8,128)(2,1)} %copy-done.20), channel_id=1, source_target_pairs={{0,128},{64,460},{128,256},{192,64},{256,384},{320,192},{384,4},{4... | collective-permute-start | bytes 1572872 | tf_op jit(solution)/shard_map/ppermute | solution.py:66
  152.3 1.1 shard_map.183.refs_2_
  153.4 0.0 copy-start.13
  153.4 0.0 collective-permute-done.6.refs_0_
  153.4 0.0 collective-permute-done.7.refs_1_
  153.4 7.1 %all-to-all-done.4.refs_4_ = bf16[4,80,256]{2,1,0:T(8,128)(2,1)S(1)} async-done(((bf16[4,80,256]{2,1,0:T(8,128)(2,1)}), bf16[4,80,256]{2,1,0:T(8,128)(2,1)S(1)}, u32[]{:S(2)}, u32[]{:S(2)}) %all-to-all-start.4) | async-done | bytes 163872 | tf_op jit(solution)/shard_map/all_to_all | solution.py:51
  160.6 0.0 copy-done.12
  160.6 1.7 shard_map.187
  162.3 3.2 %collective-permute-start.9 = (bf16[128,256]{1,0:T(8,128)(2,1)}, bf16[128,256]{1,0:T(8,128)(2,1)S(1)}, u32[]{:S(2)}, u32[]{:S(2)}) collective-permute-start(bf16[128,256]{1,0:T(8,128)(2,1)} %get-tuple-element.64), channel_id=1, source_target_pairs={{0,64},{64,0},{1,65},{65,1},{2,66},{66,2},{3,67},{67,3},{4,68},{68... | collective-permute-start | bytes 196616 | tf_op jit(solution)/shard_map/ppermute | solution.py:538
  165.4 5.0 %collective-permute-start.10 = (bf16[128,256]{1,0:T(8,128)(2,1)S(1)}, bf16[128,256]{1,0:T(8,128)(2,1)S(1)}, u32[]{:S(2)}, u32[]{:S(2)}) collective-permute-start(bf16[128,256]{1,0:T(8,128)(2,1)S(1)} %get-tuple-element.65), channel_id=1, source_target_pairs={{64,128},{192,256},{320,384},{128,64},{256,192},{384,320},{65,129}... | collective-permute-start | bytes 196616 | tf_op jit(solution)/shard_map/ppermute | solution.py:539
  170.5 3.6 %all-to-all-start.5 = ((f32[8,1,64]{2,1,0:T(1,128)}), f32[8,1,64]{2,1,0:T(1,128)S(1)}, u32[]{:S(2)}, u32[]{:S(2)}) async-start(f32[8,1,64]{2,1,0:T(1,128)} %bitcast.16), calls=%async_computation.5 | async-start | bytes 8192 | tf_op jit(solution)/shard_map/all_to_all | solution.py:51
  174.1 0.0 collective-permute-done.8.refs_2_
  174.1 1.0 shard_map.189
  175.1 3.8 %all-to-all-done.5 = f32[8,1,64]{2,1,0:T(1,128)S(1)} async-done(((f32[8,1,64]{2,1,0:T(1,128)}), f32[8,1,64]{2,1,0:T(1,128)S(1)}, u32[]{:S(2)}, u32[]{:S(2)}) %all-to-all-start.5) | async-done | bytes 2080 | tf_op jit(solution)/shard_map/all_to_all | solution.py:51
  178.9 0.0 collective-permute-done.9.inside
  178.9 0.0 collective-permute-done.10.outside
  178.9 0.6 shard_map.188
  (30 shorter events, 0.1 us)
Async XLA Ops:
  2.7 42.3 %collective-permute-start.2 = (bf16[16,128,128]{2,1,0:T(8,128)(2,1)}, bf16[16,128,128]{2,1,0:T(8,128)(2,1)S(1)}, u32[]{:S(2)}, u32[]{:S(2)}) collective-permute-start(bf16[16,128,128]{2,1,0:T(8,128)(2,1)} %get-tuple-element.47.refs_2_), channel_id=1, source_target_pairs={{268,0},{320,64},{396,128},{448,192},{0,256},{68,320},{128,384},{1... | collective-permute-start | bytes 1572872 | tf_op jit(solution)/shard_map/ppermute | solution.py:66
  15.1 7.4 %collective-permute-start.1 = (bf16[128,256]{1,0:T(8,128)(2,1)}, bf16[128,256]{1,0:T(8,128)(2,1)S(1)}, u32[]{:S(2)}, u32[]{:S(2)}) collective-permute-start(bf16[128,256]{1,0:T(8,128)(2,1)} %get-tuple-element.42.refs_7_.own.refs_9_), channel_id=1, source_target_pairs={{64,128},{192,256},{320,384},{128,64},{256,192},{384,320},{65,129}... | collective-permute-start | bytes 196616 | tf_op jit(solution)/shard_map/ppermute | solution.py:423
  17.0 5.5 %collective-permute-start = (bf16[128,256]{1,0:T(8,128)(2,1)}, bf16[128,256]{1,0:T(8,128)(2,1)S(1)}, u32[]{:S(2)}, u32[]{:S(2)}) collective-permute-start(bf16[128,256]{1,0:T(8,128)(2,1)} %get-tuple-element.42.refs_7_.own.refs_9_), channel_id=1, source_target_pairs={{0,64},{64,0},{1,65},{65,1},{2,66},{66,2},{3,67},{67,3},{4,68},{68... | collective-permute-start | bytes 196616 | tf_op jit(solution)/shard_map/ppermute | solution.py:422
  22.5 0.6 copy-start.6
  22.5 0.6 copy-start.8
  46.1 5.1 %copy-start = (bf16[16,128,128]{2,1,0:T(8,128)(2,1)S(1)}, bf16[16,128,128]{2,1,0:T(8,128)(2,1)}, u32[]{:S(2)}) copy-start(bf16[16,128,128]{2,1,0:T(8,128)(2,1)} %get-tuple-element.47.refs_2_) | copy-start | bytes 1572868
  46.1 23.2 %all-to-all-start = ((bf16[4,4,144,256]{3,2,1,0:T(8,128)(2,1)}), bf16[4,4,144,256]{3,2,1,0:T(8,128)(2,1)S(1)}, u32[]{:S(2)}, u32[]{:S(2)}) async-start(bf16[4,4,144,256]{3,2,1,0:T(8,128)(2,1)} %broadcast_in_dim.7), calls=%async_computation | async-start | bytes 2359296 | tf_op jit(solution)/shard_map/all_to_all | solution.py:47
  51.2 11.4 %collective-permute-start.4 = (bf16[16,128,128]{2,1,0:T(8,128)(2,1)S(1)}, bf16[16,128,128]{2,1,0:T(8,128)(2,1)S(1)}, u32[]{:S(2)}, u32[]{:S(2)}) collective-permute-start(bf16[16,128,128]{2,1,0:T(8,128)(2,1)S(1)} %copy-done), channel_id=1, source_target_pairs={{128,0},{460,64},{256,128},{64,192},{384,256},{192,320},{4,384},{3... | collective-permute-start | bytes 1572872 | tf_op jit(solution)/shard_map/ppermute | solution.py:66
  54.5 14.7 %collective-permute-start.3 = (bf16[16,128,128]{2,1,0:T(8,128)(2,1)S(1)}, bf16[16,128,128]{2,1,0:T(8,128)(2,1)S(1)}, u32[]{:S(2)}, u32[]{:S(2)}) collective-permute-start(bf16[16,128,128]{2,1,0:T(8,128)(2,1)S(1)} %copy-done), channel_id=1, source_target_pairs={{396,0},{192,64},{0,128},{320,192},{128,256},{448,320},{256,384},{... | collective-permute-start | bytes 1572872 | tf_op jit(solution)/shard_map/ppermute | solution.py:66
  62.6 15.2 %copy-start.1 = (bf16[16,128,128]{2,1,0:T(8,128)(2,1)}, bf16[16,128,128]{2,1,0:T(8,128)(2,1)S(1)}, u32[]{:S(2)}) copy-start(bf16[16,128,128]{2,1,0:T(8,128)(2,1)S(1)} %collective-permute-done.4.refs_3_) | copy-start | bytes 1572868
  69.2 8.6 %copy-start.3 = (bf16[16,128,128]{2,1,0:T(8,128)(2,1)}, bf16[16,128,128]{2,1,0:T(8,128)(2,1)S(1)}, u32[]{:S(2)}) copy-start(bf16[16,128,128]{2,1,0:T(8,128)(2,1)S(1)} %collective-permute-done.3.refs_1_) | copy-start | bytes 1572868
  69.2 6.8 %collective-permute-start.5 = (bf16[4,4,144,256]{3,2,1,0:T(8,128)(2,1)S(1)}, bf16[4,4,144,256]{3,2,1,0:T(8,128)(2,1)S(1)}, u32[]{:S(2)}, u32[]{:S(2)}) collective-permute-start(bf16[4,4,144,256]{3,2,1,0:T(8,128)(2,1)S(1)} %all-to-all-done.refs_4_), channel_id=1, source_target_pairs={{0,64},{64,0},{1,65},{65,1},{2,66},{66,2},{3,67},{67,3},{4,68},{68... | collective-permute-start | bytes 3538952 | tf_op jit(solution)/shard_map/ppermute | solution.py:449
  77.9 19.2 %copy-start.16 = (bf16[1024,512]{1,0:T(8,128)(2,1)}, bf16[1024,512]{1,0:T(8,128)(2,1)S(1)}, u32[]{:S(2)}) copy-start(bf16[1024,512]{1,0:T(8,128)(2,1)S(1)} %get-tuple-element.51.feats) | copy-start | bytes 3145732
  77.9 19.2 %copy-start.18 = (bf16[1024,512]{1,0:T(8,128)(2,1)}, bf16[1024,512]{1,0:T(8,128)(2,1)S(1)}, u32[]{:S(2)}) copy-start(bf16[1024,512]{1,0:T(8,128)(2,1)S(1)} %get-tuple-element.54.cots) | copy-start | bytes 3145732
  97.7 16.9 %copy-start.2 = (bf16[16,128,128]{2,1,0:T(8,128)(2,1)S(1)}, bf16[16,128,128]{2,1,0:T(8,128)(2,1)}, u32[]{:S(2)}) copy-start(bf16[16,128,128]{2,1,0:T(8,128)(2,1)} %copy-done.1) | copy-start | bytes 1572868
  97.7 16.9 %copy-start.4 = (bf16[16,128,128]{2,1,0:T(8,128)(2,1)S(1)}, bf16[16,128,128]{2,1,0:T(8,128)(2,1)}, u32[]{:S(2)}) copy-start(bf16[16,128,128]{2,1,0:T(8,128)(2,1)} %copy-done.3) | copy-start | bytes 1572868
  116.8 23.1 %all-to-all-start.3 = ((bf16[8,272,256]{2,1,0:T(8,128)(2,1)}), bf16[8,272,256]{2,1,0:T(8,128)(2,1)S(1)}, u32[]{:S(2)}, u32[]{:S(2)}) async-start(bf16[8,272,256]{2,1,0:T(8,128)(2,1)} %shard_map.184), calls=%async_computation.3 | async-start | bytes 2228224 | tf_op jit(solution)/shard_map/all_to_all | solution.py:51
  124.0 1.2 copy-start.17
  125.3 1.2 copy-start.19
  128.8 18.2 %copy-start.20 = (bf16[16,128,128]{2,1,0:T(8,128)(2,1)}, bf16[16,128,128]{2,1,0:T(8,128)(2,1)S(1)}, u32[]{:S(2)}) copy-start(bf16[16,128,128]{2,1,0:T(8,128)(2,1)S(1)} %get-tuple-element.62) | copy-start | bytes 1572868
  128.9 23.4 %copy-start.5 = (bf16[128,256]{1,0:T(8,128)(2,1)S(1)}, bf16[128,256]{1,0:T(8,128)(2,1)}, u32[]{:S(2)}) copy-start(bf16[128,256]{1,0:T(8,128)(2,1)} %get-tuple-element.42.refs_7_.own.refs_9_) | copy-start | bytes 196612
  128.9 23.4 %copy-start.7 = (bf16[128,256]{1,0:T(8,128)(2,1)S(1)}, bf16[128,256]{1,0:T(8,128)(2,1)}, u32[]{:S(2)}) copy-start(bf16[128,256]{1,0:T(8,128)(2,1)} %copy-done.6) | copy-start | bytes 196612
  128.9 23.4 %copy-start.9 = (bf16[128,256]{1,0:T(8,128)(2,1)S(1)}, bf16[128,256]{1,0:T(8,128)(2,1)}, u32[]{:S(2)}) copy-start(bf16[128,256]{1,0:T(8,128)(2,1)} %copy-done.8) | copy-start | bytes 196612
  128.9 23.4 %copy-start.11 = (bf16[256,64]{0,1:T(8,128)(2,1)S(1)}, bf16[256,64]{0,1:T(8,128)(2,1)}, u32[]{:S(2)}) copy-start(bf16[256,64]{0,1:T(8,128)(2,1)} %param.14) | copy-start | bytes 98308
  128.9 23.4 %copy-start.15 = (s32[64]{0:T(128)S(1)}, s32[64]{0:T(128)}, u32[]{:S(2)}) copy-start(s32[64]{0:T(128)} %reaches.1) | copy-start | bytes 772
  128.9 24.5 %collective-permute-start.6 = (bf16[16,128,128]{2,1,0:T(8,128)(2,1)}, bf16[16,128,128]{2,1,0:T(8,128)(2,1)S(1)}, u32[]{:S(2)}, u32[]{:S(2)}) collective-permute-start(bf16[16,128,128]{2,1,0:T(8,128)(2,1)} %get-tuple-element.55), channel_id=1, source_target_pairs={{0,268},{64,320},{128,396},{192,448},{256,0},{320,68},{384,128},{4... | collective-permute-start | bytes 1572872 | tf_op jit(solution)/shard_map/ppermute | solution.py:66
  131.0 22.4 %collective-permute-start.7 = (bf16[16,128,128]{2,1,0:T(8,128)(2,1)}, bf16[16,128,128]{2,1,0:T(8,128)(2,1)S(1)}, u32[]{:S(2)}, u32[]{:S(2)}) collective-permute-start(bf16[16,128,128]{2,1,0:T(8,128)(2,1)} %get-tuple-element.56), channel_id=1, source_target_pairs={{0,396},{64,192},{128,0},{192,320},{256,128},{320,448},{384,256},{... | collective-permute-start | bytes 1572872 | tf_op jit(solution)/shard_map/ppermute | solution.py:66
  140.7 19.9 %all-to-all-start.4 = ((bf16[4,80,256]{2,1,0:T(8,128)(2,1)}), bf16[4,80,256]{2,1,0:T(8,128)(2,1)S(1)}, u32[]{:S(2)}, u32[]{:S(2)}) async-start(bf16[4,80,256]{2,1,0:T(8,128)(2,1)} %shard_map.185), calls=%async_computation.4 | async-start | bytes 327680 | tf_op jit(solution)/shard_map/all_to_all | solution.py:51
  147.0 13.5 %copy-start.10 = (bf16[256,64]{0,1:T(8,128)(2,1)S(1)}, bf16[256,64]{0,1:T(8,128)(2,1)}, u32[]{:S(2)}) copy-start(bf16[256,64]{0,1:T(8,128)(2,1)} %param.25) | copy-start | bytes 98308
  147.0 13.5 %copy-start.12 = (bf16[64,256]{1,0:T(8,128)(2,1)S(1)}, bf16[64,256]{1,0:T(8,128)(2,1)}, u32[]{:S(2)}) copy-start(bf16[64,256]{1,0:T(8,128)(2,1)} %get-tuple-element.58.refs_5_) | copy-start | bytes 98308
  147.0 13.5 %copy-start.14 = (f32[64]{0:T(128)S(1)}, f32[64]{0:T(128)}, u32[]{:S(2)}) copy-start(f32[64]{0:T(128)} %param.18) | copy-start | bytes 772
  147.0 27.1 %collective-permute-start.8 = (bf16[16,128,128]{2,1,0:T(8,128)(2,1)}, bf16[16,128,128]{2,1,0:T(8,128)(2,1)S(1)}, u32[]{:S(2)}, u32[]{:S(2)}) collective-permute-start(bf16[16,128,128]{2,1,0:T(8,128)(2,1)} %copy-done.20), channel_id=1, source_target_pairs={{0,128},{64,460},{128,256},{192,64},{256,384},{320,192},{384,4},{4... | collective-permute-start | bytes 1572872 | tf_op jit(solution)/shard_map/ppermute | solution.py:66
  153.4 20.7 %copy-start.13 = (f32[16,128]{1,0:T(8,128)S(1)}, f32[16,128]{1,0:T(8,128)}, u32[]{:S(2)}) copy-start(f32[16,128]{1,0:T(8,128)} %get-tuple-element.74.refs_4_) | copy-start | bytes 24580
  162.3 16.7 %collective-permute-start.9 = (bf16[128,256]{1,0:T(8,128)(2,1)}, bf16[128,256]{1,0:T(8,128)(2,1)S(1)}, u32[]{:S(2)}, u32[]{:S(2)}) collective-permute-start(bf16[128,256]{1,0:T(8,128)(2,1)} %get-tuple-element.64), channel_id=1, source_target_pairs={{0,64},{64,0},{1,65},{65,1},{2,66},{66,2},{3,67},{67,3},{4,68},{68... | collective-permute-start | bytes 196616 | tf_op jit(solution)/shard_map/ppermute | solution.py:538
  165.4 13.5 %collective-permute-start.10 = (bf16[128,256]{1,0:T(8,128)(2,1)S(1)}, bf16[128,256]{1,0:T(8,128)(2,1)S(1)}, u32[]{:S(2)}, u32[]{:S(2)}) collective-permute-start(bf16[128,256]{1,0:T(8,128)(2,1)S(1)} %get-tuple-element.65), channel_id=1, source_target_pairs={{64,128},{192,256},{320,384},{128,64},{256,192},{384,320},{65,129}... | collective-permute-start | bytes 196616 | tf_op jit(solution)/shard_map/ppermute | solution.py:539
  170.5 8.4 %all-to-all-start.5 = ((f32[8,1,64]{2,1,0:T(1,128)}), f32[8,1,64]{2,1,0:T(1,128)S(1)}, u32[]{:S(2)}, u32[]{:S(2)}) async-start(f32[8,1,64]{2,1,0:T(1,128)} %bitcast.16), calls=%async_computation.5 | async-start | bytes 8192 | tf_op jit(solution)/shard_map/all_to_all | solution.py:51

commit v5 on v4

--- a/solution.py
+++ b/solution.py
@@ -226,18 +226,36 @@
     units = weights[0].shape[2]
     blocks = weights[0].shape[0] // 2
     depth = n_x * n_zh * head
-    squares = []
-    for side, panel in enumerate((mine, theirs)):
+    core = lax.axis_index("core")
+
+    def place(side, panel):
         lanes = slice(side * tok, (side + 1) * tok)
-        square = jnp.zeros((1, tok), F32)
         for zh in range(n_zh):
             for x in range(n_x):
                 rows = slice((zh * n_x + x) * head, (zh * n_x + x + 1) * head)
                 feats[rows, lanes] = panel[x, zh, :head, :]
                 cots[rows, lanes] = panel[x, zh, head : 2 * head, :]
-                square += read_tail(panel[x, zh, 2 * head :, :])
-        squares.append(square)
-    square = jnp.concatenate(squares, axis=1)
+
+    @pl.when(core == 0)
+    def _():
+        place(0, mine)
+        place(1, theirs)
+
+    @pl.when(core != 0)
+    def _():
+        place(0, theirs)
+        place(1, mine)
+
+    squares = [jnp.zeros((1, tok), F32), jnp.zeros((1, tok), F32)]
+    for zh in range(n_zh):
+        for x in range(n_x):
+            for side, panel in enumerate((mine, theirs)):
+                squares[side] += read_tail(panel[x, zh, 2 * head :, :])
+    square = jnp.where(
+        core == 0,
+        jnp.concatenate(squares, axis=1),
+        jnp.concatenate(squares[::-1], axis=1),
+    )
     for w in range(slots):
         up = weights[w][:blocks].reshape(depth, units)
         parts[w, :units, :] = dot_first(up, feats[...]).astype(BF)
@@ -254,8 +272,7 @@
     blocks = weights[0].shape[0] // 2
     tok = acts.shape[2] // 2
     per_block = BLK // head
-    own = lax.axis_index("core") * n_x
-    other = (1 - lax.axis_index("core")) * n_x
+    n_core = out.shape[0] // n_x
     for b in range(blocks):
         total = jnp.zeros((BLK, 2 * tok), F32)
         for w in range(slots):
@@ -264,12 +281,14 @@
         for k in range(per_block):
             zh, x = divmod(b * per_block + k, n_x)
             rows = slice(zh * head, (zh + 1) * head)
-            out[own + x, rows, :] = total[k * head : (k + 1) * head, :tok]
-            out[other + x, rows, :] = total[k * head : (k + 1) * head, tok:]
+            for c in range(n_core):
+                out[c * n_x + x, rows, :] = total[
+                    k * head : (k + 1) * head, c * tok : (c + 1) * tok
+                ]
     inner = sum(read_tail(acts[w, 2 * units :, :]) for w in range(slots))
     for x in range(n_x):
-        write_tail(out, (own + x,), n_zh * head, inner[:, :tok])
-        write_tail(out, (other + x,), n_zh * head, inner[:, tok:])
+        for c in range(n_core):
+            write_tail(out, (c * n_x + x,), n_zh * head, inner[:, c * tok : (c + 1) * tok])
 
 
 def weight_grad_body(slots, acts, feats, cots, *homes):
@@ -318,7 +337,8 @@
         precision=lax.Precision.HIGHEST,
         preferred_element_type=F32,
     )
-    shrink = inv_rms[:, :tok] * inner / width_total
+    own_inv = jnp.where(lax.axis_index("core") == 0, inv_rms[:, :tok], inv_rms[:, tok:])
+    shrink = own_inv * inner / width_total
     grad_hidden = column(gain_row[...]) * grad_norm - hidden_f * shrink + cot[...].astype(F32)
     grad_stream = grad_hidden.astype(BF)
     stream_out[...] = grad_stream
@@ -439,15 +459,18 @@
         loads=5,
         scratch=[held(query_t), held(stream_t), held(gain), reaches, halo],
     )
-    far = window_send(both, 0, n_zh, n_zl, n_core, False)
+    first = window_send(both, 1, n_zh, n_zl, n_core, False)
 
     panel = lax.all_gather(send, "zh", axis=0, tiled=False)
-    panel, far, both = lax.optimization_barrier((panel, far, both))
-    near = [window_send(both, w, n_zh, n_zl, n_core, False) for w in (1, 3)]
+    panel, first, both = lax.optimization_barrier((panel, first, both))
+    near = [
+        window_send(first, 1, n_zh, n_zl, n_core, False),
+        window_send(both, 3, n_zh, n_zl, n_core, False),
+    ]
     panel = spread(panel, "x")
     panel, near = lax.optimization_barrier((panel, near))
     other = lax.ppermute(panel, "core", swap)
-    slots = [far, near[0], both, near[1]]
+    slots = [near[0], first, both, near[1]]
 
     parts, feats, cots = call_kernel(
         functools.partial(project_body, head, n_zl),
@@ -493,8 +516,8 @@
         0,
         pieces,
     )[0]
-    early = [window_send(homes[w], w, n_zh, n_zl, n_core, True) for w in (0, 1)]
-    late = window_send(homes[3], 3, n_zh, n_zl, n_core, True)
+    joined = window_send(homes[0], 1, n_zh, n_zl, n_core, True)
+    early = window_send(homes[3], 3, n_zh, n_zl, n_core, True)
     query_t, feats = lax.optimization_barrier((query_t, feats))
     probs = call_kernel(
         functools.partial(probs_body, seq_devs),
@@ -508,6 +531,8 @@
         scratch=[halo],
     )[0]
     pieces = exchange(pieces, "zh")
+    joined = (homes[1].astype(F32) + joined.astype(F32)).astype(BF)
+    late = window_send(joined, 1, n_zh, n_zl, n_core, True)
     pieces, early = lax.optimization_barrier((pieces, early))
 
     grad_stream, grad_query, inside_grad, outside_grad, own, gain_parts = call_kernel(
@@ -538,10 +563,10 @@
     inside_grad = lax.ppermute(inside_grad, "core", swap)
     outside_grad = lax.ppermute(outside_grad, ("zl", "core"), cross)
     grad_up, grad_down = call_kernel(
-        functools.partial(home_sum_body, n_zl),
+        functools.partial(home_sum_body, 3),
         [shaped((depth, units), BF), shaped((units, depth), BF)],
         0,
-        *early,
+        early,
         late,
         homes[2],
         flags,

time: 181 us -> 176 us (0.972)
  starting transfers between devices: 67.6 us -> 62.5 us
    ppermute x6, starting transfers between devices: 29 us -> 25.7 us  [window_send(): return lax.ppermute(array, ('zl', 'core', 'zh'), pairs)]
    ppermute x1, starting transfers between devices: 5.04 us -> 3.15 us  [on_device(): outside_grad = lax.ppermute(outside_grad, ('zl', 'core'), cross)]
  transfers between devices with their start and end apart: 15 -> 15, of which waited for: 7 -> 7; matrix products, arithmetic and copies ran while one was open for 0% -> 1% of each run, Pallas kernels for 6% -> 6%
where the time goes in v5:
time: 176 us; the launch traced here: 175 us
  starting transfers between devices  62.5 us (36%)
  blocking collectives  53.8 us (31%)
  waiting for transfers between devices  33.9 us (19%)
  Pallas kernels  17.9 us (10%)
  local copies, waits for them, and re-layouts  4.32 us (2%)
    ppermute x6, starting transfers between devices, window_send(): return lax.ppermute(array, ('zl', 'core', 'zh'), pairs)  25.7 us
    all_to_all x1, blocking collectives, exchange(): return lax.all_to_all(pieces, axis, 0, 0, tiled=True)  19.2 us
    pallas_call x10, Pallas kernels, call_kernel(): pl.pallas_call(body, out_shape=out_shapes, in_specs=[pl.BlockSpec(memory_...  17.9 us
    all_to_all x3, starting transfers between devices, exchange(): return lax.all_to_all(pieces, axis, 0, 0, tiled=True)  17.8 us
    all_gather x1, blocking collectives, on_device(): panel = lax.all_gather(send, 'zh', axis=0, tiled=False)  17.7 us
    all_to_all x1, blocking collectives, spread(): return lax.all_to_all(copies, axis, 0, 0, tiled=True)  16.8 us
    all_to_all x3, waiting for transfers between devices, exchange(): return lax.all_to_all(pieces, axis, 0, 0, tiled=True)  16.3 us
    ppermute x6, waiting for transfers between devices, window_send(): return lax.ppermute(array, ('zl', 'core', 'zh'), pairs)  12.9 us
  transfers between devices with their start and end apart: 15, of which 7 were waited for; matrix products, arithmetic and copies ran while one was open for 1% of the time, Pallas kernels for 6%

profile of v5, /device:TPU:1, one launch (start us, length us, event | category | flops | bytes accessed | tf_op | source)
XLA Modules:
  0.0 174.7 jit_solution(2925747728203299359)
XLA Ops:
  0.6 2.1 %shard_map.180 = (bf16[16,128,128]{2,1,0:T(8,128)(2,1)}, f32[16,128]{1,0:T(8,128)}, bf16[128,256]{1,0:T(8,128)(2,1)}) custom-call(bf16[1024,128]{1,0:T(8,128)(2,1)} %refs_0_.1, bf16[128,1024]{1,0:T(8,128)(2,1)} %refs_1_.1, s32[16,128]{1,0:T(8,128)} %bitcast.35, s32[16,128]{1,0:T(8,128)} %bitcast.36, s32[16,128]{1,0:T(8,128)} %bitcast.37, ...), custom_call_target="tpu_custom_call" | custom-call | bytes 1220608 | tf_op jit(solution)/shard_map/pallas_call | solution.py:74
  2.7 12.0 %collective-permute-start.2 = (bf16[16,128,128]{2,1,0:T(8,128)(2,1)}, bf16[16,128,128]{2,1,0:T(8,128)(2,1)S(1)}, u32[]{:S(2)}, u32[]{:S(2)}) collective-permute-start(bf16[16,128,128]{2,1,0:T(8,128)(2,1)} %get-tuple-element.46.refs_2_), channel_id=1, source_target_pairs={{396,0},{192,64},{0,128},{320,192},{128,256},{448,320},{256,384},{... | collective-permute-start | bytes 1572872 | tf_op jit(solution)/shard_map/ppermute | solution.py:66
  14.7 1.9 %collective-permute-start.1 = (bf16[128,256]{1,0:T(8,128)(2,1)}, bf16[128,256]{1,0:T(8,128)(2,1)S(1)}, u32[]{:S(2)}, u32[]{:S(2)}) collective-permute-start(bf16[128,256]{1,0:T(8,128)(2,1)} %get-tuple-element.41.refs_7_.own.refs_9_), channel_id=1, source_target_pairs={{64,128},{192,256},{320,384},{128,64},{256,192},{384,320},{65,129}... | collective-permute-start | bytes 196616 | tf_op jit(solution)/shard_map/ppermute | solution.py:443
  16.6 1.9 %collective-permute-start = (bf16[128,256]{1,0:T(8,128)(2,1)}, bf16[128,256]{1,0:T(8,128)(2,1)S(1)}, u32[]{:S(2)}, u32[]{:S(2)}) collective-permute-start(bf16[128,256]{1,0:T(8,128)(2,1)} %get-tuple-element.41.refs_7_.own.refs_9_), channel_id=1, source_target_pairs={{0,64},{64,0},{1,65},{65,1},{2,66},{66,2},{3,67},{67,3},{4,68},{68... | collective-permute-start | bytes 196616 | tf_op jit(solution)/shard_map/ppermute | solution.py:442
  18.5 2.2 %collective-permute-done.1.refs_6_.outside.refs_8_ = bf16[128,256]{1,0:T(8,128)(2,1)S(1)} collective-permute-done((bf16[128,256]{1,0:T(8,128)(2,1)}, bf16[128,256]{1,0:T(8,128)(2,1)S(1)}, u32[]{:S(2)}, u32[]{:S(2)}) %collective-permute-start.1) | collective-permute-done | bytes 65568 | tf_op jit(solution)/shard_map/ppermute | solution.py:443
  20.8 0.0 collective-permute-done.refs_5_.inside.refs_7_
  20.8 0.6 copy-done.6
  21.4 0.0 copy-done.8
  21.4 3.2 %shard_map.181 = (bf16[144,256]{1,0:T(8,128)(2,1)}, bf16[64,256]{1,0:T(8,128)(2,1)}) custom-call(bf16[64,256]{1,0:T(8,128)(2,1)} %bitcast.24, bf16[64,256]{1,0:T(8,128)(2,1)} %bitcast.34, f32[1,64]{1,0:T(1,128)} %bitcast.29, s32[64]{0:T(128)} %reaches.1, bf16[64,256]{1,0:T(8,128)(2,1)} %bitcast.22, bf16[128,256]{1,0:T(8,128)(2,1)} %copy-done.8, ...), custom_call_target="tpu_custom_call" | custom-call | flops 50331648 | bytes 401920 | tf_op jit(solution)/shard_map/pallas_call | solution.py:74
  24.6 17.7 %all-gather = bf16[576,256]{1,0:T(8,128)(2,1)S(1)} all-gather(bf16[144,256]{1,0:T(8,128)(2,1)} %get-tuple-element.42), channel_id=2, replica_groups=mesh['zl'=4,'core'=2,'row'=4,'zh'=4,'x'=4] {'zh'}, dimensions={0}, use_global_device_ids=true | all-gather | bytes 368640 | tf_op jit(solution)/shard_map/all_gather | solution.py:464
  42.3 0.0 collective-permute-done.2.refs_1_
  42.4 1.1 broadcast_in_dim.7
  43.4 4.1 %all-to-all-start = ((bf16[4,4,144,256]{3,2,1,0:T(8,128)(2,1)}), bf16[4,4,144,256]{3,2,1,0:T(8,128)(2,1)S(1)}, u32[]{:S(2)}, u32[]{:S(2)}) async-start(bf16[4,4,144,256]{3,2,1,0:T(8,128)(2,1)} %broadcast_in_dim.7), calls=%async_computation | async-start | bytes 2359296 | tf_op jit(solution)/shard_map/all_to_all | solution.py:47
  47.6 2.9 %collective-permute-start.3 = (bf16[16,128,128]{2,1,0:T(8,128)(2,1)S(1)}, bf16[16,128,128]{2,1,0:T(8,128)(2,1)S(1)}, u32[]{:S(2)}, u32[]{:S(2)}) collective-permute-start(bf16[16,128,128]{2,1,0:T(8,128)(2,1)S(1)} %collective-permute-done.2.refs_1_), channel_id=1, source_target_pairs={{396,0},{192,64},{0,128},{320,192},{128,256},{448,320},{256,384},{... | collective-permute-start | bytes 1572872 | tf_op jit(solution)/shard_map/ppermute | solution.py:66
  50.5 0.0 copy-done
  50.5 2.4 %collective-permute-start.4 = (bf16[16,128,128]{2,1,0:T(8,128)(2,1)S(1)}, bf16[16,128,128]{2,1,0:T(8,128)(2,1)S(1)}, u32[]{:S(2)}, u32[]{:S(2)}) collective-permute-start(bf16[16,128,128]{2,1,0:T(8,128)(2,1)S(1)} %copy-done), channel_id=1, source_target_pairs={{128,0},{460,64},{256,128},{64,192},{384,256},{192,320},{4,384},{3... | collective-permute-start | bytes 1572872 | tf_op jit(solution)/shard_map/ppermute | solution.py:66
  52.9 4.9 %collective-permute-done.3.refs_0_ = bf16[16,128,128]{2,1,0:T(8,128)(2,1)S(1)} collective-permute-done((bf16[16,128,128]{2,1,0:T(8,128)(2,1)S(1)}, bf16[16,128,128]{2,1,0:T(8,128)(2,1)S(1)}, u32[]{:S(2)}, u32[]{:S(2)}) %collective-permute-start.3) | collective-permute-done | bytes 524320 | tf_op jit(solution)/shard_map/ppermute | solution.py:66
  57.8 8.0 %collective-permute-done.4.refs_3_ = bf16[16,128,128]{2,1,0:T(8,128)(2,1)S(1)} collective-permute-done((bf16[16,128,128]{2,1,0:T(8,128)(2,1)S(1)}, bf16[16,128,128]{2,1,0:T(8,128)(2,1)S(1)}, u32[]{:S(2)}, u32[]{:S(2)}) %collective-permute-start.4) | collective-permute-done | bytes 524320 | tf_op jit(solution)/shard_map/ppermute | solution.py:66
  65.8 0.0 all-to-all-done.refs_4_
  65.8 4.1 %collective-permute-start.5 = (bf16[4,4,144,256]{3,2,1,0:T(8,128)(2,1)S(1)}, bf16[4,4,144,256]{3,2,1,0:T(8,128)(2,1)S(1)}, u32[]{:S(2)}, u32[]{:S(2)}) collective-permute-start(bf16[4,4,144,256]{3,2,1,0:T(8,128)(2,1)S(1)} %all-to-all-done.refs_4_), channel_id=1, source_target_pairs={{0,64},{64,0},{1,65},{65,1},{2,66},{66,2},{3,67},{67,3},{4,68},{68... | collective-permute-start | bytes 3538952 | tf_op jit(solution)/shard_map/ppermute | solution.py:472
  69.9 2.5 %collective-permute-done.5.refs_5_ = bf16[4,4,144,256]{3,2,1,0:T(8,128)(2,1)S(1)} collective-permute-done((bf16[4,4,144,256]{3,2,1,0:T(8,128)(2,1)S(1)}, bf16[4,4,144,256]{3,2,1,0:T(8,128)(2,1)S(1)}, u32[]{:S(2)}, u32[]{:S(2)}) %collective-permute-start.5) | collective-permute-done | bytes 1179680 | tf_op jit(solution)/shard_map/ppermute | solution.py:472
  72.3 2.0 %shard_map.182 = (bf16[4,272,512]{2,1,0:T(8,128)(2,1)S(1)}, bf16[1024,512]{1,0:T(8,128)(2,1)S(1)}, bf16[1024,512]{1,0:T(8,128)(2,1)S(1)}) custom-call(bf16[16,128,128]{2,1,0:T(8,128)(2,1)S(1)} %collective-permute-done.3.refs_0_, bf16[16,128,128]{2,1,0:T(8,128)(2,1)S(1)} %collective-permute-done.2.refs_1_, bf16[16,128,128]{2,1,0:T(8,128)(2,1)S(1)} %copy-done, ...), custom_call_target="tpu_custom_call" | custom-call | flops 1073741824 | bytes 7667712 | tf_op jit(solution)/shard_map/pallas_call | solution.py:74
  74.3 0.0 copy-done.1
  74.3 0.0 copy-done.3
  74.3 0.0 copy-start.16
  74.3 0.0 copy-start.18
  74.3 19.2 %all_to_all.36 = bf16[4,272,512]{2,1,0:T(8,128)(2,1)S(1)} all-to-all(bf16[4,272,512]{2,1,0:T(8,128)(2,1)S(1)} %get-tuple-element.52), channel_id=1, replica_groups=mesh['zl'=4,'core'=2,'row'=4,'zh'=4,'x'=4] {'row'}, dimensions={0} | all-to-all | bytes 2228224 | tf_op jit(solution)/shard_map/all_to_all | solution.py:51
  93.5 0.0 copy-done.16
  93.5 0.0 copy-done.18
  93.6 0.1 convert_reduce_fusion
  93.7 0.2 multiply_reduce_fusion
  94.0 0.1 broadcast_in_dim.8
  94.1 0.0 copy-start.2
  94.1 0.0 copy-start.4
  94.1 16.8 %all_to_all.37.acts = bf16[4,272,512]{2,1,0:T(8,128)(2,1)S(1)} all-to-all(bf16[4,272,512]{2,1,0:T(8,128)(2,1)S(1)} %broadcast_in_dim.8), channel_id=1, replica_groups=mesh['zl'=4,'core'=2,'row'=4,'zh'=4,'x'=4] {'row'}, dimensions={0} | all-to-all | bytes 2228224 | tf_op jit(solution)/shard_map/all_to_all | solution.py:47
  111.0 0.0 copy-done.2
  111.0 2.3 %shard_map.184 = bf16[8,272,256]{2,1,0:T(8,128)(2,1)} custom-call(bf16[4,272,512]{2,1,0:T(8,128)(2,1)S(1)} %all_to_all.37.acts, bf16[16,128,128]{2,1,0:T(8,128)(2,1)S(1)} %copy-done.2, bf16[16,128,128]{2,1,0:T(8,128)(2,1)S(1)} %collective-permute-done.2.refs_1_, bf16[16,128,128]{2,1,0:T(8,128)(2,1)S(1)} %copy-done, bf16[16,128,128]{2,1,0:T(8,128)(2,1)S(1)} %copy-done.4), custom_call_target="tpu_custom_call" | custom-call | flops 536870912 | bytes 4325376 | tf_op jit(solution)/shard_map/pallas_call | solution.py:74
  113.2 7.0 %all-to-all-start.3 = ((bf16[8,272,256]{2,1,0:T(8,128)(2,1)}), bf16[8,272,256]{2,1,0:T(8,128)(2,1)S(1)}, u32[]{:S(2)}, u32[]{:S(2)}) async-start(bf16[8,272,256]{2,1,0:T(8,128)(2,1)} %shard_map.184), calls=%async_computation.3 | async-start | bytes 2228224 | tf_op jit(solution)/shard_map/all_to_all | solution.py:51
  120.2 1.2 copy-done.17
  121.5 1.2 copy-done.19
  122.7 3.2 %shard_map.186 = (bf16[16,128,128]{2,1,0:T(8,128)(2,1)}, bf16[16,128,128]{2,1,0:T(8,128)(2,1)S(1)}, bf16[16,128,128]{2,1,0:T(8,128)(2,1)S(1)}, bf16[16,128,128]{2,1,0:T(8,128)(2,1)}) custom-call(bf16[4,272,512]{2,1,0:T(8,128)(2,1)S(1)} %all_to_all.37.acts, bf16[1024,512]{1,0:T(8,128)(2,1)S(1)} %copy-done.17, bf16[1024,512]{1,0:T(8,128)(2,1)S(1)} %copy-done.19), custom_call_target="tpu_custom_call" | custom-call | flops 1073741824 | bytes 5308416 | tf_op jit(solution)/shard_map/pallas_call | solution.py:74
  125.9 1.9 %collective-permute-start.7 = (bf16[16,128,128]{2,1,0:T(8,128)(2,1)}, bf16[16,128,128]{2,1,0:T(8,128)(2,1)S(1)}, u32[]{:S(2)}, u32[]{:S(2)}) collective-permute-start(bf16[16,128,128]{2,1,0:T(8,128)(2,1)} %get-tuple-element.61), channel_id=1, source_target_pairs={{0,396},{64,192},{128,0},{192,320},{256,128},{320,448},{384,256},{... | collective-permute-start | bytes 1572872 | tf_op jit(solution)/shard_map/ppermute | solution.py:66
  127.8 4.6 %collective-permute-start.6 = (bf16[16,128,128]{2,1,0:T(8,128)(2,1)}, bf16[16,128,128]{2,1,0:T(8,128)(2,1)S(1)}, u32[]{:S(2)}, u32[]{:S(2)}) collective-permute-start(bf16[16,128,128]{2,1,0:T(8,128)(2,1)} %get-tuple-element.54), channel_id=1, source_target_pairs={{0,128},{64,460},{128,256},{192,64},{256,384},{320,192},{384,4},{4... | collective-permute-start | bytes 1572872 | tf_op jit(solution)/shard_map/ppermute | solution.py:66
  132.4 3.9 %all-to-all-done.3.pieces = bf16[8,272,256]{2,1,0:T(8,128)(2,1)S(1)} async-done(((bf16[8,272,256]{2,1,0:T(8,128)(2,1)}), bf16[8,272,256]{2,1,0:T(8,128)(2,1)S(1)}, u32[]{:S(2)}, u32[]{:S(2)}) %all-to-all-start.3) | async-done | bytes 1114144 | tf_op jit(solution)/shard_map/all_to_all | solution.py:51
  136.2 0.8 shard_map.185
  137.0 0.0 copy-start.15
  137.1 6.5 %all-to-all-start.4 = ((bf16[4,80,256]{2,1,0:T(8,128)(2,1)}), bf16[4,80,256]{2,1,0:T(8,128)(2,1)S(1)}, u32[]{:S(2)}, u32[]{:S(2)}) async-start(bf16[4,80,256]{2,1,0:T(8,128)(2,1)} %shard_map.185), calls=%async_computation.4 | async-start | bytes 327680 | tf_op jit(solution)/shard_map/all_to_all | solution.py:51
  143.5 0.0 collective-permute-done.7
  143.6 1.0 add_convert_fusion
  144.5 2.0 %collective-permute-start.8 = (bf16[16,128,128]{2,1,0:T(8,128)(2,1)}, bf16[16,128,128]{2,1,0:T(8,128)(2,1)S(1)}, u32[]{:S(2)}, u32[]{:S(2)}) collective-permute-start(bf16[16,128,128]{2,1,0:T(8,128)(2,1)} %add_convert_fusion), channel_id=1, source_target_pairs={{0,396},{64,192},{128,0},{192,320},{256,128},{320,448},{384,256},{... | collective-permute-start | bytes 1572872 | tf_op jit(solution)/shard_map/ppermute | solution.py:66
  146.6 1.1 shard_map.183.refs_2_
  147.8 0.0 copy-start.13
  147.8 0.0 collective-permute-done.6.refs_0_
  147.8 8.6 %all-to-all-done.4.refs_4_ = bf16[4,80,256]{2,1,0:T(8,128)(2,1)S(1)} async-done(((bf16[4,80,256]{2,1,0:T(8,128)(2,1)}), bf16[4,80,256]{2,1,0:T(8,128)(2,1)S(1)}, u32[]{:S(2)}, u32[]{:S(2)}) %all-to-all-start.4) | async-done | bytes 163872 | tf_op jit(solution)/shard_map/all_to_all | solution.py:51
  156.3 1.7 shard_map.187
  158.0 3.8 %collective-permute-start.9 = (bf16[128,256]{1,0:T(8,128)(2,1)S(1)}, bf16[128,256]{1,0:T(8,128)(2,1)S(1)}, u32[]{:S(2)}, u32[]{:S(2)}) collective-permute-start(bf16[128,256]{1,0:T(8,128)(2,1)S(1)} %get-tuple-element.63), channel_id=1, source_target_pairs={{0,64},{64,0},{1,65},{65,1},{2,66},{66,2},{3,67},{67,3},{4,68},{68... | collective-permute-start | bytes 196616 | tf_op jit(solution)/shard_map/ppermute | solution.py:563
  161.8 3.2 %collective-permute-start.10 = (bf16[128,256]{1,0:T(8,128)(2,1)S(1)}, bf16[128,256]{1,0:T(8,128)(2,1)S(1)}, u32[]{:S(2)}, u32[]{:S(2)}) collective-permute-start(bf16[128,256]{1,0:T(8,128)(2,1)S(1)} %get-tuple-element.64), channel_id=1, source_target_pairs={{64,128},{192,256},{320,384},{128,64},{256,192},{384,320},{65,129}... | collective-permute-start | bytes 196616 | tf_op jit(solution)/shard_map/ppermute | solution.py:564
  165.0 4.3 %all-to-all-start.5 = ((f32[8,1,64]{2,1,0:T(1,128)}), f32[8,1,64]{2,1,0:T(1,128)S(1)}, u32[]{:S(2)}, u32[]{:S(2)}) async-start(f32[8,1,64]{2,1,0:T(1,128)} %bitcast.16), calls=%async_computation.5 | async-start | bytes 8192 | tf_op jit(solution)/shard_map/all_to_all | solution.py:51
  169.3 0.0 collective-permute-done.8.refs_1_
  169.3 0.9 shard_map.189
  170.2 3.8 %all-to-all-done.5 = f32[8,1,64]{2,1,0:T(1,128)S(1)} async-done(((f32[8,1,64]{2,1,0:T(1,128)}), f32[8,1,64]{2,1,0:T(1,128)S(1)}, u32[]{:S(2)}, u32[]{:S(2)}) %all-to-all-start.5) | async-done | bytes 2080 | tf_op jit(solution)/shard_map/all_to_all | solution.py:51
  174.1 0.0 collective-permute-done.9.inside
  174.1 0.0 collective-permute-done.10.outside
  174.1 0.6 shard_map.188
  (29 shorter events, 0.1 us)
Async XLA Ops:
  2.7 39.6 %collective-permute-start.2 = (bf16[16,128,128]{2,1,0:T(8,128)(2,1)}, bf16[16,128,128]{2,1,0:T(8,128)(2,1)S(1)}, u32[]{:S(2)}, u32[]{:S(2)}) collective-permute-start(bf16[16,128,128]{2,1,0:T(8,128)(2,1)} %get-tuple-element.46.refs_2_), channel_id=1, source_target_pairs={{396,0},{192,64},{0,128},{320,192},{128,256},{448,320},{256,384},{... | collective-permute-start | bytes 1572872 | tf_op jit(solution)/shard_map/ppermute | solution.py:66
  14.7 6.1 %collective-permute-start.1 = (bf16[128,256]{1,0:T(8,128)(2,1)}, bf16[128,256]{1,0:T(8,128)(2,1)S(1)}, u32[]{:S(2)}, u32[]{:S(2)}) collective-permute-start(bf16[128,256]{1,0:T(8,128)(2,1)} %get-tuple-element.41.refs_7_.own.refs_9_), channel_id=1, source_target_pairs={{64,128},{192,256},{320,384},{128,64},{256,192},{384,320},{65,129}... | collective-permute-start | bytes 196616 | tf_op jit(solution)/shard_map/ppermute | solution.py:443
  16.6 4.2 %collective-permute-start = (bf16[128,256]{1,0:T(8,128)(2,1)}, bf16[128,256]{1,0:T(8,128)(2,1)S(1)}, u32[]{:S(2)}, u32[]{:S(2)}) collective-permute-start(bf16[128,256]{1,0:T(8,128)(2,1)} %get-tuple-element.41.refs_7_.own.refs_9_), channel_id=1, source_target_pairs={{0,64},{64,0},{1,65},{65,1},{2,66},{66,2},{3,67},{67,3},{4,68},{68... | collective-permute-start | bytes 196616 | tf_op jit(solution)/shard_map/ppermute | solution.py:442
  20.8 0.6 copy-start.6
  20.8 0.6 copy-start.8
  43.4 7.0 %copy-start = (bf16[16,128,128]{2,1,0:T(8,128)(2,1)S(1)}, bf16[16,128,128]{2,1,0:T(8,128)(2,1)}, u32[]{:S(2)}) copy-start(bf16[16,128,128]{2,1,0:T(8,128)(2,1)} %get-tuple-element.46.refs_2_) | copy-start | bytes 1572868
  43.4 22.3 %all-to-all-start = ((bf16[4,4,144,256]{3,2,1,0:T(8,128)(2,1)}), bf16[4,4,144,256]{3,2,1,0:T(8,128)(2,1)S(1)}, u32[]{:S(2)}, u32[]{:S(2)}) async-start(bf16[4,4,144,256]{3,2,1,0:T(8,128)(2,1)} %broadcast_in_dim.7), calls=%async_computation | async-start | bytes 2359296 | tf_op jit(solution)/shard_map/all_to_all | solution.py:47
  47.6 10.2 %collective-permute-start.3 = (bf16[16,128,128]{2,1,0:T(8,128)(2,1)S(1)}, bf16[16,128,128]{2,1,0:T(8,128)(2,1)S(1)}, u32[]{:S(2)}, u32[]{:S(2)}) collective-permute-start(bf16[16,128,128]{2,1,0:T(8,128)(2,1)S(1)} %collective-permute-done.2.refs_1_), channel_id=1, source_target_pairs={{396,0},{192,64},{0,128},{320,192},{128,256},{448,320},{256,384},{... | collective-permute-start | bytes 1572872 | tf_op jit(solution)/shard_map/ppermute | solution.py:66
  50.5 15.3 %collective-permute-start.4 = (bf16[16,128,128]{2,1,0:T(8,128)(2,1)S(1)}, bf16[16,128,128]{2,1,0:T(8,128)(2,1)S(1)}, u32[]{:S(2)}, u32[]{:S(2)}) collective-permute-start(bf16[16,128,128]{2,1,0:T(8,128)(2,1)S(1)} %copy-done), channel_id=1, source_target_pairs={{128,0},{460,64},{256,128},{64,192},{384,256},{192,320},{4,384},{3... | collective-permute-start | bytes 1572872 | tf_op jit(solution)/shard_map/ppermute | solution.py:66
  57.8 16.5 %copy-start.1 = (bf16[16,128,128]{2,1,0:T(8,128)(2,1)}, bf16[16,128,128]{2,1,0:T(8,128)(2,1)S(1)}, u32[]{:S(2)}) copy-start(bf16[16,128,128]{2,1,0:T(8,128)(2,1)S(1)} %collective-permute-done.3.refs_0_) | copy-start | bytes 1572868
  65.8 8.5 %copy-start.3 = (bf16[16,128,128]{2,1,0:T(8,128)(2,1)}, bf16[16,128,128]{2,1,0:T(8,128)(2,1)S(1)}, u32[]{:S(2)}) copy-start(bf16[16,128,128]{2,1,0:T(8,128)(2,1)S(1)} %collective-permute-done.4.refs_3_) | copy-start | bytes 1572868
  65.8 6.5 %collective-permute-start.5 = (bf16[4,4,144,256]{3,2,1,0:T(8,128)(2,1)S(1)}, bf16[4,4,144,256]{3,2,1,0:T(8,128)(2,1)S(1)}, u32[]{:S(2)}, u32[]{:S(2)}) collective-permute-start(bf16[4,4,144,256]{3,2,1,0:T(8,128)(2,1)S(1)} %all-to-all-done.refs_4_), channel_id=1, source_target_pairs={{0,64},{64,0},{1,65},{65,1},{2,66},{66,2},{3,67},{67,3},{4,68},{68... | collective-permute-start | bytes 3538952 | tf_op jit(solution)/shard_map/ppermute | solution.py:472
  74.3 19.2 %copy-start.16 = (bf16[1024,512]{1,0:T(8,128)(2,1)}, bf16[1024,512]{1,0:T(8,128)(2,1)S(1)}, u32[]{:S(2)}) copy-start(bf16[1024,512]{1,0:T(8,128)(2,1)S(1)} %get-tuple-element.50.feats) | copy-start | bytes 3145732
  74.3 19.2 %copy-start.18 = (bf16[1024,512]{1,0:T(8,128)(2,1)}, bf16[1024,512]{1,0:T(8,128)(2,1)S(1)}, u32[]{:S(2)}) copy-start(bf16[1024,512]{1,0:T(8,128)(2,1)S(1)} %get-tuple-element.53.cots) | copy-start | bytes 3145732
  94.1 16.9 %copy-start.2 = (bf16[16,128,128]{2,1,0:T(8,128)(2,1)S(1)}, bf16[16,128,128]{2,1,0:T(8,128)(2,1)}, u32[]{:S(2)}) copy-start(bf16[16,128,128]{2,1,0:T(8,128)(2,1)} %copy-done.1) | copy-start | bytes 1572868
  94.1 16.8 %copy-start.4 = (bf16[16,128,128]{2,1,0:T(8,128)(2,1)S(1)}, bf16[16,128,128]{2,1,0:T(8,128)(2,1)}, u32[]{:S(2)}) copy-start(bf16[16,128,128]{2,1,0:T(8,128)(2,1)} %copy-done.3) | copy-start | bytes 1572868
  113.2 23.0 %all-to-all-start.3 = ((bf16[8,272,256]{2,1,0:T(8,128)(2,1)}), bf16[8,272,256]{2,1,0:T(8,128)(2,1)S(1)}, u32[]{:S(2)}, u32[]{:S(2)}) async-start(bf16[8,272,256]{2,1,0:T(8,128)(2,1)} %shard_map.184), calls=%async_computation.3 | async-start | bytes 2228224 | tf_op jit(solution)/shard_map/all_to_all | solution.py:51
  120.2 1.2 copy-start.17
  121.5 1.2 copy-start.19
  125.9 17.7 %collective-permute-start.7 = (bf16[16,128,128]{2,1,0:T(8,128)(2,1)}, bf16[16,128,128]{2,1,0:T(8,128)(2,1)S(1)}, u32[]{:S(2)}, u32[]{:S(2)}) collective-permute-start(bf16[16,128,128]{2,1,0:T(8,128)(2,1)} %get-tuple-element.61), channel_id=1, source_target_pairs={{0,396},{64,192},{128,0},{192,320},{256,128},{320,448},{384,256},{... | collective-permute-start | bytes 1572872 | tf_op jit(solution)/shard_map/ppermute | solution.py:66
  127.8 20.0 %collective-permute-start.6 = (bf16[16,128,128]{2,1,0:T(8,128)(2,1)}, bf16[16,128,128]{2,1,0:T(8,128)(2,1)S(1)}, u32[]{:S(2)}, u32[]{:S(2)}) collective-permute-start(bf16[16,128,128]{2,1,0:T(8,128)(2,1)} %get-tuple-element.54), channel_id=1, source_target_pairs={{0,128},{64,460},{128,256},{192,64},{256,384},{320,192},{384,4},{4... | collective-permute-start | bytes 1572872 | tf_op jit(solution)/shard_map/ppermute | solution.py:66
  137.0 9.6 %copy-start.5 = (bf16[128,256]{1,0:T(8,128)(2,1)S(1)}, bf16[128,256]{1,0:T(8,128)(2,1)}, u32[]{:S(2)}) copy-start(bf16[128,256]{1,0:T(8,128)(2,1)} %get-tuple-element.41.refs_7_.own.refs_9_) | copy-start | bytes 196612
  137.0 9.6 %copy-start.7 = (bf16[128,256]{1,0:T(8,128)(2,1)S(1)}, bf16[128,256]{1,0:T(8,128)(2,1)}, u32[]{:S(2)}) copy-start(bf16[128,256]{1,0:T(8,128)(2,1)} %copy-done.6) | copy-start | bytes 196612
  137.0 9.6 %copy-start.9 = (bf16[128,256]{1,0:T(8,128)(2,1)S(1)}, bf16[128,256]{1,0:T(8,128)(2,1)}, u32[]{:S(2)}) copy-start(bf16[128,256]{1,0:T(8,128)(2,1)} %copy-done.8) | copy-start | bytes 196612
  137.0 9.6 %copy-start.11 = (bf16[256,64]{0,1:T(8,128)(2,1)S(1)}, bf16[256,64]{0,1:T(8,128)(2,1)}, u32[]{:S(2)}) copy-start(bf16[256,64]{0,1:T(8,128)(2,1)} %param.14) | copy-start | bytes 98308
  137.0 9.6 %copy-start.15 = (s32[64]{0:T(128)S(1)}, s32[64]{0:T(128)}, u32[]{:S(2)}) copy-start(s32[64]{0:T(128)} %reaches.1) | copy-start | bytes 772
  137.1 19.3 %all-to-all-start.4 = ((bf16[4,80,256]{2,1,0:T(8,128)(2,1)}), bf16[4,80,256]{2,1,0:T(8,128)(2,1)S(1)}, u32[]{:S(2)}, u32[]{:S(2)}) async-start(bf16[4,80,256]{2,1,0:T(8,128)(2,1)} %shard_map.185), calls=%async_computation.4 | async-start | bytes 327680 | tf_op jit(solution)/shard_map/all_to_all | solution.py:51
  144.5 11.8 %copy-start.10 = (bf16[256,64]{0,1:T(8,128)(2,1)S(1)}, bf16[256,64]{0,1:T(8,128)(2,1)}, u32[]{:S(2)}) copy-start(bf16[256,64]{0,1:T(8,128)(2,1)} %param.25) | copy-start | bytes 98308
  144.5 11.8 %copy-start.12 = (bf16[64,256]{1,0:T(8,128)(2,1)S(1)}, bf16[64,256]{1,0:T(8,128)(2,1)}, u32[]{:S(2)}) copy-start(bf16[64,256]{1,0:T(8,128)(2,1)} %get-tuple-element.56.refs_5_) | copy-start | bytes 98308
  144.5 11.8 %copy-start.14 = (f32[64]{0:T(128)S(1)}, f32[64]{0:T(128)}, u32[]{:S(2)}) copy-start(f32[64]{0:T(128)} %param.18) | copy-start | bytes 772
  144.5 24.8 %collective-permute-start.8 = (bf16[16,128,128]{2,1,0:T(8,128)(2,1)}, bf16[16,128,128]{2,1,0:T(8,128)(2,1)S(1)}, u32[]{:S(2)}, u32[]{:S(2)}) collective-permute-start(bf16[16,128,128]{2,1,0:T(8,128)(2,1)} %add_convert_fusion), channel_id=1, source_target_pairs={{0,396},{64,192},{128,0},{192,320},{256,128},{320,448},{384,256},{... | collective-permute-start | bytes 1572872 | tf_op jit(solution)/shard_map/ppermute | solution.py:66
  147.8 21.6 %copy-start.13 = (f32[16,128]{1,0:T(8,128)S(1)}, f32[16,128]{1,0:T(8,128)}, u32[]{:S(2)}) copy-start(f32[16,128]{1,0:T(8,128)} %get-tuple-element.72.refs_3_) | copy-start | bytes 24580
  158.0 16.1 %collective-permute-start.9 = (bf16[128,256]{1,0:T(8,128)(2,1)S(1)}, bf16[128,256]{1,0:T(8,128)(2,1)S(1)}, u32[]{:S(2)}, u32[]{:S(2)}) collective-permute-start(bf16[128,256]{1,0:T(8,128)(2,1)S(1)} %get-tuple-element.63), channel_id=1, source_target_pairs={{0,64},{64,0},{1,65},{65,1},{2,66},{66,2},{3,67},{67,3},{4,68},{68... | collective-permute-start | bytes 196616 | tf_op jit(solution)/shard_map/ppermute | solution.py:563
  161.8 12.3 %collective-permute-start.10 = (bf16[128,256]{1,0:T(8,128)(2,1)S(1)}, bf16[128,256]{1,0:T(8,128)(2,1)S(1)}, u32[]{:S(2)}, u32[]{:S(2)}) collective-permute-start(bf16[128,256]{1,0:T(8,128)(2,1)S(1)} %get-tuple-element.64), channel_id=1, source_target_pairs={{64,128},{192,256},{320,384},{128,64},{256,192},{384,320},{65,129}... | collective-permute-start | bytes 196616 | tf_op jit(solution)/shard_map/ppermute | solution.py:564
  165.0 9.1 %all-to-all-start.5 = ((f32[8,1,64]{2,1,0:T(1,128)}), f32[8,1,64]{2,1,0:T(1,128)S(1)}, u32[]{:S(2)}, u32[]{:S(2)}) async-start(f32[8,1,64]{2,1,0:T(1,128)} %bitcast.16), calls=%async_computation.5 | async-start | bytes 8192 | tf_op jit(solution)/shard_map/all_to_all | solution.py:51

commit v6 on v5

--- a/solution.py
+++ b/solution.py
@@ -204,12 +204,13 @@
 
 
 def attend_body(seq_devs, *refs):
-    sources, (inside, outside, own), (send, hidden_ref) = refs[:5], refs[5:8], refs[8:10]
-    query, stream, gain_row, reaches, halo, arrived = refs[10:]
+    sources, (send, hidden_ref) = refs[:8], refs[8:10]
+    query, stream, gain_row, reaches, own, halo, arrived = refs[10:]
     head, tok = query.shape
     cot_rows = send.at[head : 2 * head, :]
-    load_all(sources, (query, stream, gain_row, reaches, cot_rows), arrived)
-    sort_halo(inside, outside, halo)
+    core = lax.axis_index("core")
+    sides = (halo.at[1 - core], halo.at[core])
+    load_all(sources, (query, stream, gain_row, reaches, cot_rows, own) + sides, arrived)
     parts = (halo.at[0], own, halo.at[1])
     probs = head_probs(parts, query, own_reach(reaches), seq_devs)
     attended = sum(dot_plain(parts[p][head:, :], probs[p].astype(BF)) for p in range(3))
@@ -267,28 +268,30 @@
 
 
 def norm_grad_body(head, n_zh, n_x, slots, acts, *refs):
-    weights, out = refs[:slots], refs[slots]
+    weights, outs = refs[:slots], refs[slots:]
     units = weights[0].shape[2]
     blocks = weights[0].shape[0] // 2
     tok = acts.shape[2] // 2
     per_block = BLK // head
-    n_core = out.shape[0] // n_x
+    core = lax.axis_index("core")
     for b in range(blocks):
         total = jnp.zeros((BLK, 2 * tok), F32)
         for w in range(slots):
             total += dot_plain(weights[w][b], acts[w, units : 2 * units, :])
-        total = total.astype(BF)
-        for k in range(per_block):
-            zh, x = divmod(b * per_block + k, n_x)
-            rows = slice(zh * head, (zh + 1) * head)
-            for c in range(n_core):
-                out[c * n_x + x, rows, :] = total[
-                    k * head : (k + 1) * head, c * tok : (c + 1) * tok
-                ]
+        first, second = total[:, :tok], total[:, tok:]
+        halves = (jnp.where(core == 0, first, second), jnp.where(core == 0, second, first))
+        for half, out in zip(halves, outs, strict=True):
+            half = half.astype(BF)
+            for k in range(per_block):
+                zh, x = divmod(b * per_block + k, n_x)
+                rows = slice(zh * head, (zh + 1) * head)
+                out[x, rows, :] = half[k * head : (k + 1) * head, :]
     inner = sum(read_tail(acts[w, 2 * units :, :]) for w in range(slots))
-    for x in range(n_x):
-        for c in range(n_core):
-            write_tail(out, (c * n_x + x,), n_zh * head, inner[:, c * tok : (c + 1) * tok])
+    first, second = inner[:, :tok], inner[:, tok:]
+    halves = (jnp.where(core == 0, first, second), jnp.where(core == 0, second, first))
+    for half, out in zip(halves, outs, strict=True):
+        for x in range(n_x):
+            write_tail(out, (x,), n_zh * head, half)
 
 
 def weight_grad_body(slots, acts, feats, cots, *homes):
@@ -301,6 +304,13 @@
         for b in range(blocks):
             block = dot_last(active, cots[b * BLK : (b + 1) * BLK, :])
             homes[w][blocks + b] = block.astype(BF)
+
+
+def core_sum_body(rows, own, theirs, out):
+    for x in range(own.shape[0]):
+        total = own[x, :rows, :].astype(F32) + theirs[x, :rows, :].astype(F32)
+        out[x, :rows, :] = total.astype(BF)
+        write_tail(out, (x,), rows, read_tail(own[x, rows:, :]) + read_tail(theirs[x, rows:, :]))
 
 
 def x_sum_body(head, pieces, out):
@@ -453,11 +463,11 @@
         gain,
         windows,
         cot_t,
+        paired,
         inside,
         outside,
-        paired,
-        loads=5,
-        scratch=[held(query_t), held(stream_t), held(gain), reaches, halo],
+        loads=8,
+        scratch=[held(query_t), held(stream_t), held(gain), reaches, held(paired), halo],
     )
     first = window_send(both, 1, n_zh, n_zl, n_core, False)
 
@@ -494,13 +504,14 @@
     inner_part = jnp.sum(grad_act.astype(F32) * pre_act, axis=0)
     acts = spread(jnp.concatenate([activation, grad_act, tail_rows(inner_part)], axis=0), "row")
 
-    pieces = call_kernel(
+    mine, theirs = call_kernel(
         functools.partial(norm_grad_body, head, n_zh, n_x, n_zl),
-        [shaped((n_core * n_x, n_zh * head + TAIL, tok), BF)],
+        [shaped((n_x, n_zh * head + TAIL, tok), BF)] * 2,
         2 * n_zl * depth * units * both_toks,
         acts,
         *slots,
-    )[0]
+    )
+    theirs = lax.ppermute(theirs, "core", swap)
     homes = call_kernel(
         functools.partial(weight_grad_body, n_zl),
         [shaped((2 * blocks, BLK, units), BF)] * n_zl,
@@ -509,7 +520,14 @@
         feats,
         cots,
     )
-    pieces = exchange(pieces, ("core", "x"))
+    pieces = call_kernel(
+        functools.partial(core_sum_body, n_zh * head),
+        [shaped((n_x, n_zh * head + TAIL, tok), BF)],
+        0,
+        mine,
+        theirs,
+    )[0]
+    pieces = exchange(pieces, "x")
     pieces = call_kernel(
         functools.partial(x_sum_body, head),
         [shaped((n_zh, head + TAIL, tok), BF)],

time: 176 us -> 175 us (level)
  starting transfers between devices: 62.5 us -> 66.6 us
  local copies, waits for them, and re-layouts: 4.32 us -> 1.87 us
  waiting for transfers between devices: 33.9 us -> 31.7 us
    ppermute x1, starting transfers between devices: 3.8 us -> 8.2 us  [on_device(): inside_grad = lax.ppermute(inside_grad, 'core', swap)]
    ppermute x0 -> x1, starting transfers between devices: none -> 4.35 us  [on_device(): theirs = lax.ppermute(theirs, 'core', swap)]
    all_to_all x3, starting transfers between devices: 17.8 us -> 14.3 us  [exchange(): return lax.all_to_all(pieces, axis, 0, 0, tiled=True)]
    unnamed x40 -> x24, local copies, waits for them, and re-layouts: 3.16 us -> 0.68 us
    all_to_all x3, waiting for transfers between devices: 16.3 us -> 14.1 us  [exchange(): return lax.all_to_all(pieces, axis, 0, 0, tiled=True)]
    pallas_call x10 -> x11, Pallas kernels: 17.9 us -> 17 us  [call_kernel(): pl.pallas_call(body, out_shape=out_shapes, in_specs=[pl.BlockSpec(memory_...]
  transfers between devices with their start and end apart: 15 -> 16, of which waited for: 7 -> 7; matrix products, arithmetic and copies ran while one was open for 1% -> 1% of each run, Pallas kernels for 6% -> 6%
where the time goes in v6:
time: 175 us; the launch traced here: 174 us
  starting transfers between devices  66.6 us (38%)
  blocking collectives  53.7 us (31%)
  waiting for transfers between devices  31.7 us (18%)
  Pallas kernels  17 us (10%)
  other arithmetic  2.43 us (1%)
  local copies, waits for them, and re-layouts  1.87 us (1%)
    ppermute x6, starting transfers between devices, window_send(): return lax.ppermute(array, ('zl', 'core', 'zh'), pairs)  25.7 us
    all_to_all x1, blocking collectives, exchange(): return lax.all_to_all(pieces, axis, 0, 0, tiled=True)  19.2 us
    all_gather x1, blocking collectives, on_device(): panel = lax.all_gather(send, 'zh', axis=0, tiled=False)  17.7 us
    pallas_call x11, Pallas kernels, call_kernel(): pl.pallas_call(body, out_shape=out_shapes, in_specs=[pl.BlockSpec(memory_...  17 us
    all_to_all x1, blocking collectives, spread(): return lax.all_to_all(copies, axis, 0, 0, tiled=True)  16.7 us
    all_to_all x3, starting transfers between devices, exchange(): return lax.all_to_all(pieces, axis, 0, 0, tiled=True)  14.3 us
    all_to_all x3, waiting for transfers between devices, exchange(): return lax.all_to_all(pieces, axis, 0, 0, tiled=True)  14.1 us
    ppermute x6, waiting for transfers between devices, window_send(): return lax.ppermute(array, ('zl', 'core', 'zh'), pairs)  12.9 us
  transfers between devices with their start and end apart: 16, of which 7 were waited for; matrix products, arithmetic and copies ran while one was open for 1% of the time, Pallas kernels for 6%

profile of v6, /device:TPU:1, one launch (start us, length us, event | category | flops | bytes accessed | tf_op | source)
XLA Modules:
  0.0 174.2 jit_solution(6970928434727140985)
XLA Ops:
  0.6 2.0 %shard_map.180 = (bf16[16,128,128]{2,1,0:T(8,128)(2,1)}, f32[16,128]{1,0:T(8,128)}, bf16[128,256]{1,0:T(8,128)(2,1)}) custom-call(bf16[1024,128]{1,0:T(8,128)(2,1)} %refs_0_.1, bf16[128,1024]{1,0:T(8,128)(2,1)} %refs_1_.1, s32[16,128]{1,0:T(8,128)} %bitcast.35, s32[16,128]{1,0:T(8,128)} %bitcast.36, s32[16,128]{1,0:T(8,128)} %bitcast.37, ...), custom_call_target="tpu_custom_call" | custom-call | bytes 1220608 | tf_op jit(solution)/shard_map/pallas_call | solution.py:74
  2.7 12.0 %collective-permute-start.2 = (bf16[16,128,128]{2,1,0:T(8,128)(2,1)}, bf16[16,128,128]{2,1,0:T(8,128)(2,1)S(1)}, u32[]{:S(2)}, u32[]{:S(2)}) collective-permute-start(bf16[16,128,128]{2,1,0:T(8,128)(2,1)} %get-tuple-element.48.refs_2_), channel_id=1, source_target_pairs={{396,0},{192,64},{0,128},{320,192},{128,256},{448,320},{256,384},{... | collective-permute-start | bytes 1572872 | tf_op jit(solution)/shard_map/ppermute | solution.py:66
  14.7 1.9 %collective-permute-start.1 = (bf16[128,256]{1,0:T(8,128)(2,1)}, bf16[128,256]{1,0:T(8,128)(2,1)S(1)}, u32[]{:S(2)}, u32[]{:S(2)}) collective-permute-start(bf16[128,256]{1,0:T(8,128)(2,1)} %get-tuple-element.43.refs_5_.own.refs_9_), channel_id=1, source_target_pairs={{64,128},{192,256},{320,384},{128,64},{256,192},{384,320},{65,129}... | collective-permute-start | bytes 196616 | tf_op jit(solution)/shard_map/ppermute | solution.py:453
  16.6 1.9 %collective-permute-start = (bf16[128,256]{1,0:T(8,128)(2,1)}, bf16[128,256]{1,0:T(8,128)(2,1)S(1)}, u32[]{:S(2)}, u32[]{:S(2)}) collective-permute-start(bf16[128,256]{1,0:T(8,128)(2,1)} %get-tuple-element.43.refs_5_.own.refs_9_), channel_id=1, source_target_pairs={{0,64},{64,0},{1,65},{65,1},{2,66},{66,2},{3,67},{67,3},{4,68},{68... | collective-permute-start | bytes 196616 | tf_op jit(solution)/shard_map/ppermute | solution.py:452
  18.5 2.2 %collective-permute-done.1.refs_7_.outside.refs_8_ = bf16[128,256]{1,0:T(8,128)(2,1)S(1)} collective-permute-done((bf16[128,256]{1,0:T(8,128)(2,1)}, bf16[128,256]{1,0:T(8,128)(2,1)S(1)}, u32[]{:S(2)}, u32[]{:S(2)}) %collective-permute-start.1) | collective-permute-done | bytes 65568 | tf_op jit(solution)/shard_map/ppermute | solution.py:453
  20.7 0.0 collective-permute-done.refs_6_.inside.refs_7_
  20.7 0.6 copy-done.2
  21.4 0.0 copy-done.4
  21.4 2.5 %shard_map.181 = (bf16[144,256]{1,0:T(8,128)(2,1)}, bf16[64,256]{1,0:T(8,128)(2,1)}) custom-call(bf16[64,256]{1,0:T(8,128)(2,1)} %bitcast.24, bf16[64,256]{1,0:T(8,128)(2,1)} %bitcast.34, f32[1,64]{1,0:T(1,128)} %bitcast.29, s32[64]{0:T(128)} %reaches.1, bf16[64,256]{1,0:T(8,128)(2,1)} %bitcast.22, bf16[128,256]{1,0:T(8,128)(2,1)} %get-tuple-element.43.refs_5_.own.refs_9_, ...), custom_call_target="tpu_custom_call" | custom-call | flops 50331648 | bytes 401920 | tf_op jit(solution)/shard_map/pallas_call | solution.py:74
  23.9 17.7 %all-gather = bf16[576,256]{1,0:T(8,128)(2,1)S(1)} all-gather(bf16[144,256]{1,0:T(8,128)(2,1)} %get-tuple-element.44), channel_id=2, replica_groups=mesh['zl'=4,'core'=2,'row'=4,'zh'=4,'x'=4] {'zh'}, dimensions={0}, use_global_device_ids=true | all-gather | bytes 368640 | tf_op jit(solution)/shard_map/all_gather | solution.py:474
  41.6 0.0 collective-permute-done.2.refs_1_
  41.6 1.1 broadcast_in_dim.7
  42.7 4.1 %all-to-all-start = ((bf16[4,4,144,256]{3,2,1,0:T(8,128)(2,1)}), bf16[4,4,144,256]{3,2,1,0:T(8,128)(2,1)S(1)}, u32[]{:S(2)}, u32[]{:S(2)}) async-start(bf16[4,4,144,256]{3,2,1,0:T(8,128)(2,1)} %broadcast_in_dim.7), calls=%async_computation | async-start | bytes 2359296 | tf_op jit(solution)/shard_map/all_to_all | solution.py:47
  46.9 2.9 %collective-permute-start.3 = (bf16[16,128,128]{2,1,0:T(8,128)(2,1)S(1)}, bf16[16,128,128]{2,1,0:T(8,128)(2,1)S(1)}, u32[]{:S(2)}, u32[]{:S(2)}) collective-permute-start(bf16[16,128,128]{2,1,0:T(8,128)(2,1)S(1)} %collective-permute-done.2.refs_1_), channel_id=1, source_target_pairs={{396,0},{192,64},{0,128},{320,192},{128,256},{448,320},{256,384},{... | collective-permute-start | bytes 1572872 | tf_op jit(solution)/shard_map/ppermute | solution.py:66
  49.8 0.0 copy-done
  49.8 2.4 %collective-permute-start.4 = (bf16[16,128,128]{2,1,0:T(8,128)(2,1)S(1)}, bf16[16,128,128]{2,1,0:T(8,128)(2,1)S(1)}, u32[]{:S(2)}, u32[]{:S(2)}) collective-permute-start(bf16[16,128,128]{2,1,0:T(8,128)(2,1)S(1)} %copy-done), channel_id=1, source_target_pairs={{128,0},{460,64},{256,128},{64,192},{384,256},{192,320},{4,384},{3... | collective-permute-start | bytes 1572872 | tf_op jit(solution)/shard_map/ppermute | solution.py:66
  52.2 4.9 %collective-permute-done.3.refs_0_ = bf16[16,128,128]{2,1,0:T(8,128)(2,1)S(1)} collective-permute-done((bf16[16,128,128]{2,1,0:T(8,128)(2,1)S(1)}, bf16[16,128,128]{2,1,0:T(8,128)(2,1)S(1)}, u32[]{:S(2)}, u32[]{:S(2)}) %collective-permute-start.3) | collective-permute-done | bytes 524320 | tf_op jit(solution)/shard_map/ppermute | solution.py:66
  57.1 8.0 %collective-permute-done.4.refs_3_ = bf16[16,128,128]{2,1,0:T(8,128)(2,1)S(1)} collective-permute-done((bf16[16,128,128]{2,1,0:T(8,128)(2,1)S(1)}, bf16[16,128,128]{2,1,0:T(8,128)(2,1)S(1)}, u32[]{:S(2)}, u32[]{:S(2)}) %collective-permute-start.4) | collective-permute-done | bytes 524320 | tf_op jit(solution)/shard_map/ppermute | solution.py:66
  65.1 0.0 all-to-all-done.refs_4_
  65.1 4.1 %collective-permute-start.5 = (bf16[4,4,144,256]{3,2,1,0:T(8,128)(2,1)S(1)}, bf16[4,4,144,256]{3,2,1,0:T(8,128)(2,1)S(1)}, u32[]{:S(2)}, u32[]{:S(2)}) collective-permute-start(bf16[4,4,144,256]{3,2,1,0:T(8,128)(2,1)S(1)} %all-to-all-done.refs_4_), channel_id=1, source_target_pairs={{0,64},{64,0},{1,65},{65,1},{2,66},{66,2},{3,67},{67,3},{4,68},{68... | collective-permute-start | bytes 3538952 | tf_op jit(solution)/shard_map/ppermute | solution.py:482
  69.1 2.5 %collective-permute-done.5.refs_5_ = bf16[4,4,144,256]{3,2,1,0:T(8,128)(2,1)S(1)} collective-permute-done((bf16[4,4,144,256]{3,2,1,0:T(8,128)(2,1)S(1)}, bf16[4,4,144,256]{3,2,1,0:T(8,128)(2,1)S(1)}, u32[]{:S(2)}, u32[]{:S(2)}) %collective-permute-start.5) | collective-permute-done | bytes 1179680 | tf_op jit(solution)/shard_map/ppermute | solution.py:482
  71.6 2.0 %shard_map.182 = (bf16[4,272,512]{2,1,0:T(8,128)(2,1)S(1)}, bf16[1024,512]{1,0:T(8,128)(2,1)S(1)}, bf16[1024,512]{1,0:T(8,128)(2,1)S(1)}) custom-call(bf16[16,128,128]{2,1,0:T(8,128)(2,1)S(1)} %collective-permute-done.3.refs_0_, bf16[16,128,128]{2,1,0:T(8,128)(2,1)S(1)} %collective-permute-done.2.refs_1_, bf16[16,128,128]{2,1,0:T(8,128)(2,1)S(1)} %copy-done, ...), custom_call_target="tpu_custom_call" | custom-call | flops 1073741824 | bytes 7667712 | tf_op jit(solution)/shard_map/pallas_call | solution.py:74
  73.6 19.2 %all_to_all.36 = bf16[4,272,512]{2,1,0:T(8,128)(2,1)S(1)} all-to-all(bf16[4,272,512]{2,1,0:T(8,128)(2,1)S(1)} %get-tuple-element.54), channel_id=1, replica_groups=mesh['zl'=4,'core'=2,'row'=4,'zh'=4,'x'=4] {'row'}, dimensions={0} | all-to-all | bytes 2228224 | tf_op jit(solution)/shard_map/all_to_all | solution.py:51
  92.8 0.1 convert_reduce_fusion
  93.0 0.2 multiply_reduce_fusion
  93.3 0.1 broadcast_in_dim.8
  93.4 16.7 %all_to_all.37.acts = bf16[4,272,512]{2,1,0:T(8,128)(2,1)S(1)} all-to-all(bf16[4,272,512]{2,1,0:T(8,128)(2,1)S(1)} %broadcast_in_dim.8), channel_id=1, replica_groups=mesh['zl'=4,'core'=2,'row'=4,'zh'=4,'x'=4] {'row'}, dimensions={0} | all-to-all | bytes 2228224 | tf_op jit(solution)/shard_map/all_to_all | solution.py:47
  110.1 1.2 shard_map.184
  111.3 4.3 %collective-permute-start.6 = (bf16[4,272,256]{2,1,0:T(8,128)(2,1)S(1)}, bf16[4,272,256]{2,1,0:T(8,128)(2,1)S(1)}, u32[]{:S(2)}, u32[]{:S(2)}) collective-permute-start(bf16[4,272,256]{2,1,0:T(8,128)(2,1)S(1)} %get-tuple-element.56), channel_id=1, source_target_pairs={{0,64},{64,0},{1,65},{65,1},{2,66},{66,2},{3,67},{67,3},{4,68},{68... | collective-permute-start | bytes 1671176 | tf_op jit(solution)/shard_map/ppermute | solution.py:514
  115.7 3.2 %shard_map.187 = (bf16[16,128,128]{2,1,0:T(8,128)(2,1)}, bf16[16,128,128]{2,1,0:T(8,128)(2,1)S(1)}, bf16[16,128,128]{2,1,0:T(8,128)(2,1)S(1)}, bf16[16,128,128]{2,1,0:T(8,128)(2,1)}) custom-call(bf16[4,272,512]{2,1,0:T(8,128)(2,1)S(1)} %all_to_all.37.acts, bf16[1024,512]{1,0:T(8,128)(2,1)S(1)} %get-tuple-element.52.feats, ...), custom_call_target="tpu_custom_call" | custom-call | flops 1073741824 | bytes 5308416 | tf_op jit(solution)/shard_map/pallas_call | solution.py:74
  118.9 1.9 %collective-permute-start.8 = (bf16[16,128,128]{2,1,0:T(8,128)(2,1)}, bf16[16,128,128]{2,1,0:T(8,128)(2,1)}, u32[]{:S(2)}, u32[]{:S(2)}) collective-permute-start(bf16[16,128,128]{2,1,0:T(8,128)(2,1)} %get-tuple-element.65), channel_id=1, source_target_pairs={{0,396},{64,192},{128,0},{192,320},{256,128},{320,448},{384,256},{... | collective-permute-start | bytes 1572872 | tf_op jit(solution)/shard_map/ppermute | solution.py:66
  120.8 0.0 collective-permute-done.6.theirs
  120.8 0.9 shard_map.185
  121.8 4.2 %all-to-all-start.3 = ((bf16[4,272,256]{2,1,0:T(8,128)(2,1)}), bf16[4,272,256]{2,1,0:T(8,128)(2,1)S(1)}, u32[]{:S(2)}, u32[]{:S(2)}) async-start(bf16[4,272,256]{2,1,0:T(8,128)(2,1)} %shard_map.185), calls=%async_computation.3 | async-start | bytes 1114112 | tf_op jit(solution)/shard_map/all_to_all | solution.py:51
  126.0 4.6 %collective-permute-start.7 = (bf16[16,128,128]{2,1,0:T(8,128)(2,1)}, bf16[16,128,128]{2,1,0:T(8,128)(2,1)S(1)}, u32[]{:S(2)}, u32[]{:S(2)}) collective-permute-start(bf16[16,128,128]{2,1,0:T(8,128)(2,1)} %get-tuple-element.58), channel_id=1, source_target_pairs={{0,128},{64,460},{128,256},{192,64},{256,384},{320,192},{384,4},{4... | collective-permute-start | bytes 1572872 | tf_op jit(solution)/shard_map/ppermute | solution.py:66
  130.6 3.2 %all-to-all-done.3.pieces = bf16[4,272,256]{2,1,0:T(8,128)(2,1)S(1)} async-done(((bf16[4,272,256]{2,1,0:T(8,128)(2,1)}), bf16[4,272,256]{2,1,0:T(8,128)(2,1)S(1)}, u32[]{:S(2)}, u32[]{:S(2)}) %all-to-all-start.3) | async-done | bytes 557088 | tf_op jit(solution)/shard_map/all_to_all | solution.py:51
  133.7 0.7 shard_map.186
  134.5 0.0 copy-start.11
  134.5 6.7 %all-to-all-start.4 = ((bf16[4,80,256]{2,1,0:T(8,128)(2,1)}), bf16[4,80,256]{2,1,0:T(8,128)(2,1)S(1)}, u32[]{:S(2)}, u32[]{:S(2)}) async-start(bf16[4,80,256]{2,1,0:T(8,128)(2,1)} %shard_map.186), calls=%async_computation.4 | async-start | bytes 327680 | tf_op jit(solution)/shard_map/all_to_all | solution.py:51
  141.2 0.0 collective-permute-done.8
  141.2 2.0 %add_convert_fusion = bf16[16,128,128]{2,1,0:T(8,128)(2,1)} fusion(bf16[16,128,128]{2,1,0:T(8,128)(2,1)} %collective-permute-done.8, bf16[16,128,128]{2,1,0:T(8,128)(2,1)S(1)} %get-tuple-element.64), kind=kLoop, calls=%fused_computation.1 | loop fusion | flops 1048576 | bytes 1572864 | tf_op jit(solution)/shard_map/convert_element_type | solution.py:552
  143.1 2.0 %collective-permute-start.9 = (bf16[16,128,128]{2,1,0:T(8,128)(2,1)}, bf16[16,128,128]{2,1,0:T(8,128)(2,1)S(1)}, u32[]{:S(2)}, u32[]{:S(2)}) collective-permute-start(bf16[16,128,128]{2,1,0:T(8,128)(2,1)} %add_convert_fusion), channel_id=1, source_target_pairs={{0,396},{64,192},{128,0},{192,320},{256,128},{320,448},{384,256},{... | collective-permute-start | bytes 1572872 | tf_op jit(solution)/shard_map/ppermute | solution.py:66
  145.2 0.0 copy-done.1
  145.2 0.0 copy-done.3
  145.2 0.0 copy-done.5
  145.2 0.0 copy-done.7
  145.2 0.0 copy-done.11
  145.2 1.1 shard_map.183.refs_2_
  146.4 0.0 copy-start.9
  146.4 0.0 collective-permute-done.7.refs_0_
  146.4 7.1 %all-to-all-done.4.refs_4_ = bf16[4,80,256]{2,1,0:T(8,128)(2,1)S(1)} async-done(((bf16[4,80,256]{2,1,0:T(8,128)(2,1)}), bf16[4,80,256]{2,1,0:T(8,128)(2,1)S(1)}, u32[]{:S(2)}, u32[]{:S(2)}) %all-to-all-start.4) | async-done | bytes 163872 | tf_op jit(solution)/shard_map/all_to_all | solution.py:51
  153.5 0.0 copy-done.6
  153.5 0.0 copy-done.8
  153.5 0.0 copy-done.10
  153.5 1.7 shard_map.188
  155.2 8.2 %collective-permute-start.10 = (bf16[128,256]{1,0:T(8,128)(2,1)S(1)}, bf16[128,256]{1,0:T(8,128)(2,1)S(1)}, u32[]{:S(2)}, u32[]{:S(2)}) collective-permute-start(bf16[128,256]{1,0:T(8,128)(2,1)S(1)} %get-tuple-element.67), channel_id=1, source_target_pairs={{0,64},{64,0},{1,65},{65,1},{2,66},{66,2},{3,67},{67,3},{4,68},{68... | collective-permute-start | bytes 196616 | tf_op jit(solution)/shard_map/ppermute | solution.py:581
  163.4 1.9 %collective-permute-start.11 = (bf16[128,256]{1,0:T(8,128)(2,1)S(1)}, bf16[128,256]{1,0:T(8,128)(2,1)S(1)}, u32[]{:S(2)}, u32[]{:S(2)}) collective-permute-start(bf16[128,256]{1,0:T(8,128)(2,1)S(1)} %get-tuple-element.68), channel_id=1, source_target_pairs={{64,128},{192,256},{320,384},{128,64},{256,192},{384,320},{65,129}... | collective-permute-start | bytes 196616 | tf_op jit(solution)/shard_map/ppermute | solution.py:582
  165.4 3.4 %all-to-all-start.5 = ((f32[8,1,64]{2,1,0:T(1,128)}), f32[8,1,64]{2,1,0:T(1,128)S(1)}, u32[]{:S(2)}, u32[]{:S(2)}) async-start(f32[8,1,64]{2,1,0:T(1,128)} %bitcast.16), calls=%async_computation.5 | async-start | bytes 8192 | tf_op jit(solution)/shard_map/all_to_all | solution.py:51
  168.8 0.0 collective-permute-done.9.refs_1_
  168.8 0.9 shard_map.190
  169.7 3.8 %all-to-all-done.5 = f32[8,1,64]{2,1,0:T(1,128)S(1)} async-done(((f32[8,1,64]{2,1,0:T(1,128)}), f32[8,1,64]{2,1,0:T(1,128)S(1)}, u32[]{:S(2)}, u32[]{:S(2)}) %all-to-all-start.5) | async-done | bytes 2080 | tf_op jit(solution)/shard_map/all_to_all | solution.py:51
  173.6 0.0 collective-permute-done.10.inside
  173.6 0.0 collective-permute-done.11.outside
  173.6 0.6 shard_map.189
  (16 shorter events, 0.1 us)
Async XLA Ops:
  2.7 38.9 %collective-permute-start.2 = (bf16[16,128,128]{2,1,0:T(8,128)(2,1)}, bf16[16,128,128]{2,1,0:T(8,128)(2,1)S(1)}, u32[]{:S(2)}, u32[]{:S(2)}) collective-permute-start(bf16[16,128,128]{2,1,0:T(8,128)(2,1)} %get-tuple-element.48.refs_2_), channel_id=1, source_target_pairs={{396,0},{192,64},{0,128},{320,192},{128,256},{448,320},{256,384},{... | collective-permute-start | bytes 1572872 | tf_op jit(solution)/shard_map/ppermute | solution.py:66
  14.7 6.1 %collective-permute-start.1 = (bf16[128,256]{1,0:T(8,128)(2,1)}, bf16[128,256]{1,0:T(8,128)(2,1)S(1)}, u32[]{:S(2)}, u32[]{:S(2)}) collective-permute-start(bf16[128,256]{1,0:T(8,128)(2,1)} %get-tuple-element.43.refs_5_.own.refs_9_), channel_id=1, source_target_pairs={{64,128},{192,256},{320,384},{128,64},{256,192},{384,320},{65,129}... | collective-permute-start | bytes 196616 | tf_op jit(solution)/shard_map/ppermute | solution.py:453
  16.6 4.2 %collective-permute-start = (bf16[128,256]{1,0:T(8,128)(2,1)}, bf16[128,256]{1,0:T(8,128)(2,1)S(1)}, u32[]{:S(2)}, u32[]{:S(2)}) collective-permute-start(bf16[128,256]{1,0:T(8,128)(2,1)} %get-tuple-element.43.refs_5_.own.refs_9_), channel_id=1, source_target_pairs={{0,64},{64,0},{1,65},{65,1},{2,66},{66,2},{3,67},{67,3},{4,68},{68... | collective-permute-start | bytes 196616 | tf_op jit(solution)/shard_map/ppermute | solution.py:452
  20.7 0.6 copy-start.2
  20.7 0.6 copy-start.4
  42.7 7.0 %copy-start = (bf16[16,128,128]{2,1,0:T(8,128)(2,1)S(1)}, bf16[16,128,128]{2,1,0:T(8,128)(2,1)}, u32[]{:S(2)}) copy-start(bf16[16,128,128]{2,1,0:T(8,128)(2,1)} %get-tuple-element.48.refs_2_) | copy-start | bytes 1572868
  42.7 22.3 %all-to-all-start = ((bf16[4,4,144,256]{3,2,1,0:T(8,128)(2,1)}), bf16[4,4,144,256]{3,2,1,0:T(8,128)(2,1)S(1)}, u32[]{:S(2)}, u32[]{:S(2)}) async-start(bf16[4,4,144,256]{3,2,1,0:T(8,128)(2,1)} %broadcast_in_dim.7), calls=%async_computation | async-start | bytes 2359296 | tf_op jit(solution)/shard_map/all_to_all | solution.py:47
  46.9 10.2 %collective-permute-start.3 = (bf16[16,128,128]{2,1,0:T(8,128)(2,1)S(1)}, bf16[16,128,128]{2,1,0:T(8,128)(2,1)S(1)}, u32[]{:S(2)}, u32[]{:S(2)}) collective-permute-start(bf16[16,128,128]{2,1,0:T(8,128)(2,1)S(1)} %collective-permute-done.2.refs_1_), channel_id=1, source_target_pairs={{396,0},{192,64},{0,128},{320,192},{128,256},{448,320},{256,384},{... | collective-permute-start | bytes 1572872 | tf_op jit(solution)/shard_map/ppermute | solution.py:66
  49.8 15.3 %collective-permute-start.4 = (bf16[16,128,128]{2,1,0:T(8,128)(2,1)S(1)}, bf16[16,128,128]{2,1,0:T(8,128)(2,1)S(1)}, u32[]{:S(2)}, u32[]{:S(2)}) collective-permute-start(bf16[16,128,128]{2,1,0:T(8,128)(2,1)S(1)} %copy-done), channel_id=1, source_target_pairs={{128,0},{460,64},{256,128},{64,192},{384,256},{192,320},{4,384},{3... | collective-permute-start | bytes 1572872 | tf_op jit(solution)/shard_map/ppermute | solution.py:66
  65.1 6.5 %collective-permute-start.5 = (bf16[4,4,144,256]{3,2,1,0:T(8,128)(2,1)S(1)}, bf16[4,4,144,256]{3,2,1,0:T(8,128)(2,1)S(1)}, u32[]{:S(2)}, u32[]{:S(2)}) collective-permute-start(bf16[4,4,144,256]{3,2,1,0:T(8,128)(2,1)S(1)} %all-to-all-done.refs_4_), channel_id=1, source_target_pairs={{0,64},{64,0},{1,65},{65,1},{2,66},{66,2},{3,67},{67,3},{4,68},{68... | collective-permute-start | bytes 3538952 | tf_op jit(solution)/shard_map/ppermute | solution.py:482
  111.3 9.5 %collective-permute-start.6 = (bf16[4,272,256]{2,1,0:T(8,128)(2,1)S(1)}, bf16[4,272,256]{2,1,0:T(8,128)(2,1)S(1)}, u32[]{:S(2)}, u32[]{:S(2)}) collective-permute-start(bf16[4,272,256]{2,1,0:T(8,128)(2,1)S(1)} %get-tuple-element.56), channel_id=1, source_target_pairs={{0,64},{64,0},{1,65},{65,1},{2,66},{66,2},{3,67},{67,3},{4,68},{68... | collective-permute-start | bytes 1671176 | tf_op jit(solution)/shard_map/ppermute | solution.py:514
  118.9 22.3 %collective-permute-start.8 = (bf16[16,128,128]{2,1,0:T(8,128)(2,1)}, bf16[16,128,128]{2,1,0:T(8,128)(2,1)}, u32[]{:S(2)}, u32[]{:S(2)}) collective-permute-start(bf16[16,128,128]{2,1,0:T(8,128)(2,1)} %get-tuple-element.65), channel_id=1, source_target_pairs={{0,396},{64,192},{128,0},{192,320},{256,128},{320,448},{384,256},{... | collective-permute-start | bytes 1572872 | tf_op jit(solution)/shard_map/ppermute | solution.py:66
  121.8 12.0 %all-to-all-start.3 = ((bf16[4,272,256]{2,1,0:T(8,128)(2,1)}), bf16[4,272,256]{2,1,0:T(8,128)(2,1)S(1)}, u32[]{:S(2)}, u32[]{:S(2)}) async-start(bf16[4,272,256]{2,1,0:T(8,128)(2,1)} %shard_map.185), calls=%async_computation.3 | async-start | bytes 1114112 | tf_op jit(solution)/shard_map/all_to_all | solution.py:51
  126.0 20.4 %collective-permute-start.7 = (bf16[16,128,128]{2,1,0:T(8,128)(2,1)}, bf16[16,128,128]{2,1,0:T(8,128)(2,1)S(1)}, u32[]{:S(2)}, u32[]{:S(2)}) collective-permute-start(bf16[16,128,128]{2,1,0:T(8,128)(2,1)} %get-tuple-element.58), channel_id=1, source_target_pairs={{0,128},{64,460},{128,256},{192,64},{256,384},{320,192},{384,4},{4... | collective-permute-start | bytes 1572872 | tf_op jit(solution)/shard_map/ppermute | solution.py:66
  134.5 10.7 %copy-start.1 = (bf16[128,256]{1,0:T(8,128)(2,1)S(1)}, bf16[128,256]{1,0:T(8,128)(2,1)}, u32[]{:S(2)}) copy-start(bf16[128,256]{1,0:T(8,128)(2,1)} %get-tuple-element.43.refs_5_.own.refs_9_) | copy-start | bytes 196612
  134.5 10.7 %copy-start.3 = (bf16[128,256]{1,0:T(8,128)(2,1)S(1)}, bf16[128,256]{1,0:T(8,128)(2,1)}, u32[]{:S(2)}) copy-start(bf16[128,256]{1,0:T(8,128)(2,1)} %copy-done.2) | copy-start | bytes 196612
  134.5 10.8 %copy-start.5 = (bf16[128,256]{1,0:T(8,128)(2,1)S(1)}, bf16[128,256]{1,0:T(8,128)(2,1)}, u32[]{:S(2)}) copy-start(bf16[128,256]{1,0:T(8,128)(2,1)} %copy-done.4) | copy-start | bytes 196612
  134.5 10.8 %copy-start.7 = (bf16[256,64]{0,1:T(8,128)(2,1)S(1)}, bf16[256,64]{0,1:T(8,128)(2,1)}, u32[]{:S(2)}) copy-start(bf16[256,64]{0,1:T(8,128)(2,1)} %param.14) | copy-start | bytes 98308
  134.5 10.8 %copy-start.11 = (s32[64]{0:T(128)S(1)}, s32[64]{0:T(128)}, u32[]{:S(2)}) copy-start(s32[64]{0:T(128)} %reaches.1) | copy-start | bytes 772
  134.5 19.0 %all-to-all-start.4 = ((bf16[4,80,256]{2,1,0:T(8,128)(2,1)}), bf16[4,80,256]{2,1,0:T(8,128)(2,1)S(1)}, u32[]{:S(2)}, u32[]{:S(2)}) async-start(bf16[4,80,256]{2,1,0:T(8,128)(2,1)} %shard_map.186), calls=%async_computation.4 | async-start | bytes 327680 | tf_op jit(solution)/shard_map/all_to_all | solution.py:51
  143.1 10.4 %copy-start.6 = (bf16[256,64]{0,1:T(8,128)(2,1)S(1)}, bf16[256,64]{0,1:T(8,128)(2,1)}, u32[]{:S(2)}) copy-start(bf16[256,64]{0,1:T(8,128)(2,1)} %param.25) | copy-start | bytes 98308
  143.1 10.4 %copy-start.8 = (bf16[64,256]{1,0:T(8,128)(2,1)S(1)}, bf16[64,256]{1,0:T(8,128)(2,1)}, u32[]{:S(2)}) copy-start(bf16[64,256]{1,0:T(8,128)(2,1)} %get-tuple-element.60.refs_5_) | copy-start | bytes 98308
  143.1 10.4 %copy-start.10 = (f32[64]{0:T(128)S(1)}, f32[64]{0:T(128)}, u32[]{:S(2)}) copy-start(f32[64]{0:T(128)} %param.18) | copy-start | bytes 772
  143.1 25.6 %collective-permute-start.9 = (bf16[16,128,128]{2,1,0:T(8,128)(2,1)}, bf16[16,128,128]{2,1,0:T(8,128)(2,1)S(1)}, u32[]{:S(2)}, u32[]{:S(2)}) collective-permute-start(bf16[16,128,128]{2,1,0:T(8,128)(2,1)} %add_convert_fusion), channel_id=1, source_target_pairs={{0,396},{64,192},{128,0},{192,320},{256,128},{320,448},{384,256},{... | collective-permute-start | bytes 1572872 | tf_op jit(solution)/shard_map/ppermute | solution.py:66
  146.4 22.4 %copy-start.9 = (f32[16,128]{1,0:T(8,128)S(1)}, f32[16,128]{1,0:T(8,128)}, u32[]{:S(2)}) copy-start(f32[16,128]{1,0:T(8,128)} %get-tuple-element.76.refs_3_) | copy-start | bytes 24580
  155.2 18.3 %collective-permute-start.10 = (bf16[128,256]{1,0:T(8,128)(2,1)S(1)}, bf16[128,256]{1,0:T(8,128)(2,1)S(1)}, u32[]{:S(2)}, u32[]{:S(2)}) collective-permute-start(bf16[128,256]{1,0:T(8,128)(2,1)S(1)} %get-tuple-element.67), channel_id=1, source_target_pairs={{0,64},{64,0},{1,65},{65,1},{2,66},{66,2},{3,67},{67,3},{4,68},{68... | collective-permute-start | bytes 196616 | tf_op jit(solution)/shard_map/ppermute | solution.py:581
  163.4 10.1 %collective-permute-start.11 = (bf16[128,256]{1,0:T(8,128)(2,1)S(1)}, bf16[128,256]{1,0:T(8,128)(2,1)S(1)}, u32[]{:S(2)}, u32[]{:S(2)}) collective-permute-start(bf16[128,256]{1,0:T(8,128)(2,1)S(1)} %get-tuple-element.68), channel_id=1, source_target_pairs={{64,128},{192,256},{320,384},{128,64},{256,192},{384,320},{65,129}... | collective-permute-start | bytes 196616 | tf_op jit(solution)/shard_map/ppermute | solution.py:582
  165.4 8.2 %all-to-all-start.5 = ((f32[8,1,64]{2,1,0:T(1,128)}), f32[8,1,64]{2,1,0:T(1,128)S(1)}, u32[]{:S(2)}, u32[]{:S(2)}) async-start(f32[8,1,64]{2,1,0:T(1,128)} %bitcast.16), calls=%async_computation.5 | async-start | bytes 8192 | tf_op jit(solution)/shard_map/all_to_all | solution.py:51
